TPU v7x, 256 devices: a whole 4x4x8 slice. The times are simulated.
256 devices in a mesh: loop: 64 (over z_hi, x, y), head: 4 (over z_lo, core).
Axes of the slice: x: 4, y: 4, z: 8 (z_hi: 4, z_lo: 2; z = z_hi * 2 + z_lo), core: 2. Of those that a mesh axis runs over, the one named last changes fastest.
Arguments:
- query_left: bfloat16 [64, 32, 8, 128], P('loop', 'head'), may hold values from -6 to 6
- query_right: bfloat16 [64, 8, 4096], P('loop', None, 'head'), may hold values from -6 to 6
- train_left: bfloat16 [128, 32, 8, 128], P('loop', 'head'), may hold values from -6 to 6
- train_right: bfloat16 [128, 8, 4096], P('loop', None, 'head'), may hold values from -6 to 6
- basis: bfloat16 [32, 128, 128], P('head'), may hold values from -0.5 to 0.5
- eigen: bfloat16 [32, 128, 4096], P(None, None, 'head'), may hold values from 0.25 to 4
- counts: int32 [128], P('loop'), may hold values from 128 to 4096
Outputs:
- scores: float32 [64, 128], P('head', 'loop')
All inputs are finite; a program needn't handle non-finite values.
Results may differ from a plain program's by a relative error of at most 0.006.
Values may be sent and summed in bfloat16 or wider, within the bound.
No kernel may reach another device: no remote copies, remote signals or barrier semaphores. Data moves between devices by JAX's collectives and lax.ppermute only.
A program may use at most 128 MiB of HBM per device.

v0:
```python
import math

import jax
import jax.numpy as jnp
from jax import lax
from jax.sharding import PartitionSpec as P

HEAD_COUNT = 32
HEAD_DIM = 128
MODEL_DIM = 4096
GRAD_RANK = 8


DAMPING = 0.1


def rotated(left, basis):
    product = jnp.einsum("nhri,hij->nhrj", left, basis, preferred_element_type=jnp.float32)
    return product.astype(jnp.bfloat16)


def scale_block(train_rot, train_right, eigen):

    def scale_per_head(carry, items):
        train_head, eigen_head = items
        dense = jnp.einsum(
            "sri,srj->sij", train_head, train_right, preferred_element_type=jnp.float32
        )
        scaled = (dense / (eigen_head.astype(jnp.float32) + DAMPING)).astype(jnp.bfloat16)
        return (carry, scaled)

    _, scaled_heads = lax.scan(scale_per_head, 0, (jnp.swapaxes(train_rot, 0, 1), eigen))
    return scaled_heads


def query_scores(query_rot, query_right, scaled_heads):

    def query_per_head(running, items):
        scaled, query_head = items
        product = jnp.einsum(
            "sij,prj->prsi", scaled, query_right, preferred_element_type=jnp.float32
        )
        return (running + jnp.einsum("prsi,pri->ps", product, query_head.astype(jnp.float32)), None)

    start = jnp.zeros((query_rot.shape[0], scaled_heads.shape[1]), jnp.float32)
    total, _ = lax.scan(query_per_head, start, (scaled_heads, jnp.swapaxes(query_rot, 0, 1)))
    return total


def on_device(query_left, query_right, train_left, train_right, basis, eigen, counts):
    query_rot = rotated(query_left, basis)
    train_rot = rotated(train_left, basis)
    train_all, query_heads = (
        lax.all_gather(train_rot, "head", axis=1, tiled=True),
        lax.all_gather(query_rot, "head", axis=1, tiled=True),
    )
    scaled_heads = scale_block(train_all, train_right, eigen)
    partial_scores = query_scores(
        lax.all_gather(query_heads, "loop", axis=0, tiled=True),
        lax.all_gather(query_right, "loop", axis=0, tiled=True),
        scaled_heads,
    )
    summed = lax.psum_scatter(partial_scores, "head", scatter_dimension=0, tiled=True)
    factor = 1.0 / (GRAD_RANK * math.sqrt(HEAD_COUNT * HEAD_DIM * MODEL_DIM))
    weights = counts.astype(jnp.float32) / 2048.0
    return summed * weights[None, :] * factor


def solution(mesh):
    placed = (
        P("loop", "head", None, None),
        P("loop", None, "head"),
        P("loop", "head", None, None),
        P("loop", None, "head"),
        P("head", None, None),
        P(None, None, "head"),
        P("loop"),
    )
    return jax.shard_map(
        on_device, mesh=mesh, in_specs=placed, out_specs=P("head", "loop"), check_vma=False
    )
```

profile of v0, /device:TPU:1, one launch (start us, length us, event | category | flops | bytes accessed | tf_op | source)
XLA Modules:
  0.0 309.5 jit_solution(13901303556642400843)
XLA Ops:
  8.4 8.8 %all_gather.14 = bf16[1,32,8,128]{3,2,0,1:T(8,128)(2,1)} all-gather(bf16[1,8,8,128]{3,2,0,1:T(8,128)(2,1)S(1)} %fusion.14), channel_id=1, replica_groups=mesh['loop'=64,'head'=4] {'head'}, dimensions={1}, use_global_device_ids=true | all-gather | bytes 81920 | tf_op jit(solution)/shard_map/all_gather | solution.py:55
  18.2 5.4 %all_gather.12 = bf16[2,32,8,128]{3,2,0,1:T(8,128)(2,1)S(1)} all-gather(bf16[2,8,8,128]{3,2,0,1:T(8,128)(2,1)S(1)} %fusion.13), channel_id=1, replica_groups=mesh['loop'=64,'head'=4] {'head'}, dimensions={1}, use_global_device_ids=true | all-gather | bytes 163840 | tf_op jit(solution)/shard_map/all_gather | solution.py:54
  23.6 93.6 %while.21 = (s32[]{:T(128)}, bf16[32,2,128,1024]{3,2,1,0:T(8,128)(2,1)}, bf16[32,2,8,128]{3,2,1,0:T(8,128)(2,1)S(1)}, bf16[2,8,1024]{2,1,0:T(8,128)(2,1)}, bf16[32,128,1024]{2,1,0:T(8,128)(2,1)}, /*index=5*/s32[]{:T(128)}) while((s32[]{:T(128)}, bf16[32,2,128,1024]{3,2,1,0:T(8,128)(2,1)}, bf16[32,2,8,128]{3,2,1,0:T(8,128)(2,1)S(1)}, ...), condition=%wide.region_1.2_spmd, body=%wide.region_0.1_spmd.sunk | while | flops 4980738 | bytes 1872969 | solution.py:32
  30.4 1.9 fusion.30
  33.4 1.9 fusion.30
  36.3 1.9 fusion.30
  39.2 1.9 fusion.30
  42.1 1.9 fusion.30
  47.9 1.9 fusion.30
  53.8 1.9 fusion.30
  59.6 1.9 fusion.30
  68.4 2.0 fusion.30
  71.4 2.0 fusion.30
  74.3 2.0 fusion.30
  83.1 1.9 fusion.30
  91.9 1.9 fusion.30
  94.8 1.9 fusion.30
  97.7 1.9 fusion.30
  100.7 1.9 fusion.30
  112.3 1.9 fusion.30
  115.3 1.9 fusion.30
  119.0 60.8 %all-gather.5.cloned.1.call-done = bf16[64,32,8,128]{3,2,1,0:T(8,128)(2,1)} async-done(((bf16[1,32,8,128]{3,2,1,0:T(8,128)(2,1)}), bf16[64,32,8,128]{3,2,1,0:T(8,128)(2,1)}) %all-gather.5.cloned.1.call-update) | async-done | bytes 4194320 | tf_op jit(solution)/shard_map/all_gather | solution.py:59
  179.8 102.6 %while.22 = (s32[]{:T(128)}, f32[64,2]{0,1:T(2,128)S(1)}, bf16[32,2,128,1024]{3,2,1,0:T(8,128)(2,1)}, bf16[64,8,1024]{2,0,1:T(8,128)(2,1)S(1)}, bf16[32,64,8,128]{3,2,0,1:T(8,128)(2,1)}, /*index=5*/s32[]{:T(128)}, s32[]{:T(128)}) while((s32[]{:T(128)}, f32[64,2]{0,1:T(2,128)S(1)}, bf16[32,2,128,1024]{3,2,1,0:T(8,128)(2,1)}, ...), condition=%wide.region_3.4_spmd.clone, body=%wide.region_2.3_spmd.clone.sunk | while | flops 268697856 | bytes 2494043 | solution.py:46
  283.2 18.3 %reduce-scatter.4.cloned.1.call-done = f32[16,2]{1,0:T(8,128)} async-done(((f32[64,2]{1,0:T(8,128)}), f32[16,2]{1,0:T(8,128)}) %reduce-scatter.4.cloned.1.call-update) | async-done | bytes 144
  (226 shorter events, 167.6 us)
Async XLA Ops:
  6.5 1.0 copy-start
  6.5 110.7 %all-gather.3.cloned.1.call-start = ((), (), s32[]{:S(2)}) async-start(), calls=%async_computation.1 | async-start | bytes 1064960 | tf_op jit(solution)/shard_map/all_gather | solution.py:60
  7.3 172.5 %all-gather.5.cloned.1.call-start = ((), (), s32[]{:S(2)}) async-start(), calls=%async_computation.2 | async-start | bytes 4259840 | tf_op jit(solution)/shard_map/all_gather | solution.py:59
  17.2 284.4 %reduce-scatter.4.cloned.1.call-start = ((), (), s32[]{:S(2)}) async-start(), calls=%async_computation.3 | async-start | bytes 40960
  117.2 166.0 %copy-start.1 = (s32[2]{0:T(128)S(1)}, s32[2]{0:T(128)}, u32[]{:S(2)}) copy-start(s32[2]{0:T(128)} %param.17) | copy-start | bytes 28
Sparse Core Ops, SparseCore 0:
  10.7 78.4 all-gather.2
  92.5 87.2 all-gather.4
  283.3 18.2 reduce-scatter.3
where the time goes:
time: 315 us; the launch traced here: 310 us
  matrix products  133 us (42%)
  waiting for transfers between devices  79.9 us (25%)
  local copies, waits for them, and re-layouts  35.3 us (11%)
  other arithmetic  33 us (10%)
  blocking collectives  14.2 us (5%)
  between operations  13.1 us (4%)
    dot_general x32, matrix products, scale_per_head(): jnp.einsum('sri,srj->sij', train_head, train_right, preferred_element_typ...  61.4 us
    all_gather x1, waiting for transfers between devices, on_device(): lax.all_gather(query_heads, 'loop', axis=0, tiled=True)  60.8 us
    dot_general x32, matrix products, query_per_head(): jnp.einsum('sij,prj->prsi', scaled, query_right, preferred_element_type=j...  49.2 us
    div x32, other arithmetic, scale_per_head(): dense / (eigen_head.astype(jnp.float32) + DAMPING)  31.9 us
    squeeze x32, local copies, waits for them, and re-layouts, query_scores(): lax.scan(query_per_head, start, (scaled_heads, jnp.swapaxes(query_rot, 0,...  29.5 us
    dot_general x32, matrix products, query_per_head(): jnp.einsum('prsi,pri->ps', product, query_head.astype(jnp.float32))  20.8 us
    unnamed x4, waiting for transfers between devices  19.1 us
    all_gather x1, blocking collectives, on_device(): lax.all_gather(query_rot, 'head', axis=1, tiled=True)  8.76 us
  transfers between devices with their start and end apart: 3, of which 2 were waited for; matrix products, arithmetic and copies ran while one was open for 31% of the time, Pallas kernels for 0%

commit v1 on v0

v1 whole, which is shorter than its diff:
```python
import math

import jax
import jax.numpy as jnp
from jax import lax
from jax.experimental import pallas as pl
from jax.experimental.pallas import tpu as pltpu
from jax.sharding import PartitionSpec as P

HEAD_COUNT = 32
HEAD_DIM = 128
MODEL_DIM = 4096
GRAD_RANK = 8
QUERIES = 64
DAMPING = 0.1
FACTOR = 1.0 / (GRAD_RANK * math.sqrt(HEAD_COUNT * HEAD_DIM * MODEL_DIM))

N = 4
HEADS = 8
SEQS = 8
FEATURES = 1024
COLUMNS = QUERIES * GRAD_RANK
BLOCK = COLUMNS // N


def axis_shift(axis, step):
    pairs = []
    for z in range(N):
        for x in range(N):
            for y in range(N):
                to = {"z": z, "x": x, "y": y}
                to[axis] = (to[axis] + step) % N
                pairs.append((z * 16 + x * 4 + y, to["z"] * 16 + to["x"] * 4 + to["y"]))
    return pairs


def swap_shift(step):
    pairs = []
    for z in range(N):
        for x in range(N):
            for y in range(N):
                for g in range(N):
                    source = (z * 16 + x * 4 + y) * N + g
                    target = (((z + step) % N) * 16 + x * 4 + g) * N + y
                    pairs.append((source, target))
    return pairs


def along(axis, value, step):
    return lax.ppermute(value, "loop", axis_shift(axis, step))


def swapped(value, step):
    return lax.ppermute(value, ("loop", "head"), swap_shift(step))


def across_heads(value, mask):
    return lax.ppermute(value, "head", [(i, i ^ mask) for i in range(N)])


def rotated(left, basis):
    product = jnp.einsum("nhri,hij->nhrj", left, basis, preferred_element_type=jnp.float32)
    return product.astype(jnp.bfloat16)


def score_kernel(place, *refs):
    tl = refs[0:4]
    tr = refs[4:8]
    ql = refs[8:12]
    qr = refs[12:16]
    eigen, out = refs[16:18]
    tl_all, tr_all, qr_all, ql_head, scaled, total = refs[18:]
    z, x, y, g = (place[i] for i in range(4))
    head = pl.program_id(0)

    @pl.when(head == 0)
    def _():
        total[...] = jnp.zeros_like(total)
        for m in range(N):
            tl_all[lax.rem(y - (g ^ m) + N, N)] = tl[m][...]
        for k in range(N):
            tr_all[16 * k : 16 * (k + 1), :] = tr[k][...].reshape(16, FEATURES)
            for j in range(FEATURES // 128):
                qr_all[BLOCK * k : BLOCK * (k + 1), 128 * j : 128 * (j + 1)] = qr[k][:, :, j].reshape(BLOCK, 128)

    for m in range(N):
        block = ql[m][:, :, head].reshape(BLOCK, HEAD_DIM).astype(jnp.float32)
        ql_head[lax.rem(y - (g ^ m) + N, N)] = block.T

    inverse = 1.0 / (eigen[0].astype(jnp.float32) + DAMPING)
    left = tl_all[:, :, head].reshape(SEQS * GRAD_RANK, HEAD_DIM)
    left = jnp.concatenate([left] * SEQS, axis=1)
    own = lax.broadcasted_iota(jnp.int32, left.shape, 0) // GRAD_RANK
    own = own == lax.broadcasted_iota(jnp.int32, left.shape, 1) // HEAD_DIM
    left = jnp.where(own, left, jnp.zeros_like(left))
    dense = lax.dot_general(left, tr_all[...], (((0,), (0,)), ((), ())), preferred_element_type=jnp.float32)
    dense = dense.reshape(SEQS, HEAD_DIM, FEATURES) * inverse[None]
    scaled[...] = dense.astype(jnp.bfloat16).reshape(SEQS * HEAD_DIM, FEATURES)

    product = lax.dot_general(
        scaled[...], qr_all[...], (((1,), (1,)), ((), ())), preferred_element_type=jnp.float32
    )
    for k in range(N):
        part = product[:, BLOCK * k : BLOCK * (k + 1)].reshape(SEQS, HEAD_DIM, BLOCK)
        total[:, BLOCK * k : BLOCK * (k + 1)] += jnp.sum(part * ql_head[k][None], axis=1)

    @pl.when(head == HEADS - 1)
    def _():
        column = lax.broadcasted_iota(jnp.int32, (COLUMNS, QUERIES), 0)
        target = lax.broadcasted_iota(jnp.int32, (COLUMNS, QUERIES), 1)
        yq = (y - column // BLOCK) & 3
        xq = (x - (column // 32) % N) & 3
        zq = (z - (column // 8) % N) & 3
        pick = ((g ^ zq) * 16 + xq * 4 + yq == target).astype(jnp.float32)
        picked = lax.dot_general(
            total[...], pick, (((1,), (0,)), ((), ())),
            preferred_element_type=jnp.float32, precision=lax.Precision.HIGHEST,
        )
        for m in range(N):
            out[m] = picked[:, 16 * m : 16 * (m + 1)]


def partial_scores(place, tl, tr, ql, qr, eigen):
    whole = lambda a: pl.BlockSpec(a.shape, lambda h, p: (0,) * a.ndim)
    operands = [*tl, *tr, *ql, *qr]
    return pl.pallas_call(
        score_kernel,
        out_shape=jax.ShapeDtypeStruct((N, SEQS, 16), jnp.float32),
        grid_spec=pltpu.PrefetchScalarGridSpec(
            num_scalar_prefetch=1,
            grid=(HEADS,),
            in_specs=[whole(a) for a in operands]
            + [pl.BlockSpec((1, HEAD_DIM, FEATURES), lambda h, p: (HEADS * p[2] + h, 0, 0))],
            out_specs=pl.BlockSpec((N, SEQS, 16), lambda h, p: (0, 0, 0)),
            scratch_shapes=[
                pltpu.VMEM((N, 2, HEADS, GRAD_RANK, HEAD_DIM), jnp.bfloat16),
                pltpu.VMEM((SEQS * GRAD_RANK, FEATURES), jnp.bfloat16),
                pltpu.VMEM((COLUMNS, FEATURES), jnp.bfloat16),
                pltpu.VMEM((N, HEAD_DIM, BLOCK), jnp.float32),
                pltpu.VMEM((SEQS * HEAD_DIM, FEATURES), jnp.bfloat16),
                pltpu.VMEM((SEQS, COLUMNS), jnp.float32),
            ],
        ),
        compiler_params=pltpu.CompilerParams(vmem_limit_bytes=48 * 2**20),
    )(place, *operands, eigen)


def on_device(query_left, query_right, train_left, train_right, basis, eigen, counts):
    loop, g = lax.axis_index("loop"), lax.axis_index("head")
    place = jnp.stack([loop // 16, loop // 4 % 4, loop % 4, g]).astype(jnp.int32)

    right = query_right.reshape(GRAD_RANK, 8, 128).transpose(1, 0, 2)[None]
    rights = [right] + [along("z", right, s) for s in range(1, N)]
    query_rot = rotated(query_left, basis)
    lefts = [swapped(query_rot, s) for s in range(N)]
    train_rot = rotated(train_left, basis)
    train_rot = swapped(train_rot, 0)
    tr = [train_right] + [along("y", train_right, k) for k in range(1, N)]

    both = jnp.concatenate([jnp.concatenate([a, b], 1) for a, b in zip(lefts, rights, strict=True)], 0)
    both = jnp.stack([both] + [along("x", both, s) for s in range(1, N)])

    left, right = both[:, :, :8], both[:, :, 8:]
    tl = [train_rot] + [across_heads(train_rot, m) for m in range(1, N)]
    ql = [left] + [across_heads(left, m) for m in range(1, N)]
    qr = [right] + [along("y", right, k) for k in range(1, N)]

    partial = partial_scores(place, tl, tr, ql, qr, eigen)

    summed = sum([across_heads(partial[m], m) for m in range(1, N)], partial[0])
    summed = sum([along("y", summed[2 * k : 2 * k + 2], -k) for k in range(1, N)], summed[:2])
    weights = counts.astype(jnp.float32) / 2048.0
    return (summed * weights[:, None] * FACTOR).T


def solution(mesh):
    placed = (
        P("loop", "head", None, None),
        P("loop", None, "head"),
        P("loop", "head", None, None),
        P("loop", None, "head"),
        P("head", None, None),
        P(None, None, "head"),
        P("loop"),
    )
    return jax.shard_map(
        on_device, mesh=mesh, in_specs=placed, out_specs=P("head", "loop"), check_vma=False
    )
```

time: 315 us -> 104 us (0.33); the launches traced: 310 us -> 103 us
  matrix products: 133 us -> 1.82 us
  starting transfers between devices: 0.08 us -> 56.2 us
  waiting for transfers between devices: 79.9 us -> 25.3 us
  local copies, waits for them, and re-layouts: 35.3 us -> 0.81 us
  other arithmetic: 33 us -> 2.26 us
  Pallas kernels: 0 us -> 16.8 us
  blocking collectives: 14.2 us -> 0 us
  between operations: 13.1 us -> 0.13 us
    dot_general x96 -> x0, matrix products: 131 us -> none  [the longest x32 61.4 us: scale_per_head(): jnp.einsum('sri,srj->sij', train_head, train_right, preferred_element_typ...]
    all_gather x2 -> x0, waiting for transfers between devices: 60.8 us -> none  [the longest x1 60.8 us: on_device(): lax.all_gather(query_heads, 'loop', axis=0, tiled=True)]
    ppermute x0 -> x29, starting transfers between devices: none -> 56.2 us  [the longest x15 29.2 us: along(): return lax.ppermute(value, 'loop', axis_shift(axis, step))]
    div x32 -> x0, other arithmetic: 31.9 us -> none  [scale_per_head(): dense / (eigen_head.astype(jnp.float32) + DAMPING)]
    squeeze x32 -> x1, local copies, waits for them, and re-layouts: 29.5 us -> 0.01 us  [on_device(): summed = sum([across_heads(partial[m], m) for m in range(1, N)], partial[0])]
    ppermute x0 -> x29, waiting for transfers between devices: none -> 25.3 us  [the longest x15 9.88 us: along(): return lax.ppermute(value, 'loop', axis_shift(axis, step))]
    unnamed x4 -> x0, waiting for transfers between devices: 19.1 us -> none
    pallas_call x0 -> x1, Pallas kernels: none -> 16.8 us  [partial_scores(): pl.pallas_call(score_kernel, out_shape=jax.ShapeDtypeStruct((N, SEQS, 16)...]
  transfers between devices with their start and end apart: 3 -> 29, of which waited for: 2 -> 12; matrix products, arithmetic and copies ran while one was open for 31% -> 3% of each run, Pallas kernels for 0% -> 0%
where the time goes in v1:
time: 104 us; the launch traced here: 103 us
  starting transfers between devices  56.2 us (54%)
  waiting for transfers between devices  25.3 us (24%)
  Pallas kernels  16.8 us (16%)
  other arithmetic  2.26 us (2%)
  matrix products  1.82 us (2%)
    ppermute x15, starting transfers between devices, along(): return lax.ppermute(value, 'loop', axis_shift(axis, step))  29.2 us
    pallas_call x1, Pallas kernels, partial_scores(): pl.pallas_call(score_kernel, out_shape=jax.ShapeDtypeStruct((N, SEQS, 16)...  16.8 us
    ppermute x5, starting transfers between devices, swapped(): return lax.ppermute(value, ('loop', 'head'), swap_shift(step))  14.7 us
    ppermute x9, starting transfers between devices, across_heads(): return lax.ppermute(value, 'head', [(i, i ^ mask) for i in range(N)])  12.3 us
    ppermute x15, waiting for transfers between devices, along(): return lax.ppermute(value, 'loop', axis_shift(axis, step))  9.88 us
    ppermute x9, waiting for transfers between devices, across_heads(): return lax.ppermute(value, 'head', [(i, i ^ mask) for i in range(N)])  9.3 us
    ppermute x5, waiting for transfers between devices, swapped(): return lax.ppermute(value, ('loop', 'head'), swap_shift(step))  6.13 us
  transfers between devices with their start and end apart: 29, of which 12 were waited for; matrix products, arithmetic and copies ran while one was open for 3% of the time, Pallas kernels for 0%

profile of v1, /device:TPU:1, one launch (start us, length us, event | category | flops | bytes accessed | tf_op | source)
XLA Modules:
  0.0 103.4 jit_solution(16628857900632209144)
XLA Ops:
  0.0 7.7 %collective-permute-start.11 = (bf16[1,8,8,128]{3,2,1,0:T(8,128)(2,1)}, bf16[1,8,8,128]{3,2,1,0:T(8,128)(2,1)S(1)}, u32[]{:S(2)}, u32[]{:S(2)}) collective-permute-start(bf16[1,8,8,128]{3,2,1,0:T(8,128)(2,1)} %bitcast.47), channel_id=1, source_target_pairs={{0,128},{4,132},{8,136},{12,140},{16,144},{20,148},{24,152},{28,15... | collective-permute-start | bytes 49160 | tf_op jit(solution)/shard_map/ppermute | solution.py:50
  7.7 2.4 %collective-permute-start.9 = (bf16[1,8,8,128]{3,2,1,0:T(8,128)(2,1)}, bf16[1,8,8,128]{3,2,1,0:T(8,128)(2,1)S(1)}, u32[]{:S(2)}, u32[]{:S(2)}) collective-permute-start(bf16[1,8,8,128]{3,2,1,0:T(8,128)(2,1)} %bitcast.49), channel_id=1, source_target_pairs={{0,64},{4,68},{8,72},{12,76},{16,80},{20,84},{24,88},{28,92},{32,9... | collective-permute-start | bytes 49160 | tf_op jit(solution)/shard_map/ppermute | solution.py:50
  11.0 4.3 %collective-permute-start.10 = (bf16[1,8,8,128]{3,2,1,0:T(8,128)(2,1)S(1)}, bf16[1,8,8,128]{3,2,1,0:T(8,128)(2,1)S(1)}, u32[]{:S(2)}, u32[]{:S(2)}) collective-permute-start(bf16[1,8,8,128]{3,2,1,0:T(8,128)(2,1)S(1)} %fusion.1), channel_id=1, source_target_pairs={{0,128},{1,132},{2,136},{3,140},{4,129},{5,133},{6,137},{7,141},{8... | collective-permute-start | bytes 49160 | tf_op jit(solution)/shard_map/ppermute | solution.py:54
  15.3 2.6 %collective-permute-start.12 = (bf16[1,8,8,128]{3,2,1,0:T(8,128)(2,1)S(1)}, bf16[1,8,8,128]{3,2,1,0:T(8,128)(2,1)S(1)}, u32[]{:S(2)}, u32[]{:S(2)}) collective-permute-start(bf16[1,8,8,128]{3,2,1,0:T(8,128)(2,1)S(1)} %fusion.1), channel_id=1, source_target_pairs={{0,192},{1,196},{2,200},{3,204},{4,193},{5,197},{6,201},{7,205},{8... | collective-permute-start | bytes 49160 | tf_op jit(solution)/shard_map/ppermute | solution.py:54
  17.9 4.6 %collective-permute-start.7 = (bf16[1,8,8,128]{3,2,1,0:T(8,128)(2,1)S(1)}, bf16[1,8,8,128]{3,2,1,0:T(8,128)(2,1)S(1)}, u32[]{:S(2)}, u32[]{:S(2)}) collective-permute-start(bf16[1,8,8,128]{3,2,1,0:T(8,128)(2,1)S(1)} %fusion.1), channel_id=1, source_target_pairs={{0,0},{1,4},{2,8},{3,12},{4,1},{5,5},{6,9},{7,13},{8,2},{9,6},{10,... | collective-permute-start | bytes 49160 | tf_op jit(solution)/shard_map/ppermute | solution.py:54
  22.6 1.6 %collective-permute-done.7 = bf16[1,8,8,128]{3,2,1,0:T(8,128)(2,1)S(1)} collective-permute-done((bf16[1,8,8,128]{3,2,1,0:T(8,128)(2,1)S(1)}, bf16[1,8,8,128]{3,2,1,0:T(8,128)(2,1)S(1)}, u32[]{:S(2)}, u32[]{:S(2)}) %collective-permute-start.7) | collective-permute-done | bytes 16416 | tf_op jit(solution)/shard_map/ppermute | solution.py:54
  24.2 4.6 %collective-permute-done.8 = bf16[1,8,8,128]{3,2,1,0:T(8,128)(2,1)S(1)} collective-permute-done((bf16[1,8,8,128]{3,2,1,0:T(8,128)(2,1)S(1)}, bf16[1,8,8,128]{3,2,1,0:T(8,128)(2,1)S(1)}, u32[]{:S(2)}, u32[]{:S(2)}) %collective-permute-start.8) | collective-permute-done | bytes 16416 | tf_op jit(solution)/shard_map/ppermute | solution.py:54
  29.5 1.3 %collective-permute-start.14 = (bf16[4,16,8,128]{3,2,1,0:T(8,128)(2,1)S(1)}, bf16[4,16,8,128]{3,2,1,0:T(8,128)(2,1)S(1)}, u32[]{:S(2)}, u32[]{:S(2)}) collective-permute-start(bf16[4,16,8,128]{3,2,1,0:T(8,128)(2,1)S(1)} %maximum_maximum_fusion), channel_id=1, source_target_pairs={{0,16},{4,20},{8,24},{12,28},{16,32},{20,36},{24,40},{28,44},{32,4... | collective-permute-start | bytes 393224 | tf_op jit(solution)/shard_map/ppermute | solution.py:50
  30.8 2.5 %collective-permute-start.15 = (bf16[4,16,8,128]{3,2,1,0:T(8,128)(2,1)S(1)}, bf16[4,16,8,128]{3,2,1,0:T(8,128)(2,1)S(1)}, u32[]{:S(2)}, u32[]{:S(2)}) collective-permute-start(bf16[4,16,8,128]{3,2,1,0:T(8,128)(2,1)S(1)} %maximum_maximum_fusion), channel_id=1, source_target_pairs={{0,32},{4,36},{8,40},{12,44},{16,48},{20,52},{24,56},{28,60},{32,0... | collective-permute-start | bytes 393224 | tf_op jit(solution)/shard_map/ppermute | solution.py:50
  33.2 1.2 %collective-permute-start.16 = (bf16[4,16,8,128]{3,2,1,0:T(8,128)(2,1)S(1)}, bf16[4,16,8,128]{3,2,1,0:T(8,128)(2,1)S(1)}, u32[]{:S(2)}, u32[]{:S(2)}) collective-permute-start(bf16[4,16,8,128]{3,2,1,0:T(8,128)(2,1)S(1)} %maximum_maximum_fusion), channel_id=1, source_target_pairs={{0,48},{4,52},{8,56},{12,60},{16,0},{20,4},{24,8},{28,12},{32,16},... | collective-permute-start | bytes 393224 | tf_op jit(solution)/shard_map/ppermute | solution.py:50
  35.5 1.5 %collective-permute-done.15 = bf16[4,16,8,128]{3,2,1,0:T(8,128)(2,1)S(1)} collective-permute-done((bf16[4,16,8,128]{3,2,1,0:T(8,128)(2,1)S(1)}, bf16[4,16,8,128]{3,2,1,0:T(8,128)(2,1)S(1)}, u32[]{:S(2)}, u32[]{:S(2)}) %collective-permute-start.15) | collective-permute-done | bytes 131104 | tf_op jit(solution)/shard_map/ppermute | solution.py:50
  37.7 0.9 fusion
  38.7 3.2 %collective-permute-start = (bf16[2,8,8,128]{3,2,1,0:T(8,128)(2,1)S(1)}, bf16[2,8,8,128]{3,2,1,0:T(8,128)(2,1)S(1)}, u32[]{:S(2)}, u32[]{:S(2)}) collective-permute-start(bf16[2,8,8,128]{3,2,1,0:T(8,128)(2,1)S(1)} %fusion), channel_id=1, source_target_pairs={{0,0},{1,4},{2,8},{3,12},{4,1},{5,5},{6,9},{7,13},{8,2},{9,6},{10,... | collective-permute-start | bytes 98312 | tf_op jit(solution)/shard_map/ppermute | solution.py:54
  41.9 6.6 %collective-permute-start.5 = (bf16[2,8,1024]{2,1,0:T(8,128)(2,1)}, bf16[2,8,1024]{2,1,0:T(8,128)(2,1)S(1)}, u32[]{:S(2)}, u32[]{:S(2)}) collective-permute-start(bf16[2,8,1024]{2,1,0:T(8,128)(2,1)} %refs_4_.1), channel_id=1, source_target_pairs={{0,8},{4,12},{8,0},{12,4},{16,24},{20,28},{24,16},{28,20},{32,40},... | collective-permute-start | bytes 98312 | tf_op jit(solution)/shard_map/ppermute | solution.py:50
  49.5 5.4 %collective-permute-start.1 = (bf16[2,8,8,128]{3,2,1,0:T(8,128)(2,1)S(1)}, bf16[2,8,8,128]{3,2,1,0:T(8,128)(2,1)S(1)}, u32[]{:S(2)}, u32[]{:S(2)}) collective-permute-start(bf16[2,8,8,128]{3,2,1,0:T(8,128)(2,1)S(1)} %collective-permute-done.refs_0_), channel_id=1, source_target_pairs={{0,1},{1,0},{2,3},{3,2},{4,5},{5,4},{6,7},{7,6},{8,9},{9,8},{10,11... | collective-permute-start | bytes 98312 | tf_op jit(solution)/shard_map/ppermute | solution.py:58
  55.4 1.1 %collective-permute-start.3 = (bf16[2,8,8,128]{3,2,1,0:T(8,128)(2,1)S(1)}, bf16[2,8,8,128]{3,2,1,0:T(8,128)(2,1)S(1)}, u32[]{:S(2)}, u32[]{:S(2)}) collective-permute-start(bf16[2,8,8,128]{3,2,1,0:T(8,128)(2,1)S(1)} %collective-permute-done.refs_0_), channel_id=1, source_target_pairs={{0,3},{1,2},{2,1},{3,0},{4,7},{5,6},{6,5},{7,4},{8,11},{9,10},{10,... | collective-permute-start | bytes 98312 | tf_op jit(solution)/shard_map/ppermute | solution.py:58
  57.3 2.0 %collective-permute-start.19 = (bf16[4,4,8,8,128]{4,3,2,1,0:T(8,128)(2,1)S(1)}, bf16[4,4,8,8,128]{4,3,2,1,0:T(8,128)(2,1)S(1)}, u32[]{:S(2)}, u32[]{:S(2)}) collective-permute-start(bf16[4,4,8,8,128]{4,3,2,1,0:T(8,128)(2,1)S(1)} %get-tuple-element.6.refs_8_), channel_id=1, source_target_pairs={{0,3},{1,2},{2,1},{3,0},{4,7},{5,6},{6,5},{7,4},{8,11},{9,10},{10,... | collective-permute-start | bytes 786440 | tf_op jit(solution)/shard_map/ppermute | solution.py:58
  59.2 3.5 %collective-permute-start.21 = (bf16[4,4,8,8,128]{4,3,2,1,0:T(8,128)(2,1)S(1)}, bf16[4,4,8,8,128]{4,3,2,1,0:T(8,128)(2,1)S(1)}, u32[]{:S(2)}, u32[]{:S(2)}) collective-permute-start(bf16[4,4,8,8,128]{4,3,2,1,0:T(8,128)(2,1)S(1)} %get-tuple-element.5.refs_12_), channel_id=1, source_target_pairs={{0,8},{4,12},{8,0},{12,4},{16,24},{20,28},{24,16},{28,20},{32,40},... | collective-permute-start | bytes 786440 | tf_op jit(solution)/shard_map/ppermute | solution.py:50
  63.4 7.2 %collective-permute-done.19.refs_11_ = bf16[4,4,8,8,128]{4,3,2,1,0:T(8,128)(2,1)S(1)} collective-permute-done((bf16[4,4,8,8,128]{4,3,2,1,0:T(8,128)(2,1)S(1)}, bf16[4,4,8,8,128]{4,3,2,1,0:T(8,128)(2,1)S(1)}, u32[]{:S(2)}, u32[]{:S(2)}) %collective-permute-start.19) | collective-permute-done | bytes 262176 | tf_op jit(solution)/shard_map/ppermute | solution.py:58
  70.5 3.6 %collective-permute-done.21.refs_14_ = bf16[4,4,8,8,128]{4,3,2,1,0:T(8,128)(2,1)S(1)} collective-permute-done((bf16[4,4,8,8,128]{4,3,2,1,0:T(8,128)(2,1)S(1)}, bf16[4,4,8,8,128]{4,3,2,1,0:T(8,128)(2,1)S(1)}, u32[]{:S(2)}, u32[]{:S(2)}) %collective-permute-start.21) | collective-permute-done | bytes 262176 | tf_op jit(solution)/shard_map/ppermute | solution.py:50
  75.5 16.8 %shard_map.73 = f32[4,8,16]{2,1,0:T(8,128)S(1)} custom-call(s32[4]{0:T(128)S(1)} %pad_add_fusion.place, bf16[2,8,8,128]{3,2,1,0:T(8,128)(2,1)S(1)} %collective-permute-done.refs_0_, bf16[2,8,8,128]{3,2,1,0:T(8,128)(2,1)S(1)} %collective-permute-done.1.refs_1_, bf16[2,8,8,128]{3,2,1,0:T(8,128)(2,1)S(1)} %collective-permute-done.2.refs_2_, ...), custom_call_target="tpu_custom_call" | custom-call | tf_op jit(solution)/shard_map/pallas_call | solution.py:126
  93.1 1.7 %collective-permute-start.25 = (f32[8,16]{1,0:T(8,128)S(1)}, f32[8,16]{1,0:T(8,128)S(1)}, u32[]{:S(2)}, u32[]{:S(2)}) collective-permute-start(f32[8,16]{1,0:T(8,128)S(1)} %get-tuple-element.8), channel_id=1, source_target_pairs={{0,3},{1,2},{2,1},{3,0},{4,7},{5,6},{6,5},{7,4},{8,11},{9,10},{10,... | collective-permute-start | bytes 1544 | tf_op jit(solution)/shard_map/ppermute | solution.py:58
  96.4 2.4 %collective-permute-start.26 = (f32[2,16]{1,0:T(2,128)S(1)}, f32[2,16]{1,0:T(2,128)S(1)}, u32[]{:S(2)}, u32[]{:S(2)}) collective-permute-start(f32[2,16]{1,0:T(2,128)S(1)} %get-tuple-element.10), channel_id=1, source_target_pairs={{0,12},{4,0},{8,4},{12,8},{16,28},{20,16},{24,20},{28,24},{32,44},... | collective-permute-start | bytes 392 | tf_op jit(solution)/shard_map/ppermute | solution.py:50
  99.6 3.2 %collective-permute-done.27 = f32[2,16]{1,0:T(2,128)S(1)} collective-permute-done((f32[2,16]{1,0:T(2,128)S(1)}, f32[2,16]{1,0:T(2,128)S(1)}, u32[]{:S(2)}, u32[]{:S(2)}) %collective-permute-start.27) | collective-permute-done | bytes 160 | tf_op jit(solution)/shard_map/ppermute | solution.py:50
  (53 shorter events, 11.6 us)
Async XLA Ops:
  0.0 17.9 %collective-permute-start.11 = (bf16[1,8,8,128]{3,2,1,0:T(8,128)(2,1)}, bf16[1,8,8,128]{3,2,1,0:T(8,128)(2,1)S(1)}, u32[]{:S(2)}, u32[]{:S(2)}) collective-permute-start(bf16[1,8,8,128]{3,2,1,0:T(8,128)(2,1)} %bitcast.47), channel_id=1, source_target_pairs={{0,128},{4,132},{8,136},{12,140},{16,144},{20,148},{24,152},{28,15... | collective-permute-start | bytes 49160 | tf_op jit(solution)/shard_map/ppermute | solution.py:50
  7.7 14.8 %collective-permute-start.13 = (bf16[1,8,8,128]{3,2,1,0:T(8,128)(2,1)}, bf16[1,8,8,128]{3,2,1,0:T(8,128)(2,1)S(1)}, u32[]{:S(2)}, u32[]{:S(2)}) collective-permute-start(bf16[1,8,8,128]{3,2,1,0:T(8,128)(2,1)} %bitcast.48), channel_id=1, source_target_pairs={{0,192},{4,196},{8,200},{12,204},{16,208},{20,212},{24,216},{28,22... | collective-permute-start | bytes 49160 | tf_op jit(solution)/shard_map/ppermute | solution.py:50
  7.7 14.8 %collective-permute-start.9 = (bf16[1,8,8,128]{3,2,1,0:T(8,128)(2,1)}, bf16[1,8,8,128]{3,2,1,0:T(8,128)(2,1)S(1)}, u32[]{:S(2)}, u32[]{:S(2)}) collective-permute-start(bf16[1,8,8,128]{3,2,1,0:T(8,128)(2,1)} %bitcast.49), channel_id=1, source_target_pairs={{0,64},{4,68},{8,72},{12,76},{16,80},{20,84},{24,88},{28,92},{32,9... | collective-permute-start | bytes 49160 | tf_op jit(solution)/shard_map/ppermute | solution.py:50
  11.0 11.6 %collective-permute-start.10 = (bf16[1,8,8,128]{3,2,1,0:T(8,128)(2,1)S(1)}, bf16[1,8,8,128]{3,2,1,0:T(8,128)(2,1)S(1)}, u32[]{:S(2)}, u32[]{:S(2)}) collective-permute-start(bf16[1,8,8,128]{3,2,1,0:T(8,128)(2,1)S(1)} %fusion.1), channel_id=1, source_target_pairs={{0,128},{1,132},{2,136},{3,140},{4,129},{5,133},{6,137},{7,141},{8... | collective-permute-start | bytes 49160 | tf_op jit(solution)/shard_map/ppermute | solution.py:54
  15.3 7.3 %collective-permute-start.12 = (bf16[1,8,8,128]{3,2,1,0:T(8,128)(2,1)S(1)}, bf16[1,8,8,128]{3,2,1,0:T(8,128)(2,1)S(1)}, u32[]{:S(2)}, u32[]{:S(2)}) collective-permute-start(bf16[1,8,8,128]{3,2,1,0:T(8,128)(2,1)S(1)} %fusion.1), channel_id=1, source_target_pairs={{0,192},{1,196},{2,200},{3,204},{4,193},{5,197},{6,201},{7,205},{8... | collective-permute-start | bytes 49160 | tf_op jit(solution)/shard_map/ppermute | solution.py:54
  17.9 6.3 %collective-permute-start.7 = (bf16[1,8,8,128]{3,2,1,0:T(8,128)(2,1)S(1)}, bf16[1,8,8,128]{3,2,1,0:T(8,128)(2,1)S(1)}, u32[]{:S(2)}, u32[]{:S(2)}) collective-permute-start(bf16[1,8,8,128]{3,2,1,0:T(8,128)(2,1)S(1)} %fusion.1), channel_id=1, source_target_pairs={{0,0},{1,4},{2,8},{3,12},{4,1},{5,5},{6,9},{7,13},{8,2},{9,6},{10,... | collective-permute-start | bytes 49160 | tf_op jit(solution)/shard_map/ppermute | solution.py:54
  22.5 6.3 %collective-permute-start.8 = (bf16[1,8,8,128]{3,2,1,0:T(8,128)(2,1)S(1)}, bf16[1,8,8,128]{3,2,1,0:T(8,128)(2,1)S(1)}, u32[]{:S(2)}, u32[]{:S(2)}) collective-permute-start(bf16[1,8,8,128]{3,2,1,0:T(8,128)(2,1)S(1)} %fusion.1), channel_id=1, source_target_pairs={{0,64},{1,68},{2,72},{3,76},{4,65},{5,69},{6,73},{7,77},{8,66},{9,... | collective-permute-start | bytes 49160 | tf_op jit(solution)/shard_map/ppermute | solution.py:54
  29.5 6.0 %collective-permute-start.14 = (bf16[4,16,8,128]{3,2,1,0:T(8,128)(2,1)S(1)}, bf16[4,16,8,128]{3,2,1,0:T(8,128)(2,1)S(1)}, u32[]{:S(2)}, u32[]{:S(2)}) collective-permute-start(bf16[4,16,8,128]{3,2,1,0:T(8,128)(2,1)S(1)} %maximum_maximum_fusion), channel_id=1, source_target_pairs={{0,16},{4,20},{8,24},{12,28},{16,32},{20,36},{24,40},{28,44},{32,4... | collective-permute-start | bytes 393224 | tf_op jit(solution)/shard_map/ppermute | solution.py:50
  30.8 6.2 %collective-permute-start.15 = (bf16[4,16,8,128]{3,2,1,0:T(8,128)(2,1)S(1)}, bf16[4,16,8,128]{3,2,1,0:T(8,128)(2,1)S(1)}, u32[]{:S(2)}, u32[]{:S(2)}) collective-permute-start(bf16[4,16,8,128]{3,2,1,0:T(8,128)(2,1)S(1)} %maximum_maximum_fusion), channel_id=1, source_target_pairs={{0,32},{4,36},{8,40},{12,44},{16,48},{20,52},{24,56},{28,60},{32,0... | collective-permute-start | bytes 393224 | tf_op jit(solution)/shard_map/ppermute | solution.py:50
  33.2 4.3 %collective-permute-start.16 = (bf16[4,16,8,128]{3,2,1,0:T(8,128)(2,1)S(1)}, bf16[4,16,8,128]{3,2,1,0:T(8,128)(2,1)S(1)}, u32[]{:S(2)}, u32[]{:S(2)}) collective-permute-start(bf16[4,16,8,128]{3,2,1,0:T(8,128)(2,1)S(1)} %maximum_maximum_fusion), channel_id=1, source_target_pairs={{0,48},{4,52},{8,56},{12,60},{16,0},{20,4},{24,8},{28,12},{32,16},... | collective-permute-start | bytes 393224 | tf_op jit(solution)/shard_map/ppermute | solution.py:50
  37.6 25.1 %collective-permute-start.17 = (bf16[4,4,8,8,128]{4,3,2,1,0:T(8,128)(2,1)S(1)}, bf16[4,4,8,8,128]{4,3,2,1,0:T(8,128)(2,1)S(1)}, u32[]{:S(2)}, u32[]{:S(2)}) collective-permute-start(bf16[4,4,8,8,128]{4,3,2,1,0:T(8,128)(2,1)S(1)} %get-tuple-element.6.refs_8_), channel_id=1, source_target_pairs={{0,1},{1,0},{2,3},{3,2},{4,5},{5,4},{6,7},{7,6},{8,9},{9,8},{10,11... | collective-permute-start | bytes 786440 | tf_op jit(solution)/shard_map/ppermute | solution.py:58
  38.7 10.8 %collective-permute-start = (bf16[2,8,8,128]{3,2,1,0:T(8,128)(2,1)S(1)}, bf16[2,8,8,128]{3,2,1,0:T(8,128)(2,1)S(1)}, u32[]{:S(2)}, u32[]{:S(2)}) collective-permute-start(bf16[2,8,8,128]{3,2,1,0:T(8,128)(2,1)S(1)} %fusion), channel_id=1, source_target_pairs={{0,0},{1,4},{2,8},{3,12},{4,1},{5,5},{6,9},{7,13},{8,2},{9,6},{10,... | collective-permute-start | bytes 98312 | tf_op jit(solution)/shard_map/ppermute | solution.py:54
  41.8 13.0 %collective-permute-start.4 = (bf16[2,8,1024]{2,1,0:T(8,128)(2,1)}, bf16[2,8,1024]{2,1,0:T(8,128)(2,1)S(1)}, u32[]{:S(2)}, u32[]{:S(2)}) collective-permute-start(bf16[2,8,1024]{2,1,0:T(8,128)(2,1)} %refs_4_.1), channel_id=1, source_target_pairs={{0,4},{4,8},{8,12},{12,0},{16,20},{20,24},{24,28},{28,16},{32,36},... | collective-permute-start | bytes 98312 | tf_op jit(solution)/shard_map/ppermute | solution.py:50
  41.9 13.5 %collective-permute-start.5 = (bf16[2,8,1024]{2,1,0:T(8,128)(2,1)}, bf16[2,8,1024]{2,1,0:T(8,128)(2,1)S(1)}, u32[]{:S(2)}, u32[]{:S(2)}) collective-permute-start(bf16[2,8,1024]{2,1,0:T(8,128)(2,1)} %refs_4_.1), channel_id=1, source_target_pairs={{0,8},{4,12},{8,0},{12,4},{16,24},{20,28},{24,16},{28,20},{32,40},... | collective-permute-start | bytes 98312 | tf_op jit(solution)/shard_map/ppermute | solution.py:50
  48.6 8.0 %collective-permute-start.6 = (bf16[2,8,1024]{2,1,0:T(8,128)(2,1)}, bf16[2,8,1024]{2,1,0:T(8,128)(2,1)S(1)}, u32[]{:S(2)}, u32[]{:S(2)}) collective-permute-start(bf16[2,8,1024]{2,1,0:T(8,128)(2,1)} %refs_4_.1), channel_id=1, source_target_pairs={{0,12},{4,0},{8,4},{12,8},{16,28},{20,16},{24,20},{28,24},{32,44},... | collective-permute-start | bytes 98312 | tf_op jit(solution)/shard_map/ppermute | solution.py:50
  49.5 7.8 %collective-permute-start.1 = (bf16[2,8,8,128]{3,2,1,0:T(8,128)(2,1)S(1)}, bf16[2,8,8,128]{3,2,1,0:T(8,128)(2,1)S(1)}, u32[]{:S(2)}, u32[]{:S(2)}) collective-permute-start(bf16[2,8,8,128]{3,2,1,0:T(8,128)(2,1)S(1)} %collective-permute-done.refs_0_), channel_id=1, source_target_pairs={{0,1},{1,0},{2,3},{3,2},{4,5},{5,4},{6,7},{7,6},{8,9},{9,8},{10,11... | collective-permute-start | bytes 98312 | tf_op jit(solution)/shard_map/ppermute | solution.py:58
  54.8 4.4 %collective-permute-start.2 = (bf16[2,8,8,128]{3,2,1,0:T(8,128)(2,1)S(1)}, bf16[2,8,8,128]{3,2,1,0:T(8,128)(2,1)S(1)}, u32[]{:S(2)}, u32[]{:S(2)}) collective-permute-start(bf16[2,8,8,128]{3,2,1,0:T(8,128)(2,1)S(1)} %collective-permute-done.refs_0_), channel_id=1, source_target_pairs={{0,2},{1,3},{2,0},{3,1},{4,6},{5,7},{6,4},{7,5},{8,10},{9,11},{10,... | collective-permute-start | bytes 98312 | tf_op jit(solution)/shard_map/ppermute | solution.py:58
  56.6 6.8 %collective-permute-start.18 = (bf16[4,4,8,8,128]{4,3,2,1,0:T(8,128)(2,1)S(1)}, bf16[4,4,8,8,128]{4,3,2,1,0:T(8,128)(2,1)S(1)}, u32[]{:S(2)}, u32[]{:S(2)}) collective-permute-start(bf16[4,4,8,8,128]{4,3,2,1,0:T(8,128)(2,1)S(1)} %get-tuple-element.6.refs_8_), channel_id=1, source_target_pairs={{0,2},{1,3},{2,0},{3,1},{4,6},{5,7},{6,4},{7,5},{8,10},{9,11},{10,... | collective-permute-start | bytes 786440 | tf_op jit(solution)/shard_map/ppermute | solution.py:58
  57.3 13.2 %collective-permute-start.19 = (bf16[4,4,8,8,128]{4,3,2,1,0:T(8,128)(2,1)S(1)}, bf16[4,4,8,8,128]{4,3,2,1,0:T(8,128)(2,1)S(1)}, u32[]{:S(2)}, u32[]{:S(2)}) collective-permute-start(bf16[4,4,8,8,128]{4,3,2,1,0:T(8,128)(2,1)S(1)} %get-tuple-element.6.refs_8_), channel_id=1, source_target_pairs={{0,3},{1,2},{2,1},{3,0},{4,7},{5,6},{6,5},{7,4},{8,11},{9,10},{10,... | collective-permute-start | bytes 786440 | tf_op jit(solution)/shard_map/ppermute | solution.py:58
  59.2 11.3 %collective-permute-start.20 = (bf16[4,4,8,8,128]{4,3,2,1,0:T(8,128)(2,1)S(1)}, bf16[4,4,8,8,128]{4,3,2,1,0:T(8,128)(2,1)S(1)}, u32[]{:S(2)}, u32[]{:S(2)}) collective-permute-start(bf16[4,4,8,8,128]{4,3,2,1,0:T(8,128)(2,1)S(1)} %get-tuple-element.5.refs_12_), channel_id=1, source_target_pairs={{0,4},{4,8},{8,12},{12,0},{16,20},{20,24},{24,28},{28,16},{32,36},... | collective-permute-start | bytes 786440 | tf_op jit(solution)/shard_map/ppermute | solution.py:50
  59.2 14.9 %collective-permute-start.21 = (bf16[4,4,8,8,128]{4,3,2,1,0:T(8,128)(2,1)S(1)}, bf16[4,4,8,8,128]{4,3,2,1,0:T(8,128)(2,1)S(1)}, u32[]{:S(2)}, u32[]{:S(2)}) collective-permute-start(bf16[4,4,8,8,128]{4,3,2,1,0:T(8,128)(2,1)S(1)} %get-tuple-element.5.refs_12_), channel_id=1, source_target_pairs={{0,8},{4,12},{8,0},{12,4},{16,24},{20,28},{24,16},{28,20},{32,40},... | collective-permute-start | bytes 786440 | tf_op jit(solution)/shard_map/ppermute | solution.py:50
  62.7 12.0 %collective-permute-start.22 = (bf16[4,4,8,8,128]{4,3,2,1,0:T(8,128)(2,1)S(1)}, bf16[4,4,8,8,128]{4,3,2,1,0:T(8,128)(2,1)S(1)}, u32[]{:S(2)}, u32[]{:S(2)}) collective-permute-start(bf16[4,4,8,8,128]{4,3,2,1,0:T(8,128)(2,1)S(1)} %get-tuple-element.5.refs_12_), channel_id=1, source_target_pairs={{0,12},{4,0},{8,4},{12,8},{16,28},{20,16},{24,20},{28,24},{32,44},... | collective-permute-start | bytes 786440 | tf_op jit(solution)/shard_map/ppermute | solution.py:50
  98.8 3.9 %collective-permute-start.27 = (f32[2,16]{1,0:T(2,128)S(1)}, f32[2,16]{1,0:T(2,128)S(1)}, u32[]{:S(2)}, u32[]{:S(2)}) collective-permute-start(f32[2,16]{1,0:T(2,128)S(1)} %get-tuple-element.12), channel_id=1, source_target_pairs={{0,8},{4,12},{8,0},{12,4},{16,24},{20,28},{24,16},{28,20},{32,40},... | collective-permute-start | bytes 392 | tf_op jit(solution)/shard_map/ppermute | solution.py:50
  98.9 3.8 %collective-permute-start.28 = (f32[2,16]{1,0:T(2,128)S(1)}, f32[2,16]{1,0:T(2,128)S(1)}, u32[]{:S(2)}, u32[]{:S(2)}) collective-permute-start(f32[2,16]{1,0:T(2,128)S(1)} %get-tuple-element.11), channel_id=1, source_target_pairs={{0,4},{4,8},{8,12},{12,0},{16,20},{20,24},{24,28},{28,16},{32,36},... | collective-permute-start | bytes 392 | tf_op jit(solution)/shard_map/ppermute | solution.py:50
  (8 other events, 120.9 us)

commit v2 on v1

v2 whole, which is shorter than its diff:
```python
import math

import jax
import jax.numpy as jnp
from jax import lax
from jax.experimental import pallas as pl
from jax.experimental.pallas import tpu as pltpu
from jax.sharding import PartitionSpec as P

HEAD_COUNT = 32
HEAD_DIM = 128
MODEL_DIM = 4096
GRAD_RANK = 8
QUERIES = 64
DAMPING = 0.1
FACTOR = 1.0 / (GRAD_RANK * math.sqrt(HEAD_COUNT * HEAD_DIM * MODEL_DIM))

N = 4
HEADS = 8
SEQS = 8
FEATURES = 1024
COLUMNS = QUERIES * GRAD_RANK
BLOCK = COLUMNS // N


def axis_shift(axis, step):
    pairs = []
    for z in range(N):
        for x in range(N):
            for y in range(N):
                to = {"z": z, "x": x, "y": y}
                to[axis] = (to[axis] + step) % N
                pairs.append((z * 16 + x * 4 + y, to["z"] * 16 + to["x"] * 4 + to["y"]))
    return pairs


def swap_shift(step):
    pairs = []
    for z in range(N):
        for x in range(N):
            for y in range(N):
                for g in range(N):
                    source = (z * 16 + x * 4 + y) * N + g
                    target = (((z + step) % N) * 16 + x * 4 + g) * N + y
                    pairs.append((source, target))
    return pairs


def along(axis, value, step):
    return lax.ppermute(value, "loop", axis_shift(axis, step))


def swapped(value, step):
    return lax.ppermute(value, ("loop", "head"), swap_shift(step))


def across_heads(value, mask):
    return lax.ppermute(value, "head", [(i, i ^ mask) for i in range(N)])


VMEM = pl.BlockSpec(memory_space=pltpu.VMEM)
SMEM = pl.BlockSpec(memory_space=pltpu.SMEM)
TILES = FEATURES // 128


def rotate_kernel(query, right, train, basis, left_out, right_out):
    for h in range(HEADS):
        left = jnp.concatenate([query[0, h], train[0, h], train[1, h]], axis=0)
        left = jnp.dot(left, basis[h], preferred_element_type=jnp.float32).astype(jnp.bfloat16)
        for n in range(3):
            left_out[n, h] = left[8 * n : 8 * (n + 1)]
    for j in range(TILES):
        right_out[0, j] = right[0, :, 128 * j : 128 * (j + 1)]


def rotated(query_left, query_right, train_left, basis):
    return pl.pallas_call(
        rotate_kernel,
        out_shape=(
            jax.ShapeDtypeStruct((3, HEADS, GRAD_RANK, HEAD_DIM), jnp.bfloat16),
            jax.ShapeDtypeStruct((1, TILES, GRAD_RANK, 128), jnp.bfloat16),
        ),
    )(query_left, query_right, train_left, basis)


def score_kernel(place, *refs):
    lefts = refs[0:4]
    rights = refs[4:8]
    eigen, out, tl_all, tr_all, qr_all, ql_head, scaled, total, eigen_all, sems = refs[8:]
    z, x, y, g = (place[i] for i in range(4))
    fetches = [
        pltpu.make_async_copy(eigen.at[HEADS * y + h], eigen_all.at[h], sems.at[h]) for h in range(HEADS)
    ]
    for fetch in fetches:
        fetch.start()

    total[...] = jnp.zeros_like(total)
    for m in range(N):
        tl_all[lax.rem(y - (g ^ m) + N, N)] = lefts[m][16:]
    for k in range(N):
        m = g ^ ((y - k) & 3)
        columns = pl.ds(pl.multiple_of(m * BLOCK, BLOCK), BLOCK)
        for j in range(TILES):
            tile = slice(128 * j, 128 * (j + 1))
            tr_all[16 * k : 16 * (k + 1), tile] = rights[k][16:, j].reshape(16, 128)
            qr_all[tile, columns] = rights[k][:16, j].reshape(BLOCK, 128).T

    def expand(head, slot):
        pltpu.make_async_copy(eigen.at[HEADS * y + head], eigen_all.at[head], sems.at[head]).wait()
        inverse = 1.0 / (eigen_all[head].astype(jnp.float32) + DAMPING)
        left = tl_all[:, :, head].reshape(SEQS * GRAD_RANK, HEAD_DIM)
        left = jnp.concatenate([left] * SEQS, axis=1)
        own = lax.broadcasted_iota(jnp.int32, left.shape, 0) // GRAD_RANK
        own = own == lax.broadcasted_iota(jnp.int32, left.shape, 1) // HEAD_DIM
        left = jnp.where(own, left, jnp.zeros_like(left))
        dense = lax.dot_general(left, tr_all[...], (((0,), (0,)), ((), ())), preferred_element_type=jnp.float32)
        dense = dense.reshape(SEQS, HEAD_DIM, FEATURES) * inverse[None]
        scaled[slot] = dense.astype(jnp.bfloat16).reshape(SEQS * HEAD_DIM, FEATURES)

    def multiply(head, slot):
        for m in range(N):
            block = lefts[m][:16, head].reshape(BLOCK, HEAD_DIM)
            ql_head[:, BLOCK * m : BLOCK * (m + 1)] = block.astype(jnp.float32).T
        product = jnp.dot(scaled[slot], qr_all[...], preferred_element_type=jnp.float32)
        product = product.reshape(SEQS, HEAD_DIM, COLUMNS) * ql_head[...][None]
        total[...] += jnp.sum(product, axis=1)

    expand(0, 0)

    @pl.loop(0, HEADS - 1)
    def _(head):
        slot = lax.rem(head, 2)
        expand(head + 1, 1 - slot)
        multiply(head, slot)

    multiply(HEADS - 1, (HEADS - 1) % 2)

    column = lax.broadcasted_iota(jnp.int32, (COLUMNS, QUERIES), 0)
    target = lax.broadcasted_iota(jnp.int32, (COLUMNS, QUERIES), 1)
    yq = g ^ (column // BLOCK)
    xq = (x - (column // 32) % N) & 3
    zq = (z - (column // 8) % N) & 3
    pick = ((g ^ zq) * 16 + xq * 4 + yq == target).astype(jnp.float32)
    picked = lax.dot_general(
        total[...], pick, (((1,), (0,)), ((), ())),
        preferred_element_type=jnp.float32, precision=lax.Precision.HIGHEST,
    )
    for m in range(N):
        out[m] = picked[:, 16 * m : 16 * (m + 1)]


def partial_scores(place, lefts, rights, eigen):
    return pl.pallas_call(
        score_kernel,
        out_shape=jax.ShapeDtypeStruct((N, SEQS, 16), jnp.float32),
        in_specs=[SMEM] + [VMEM] * 8 + [pl.BlockSpec(memory_space=pltpu.HBM)],
        out_specs=VMEM,
        scratch_shapes=[
            pltpu.VMEM((N, 2, HEADS, GRAD_RANK, HEAD_DIM), jnp.bfloat16),
            pltpu.VMEM((SEQS * GRAD_RANK, FEATURES), jnp.bfloat16),
            pltpu.VMEM((FEATURES, COLUMNS), jnp.bfloat16),
            pltpu.VMEM((HEAD_DIM, COLUMNS), jnp.float32),
            pltpu.VMEM((2, SEQS * HEAD_DIM, FEATURES), jnp.bfloat16),
            pltpu.VMEM((SEQS, COLUMNS), jnp.float32),
            pltpu.VMEM((HEADS, HEAD_DIM, FEATURES), jnp.bfloat16),
            pltpu.SemaphoreType.DMA((HEADS,)),
        ],
        compiler_params=pltpu.CompilerParams(vmem_limit_bytes=40 * 2**20),
    )(place, *lefts, *rights, pltpu.with_memory_space_constraint(eigen, pltpu.HBM))


def on_device(query_left, query_right, train_left, train_right, basis, eigen, counts):
    loop, g = lax.axis_index("loop"), lax.axis_index("head")
    place = jnp.stack([loop // 16, loop // 4 % 4, loop % 4, g]).astype(jnp.int32)

    left, right = rotated(query_left, query_right, train_left, basis)
    left = swapped(left, 0)

    both = jnp.concatenate([left[:1], right], 1)
    both = jnp.concatenate([both] + [along("z", both, s) for s in range(1, N)], 0)
    both = jnp.concatenate([both] + [along("x", both, s) for s in range(1, N)], 0)

    train_right = train_right.reshape(2, GRAD_RANK, TILES, 128).transpose(0, 2, 1, 3)
    rights = jnp.concatenate([both[:, HEADS:], train_right], 0)
    rights = [rights] + [along("y", rights, k) for k in range(1, N)]
    pair = jnp.concatenate([both[:, :HEADS], left[1:]], 0)
    pair = [pair, across_heads(pair, 2)]
    pair, rights = lax.optimization_barrier((pair, rights))
    lefts = [pair[0], across_heads(pair[0], 1), pair[1], across_heads(pair[1], 1)]
    partial = partial_scores(place, lefts, rights, eigen)

    summed = sum([across_heads(partial[m], m) for m in range(1, N)], partial[0])
    summed = sum([along("y", summed[2 * k : 2 * k + 2], -k) for k in range(1, N)], summed[:2])
    weights = counts.astype(jnp.float32) / 2048.0
    return (summed * weights[:, None] * FACTOR).T


def solution(mesh):
    placed = (
        P("loop", "head", None, None),
        P("loop", None, "head"),
        P("loop", "head", None, None),
        P("loop", None, "head"),
        P("head", None, None),
        P(None, None, "head"),
        P("loop"),
    )
    return jax.shard_map(
        on_device, mesh=mesh, in_specs=placed, out_specs=P("head", "loop"), check_vma=False
    )
```

time: 104 us -> 83.1 us (0.80)
  starting transfers between devices: 56.2 us -> 36.5 us
  Pallas kernels: 16.8 us -> 18.8 us
  matrix products: 1.82 us -> 0 us
  waiting for transfers between devices: 25.3 us -> 24.2 us
    ppermute x5 -> x1, starting transfers between devices: 14.7 us -> 4.58 us  [swapped(): return lax.ppermute(value, ('loop', 'head'), swap_shift(step))]
    ppermute x15 -> x12, waiting for transfers between devices: 9.88 us -> 16 us  [along(): return lax.ppermute(value, 'loop', axis_shift(axis, step))]
    ppermute x15 -> x12, starting transfers between devices: 29.2 us -> 23.4 us  [along(): return lax.ppermute(value, 'loop', axis_shift(axis, step))]
    ppermute x5 -> x1, waiting for transfers between devices: 6.13 us -> 1.97 us  [swapped(): return lax.ppermute(value, ('loop', 'head'), swap_shift(step))]
    ppermute x9 -> x6, starting transfers between devices: 12.3 us -> 8.52 us  [across_heads(): return lax.ppermute(value, 'head', [(i, i ^ mask) for i in range(N)])]
    ppermute x9 -> x6, waiting for transfers between devices: 9.3 us -> 6.23 us  [across_heads(): return lax.ppermute(value, 'head', [(i, i ^ mask) for i in range(N)])]
    pallas_call x0 -> x1, Pallas kernels: none -> 1.82 us  [rotated(): pl.pallas_call(rotate_kernel, out_shape=(jax.ShapeDtypeStruct((3, HEADS,...]
    dot_general x2 -> x0, matrix products: 1.82 us -> none  [rotated(): jnp.einsum('nhri,hij->nhrj', left, basis, preferred_element_type=jnp.floa...]
  transfers between devices with their start and end apart: 29 -> 19, of which waited for: 12 -> 15; matrix products, arithmetic and copies ran while one was open for 3% -> 0% of each run, Pallas kernels for 0% -> 0%
where the time goes in v2:
time: 83.1 us; the launch traced here: 82.8 us
  starting transfers between devices  36.5 us (44%)
  waiting for transfers between devices  24.2 us (29%)
  Pallas kernels  18.8 us (23%)
  other arithmetic  3 us (4%)
    ppermute x12, starting transfers between devices, along(): return lax.ppermute(value, 'loop', axis_shift(axis, step))  23.4 us
    pallas_call x1, Pallas kernels, partial_scores(): pl.pallas_call(score_kernel, out_shape=jax.ShapeDtypeStruct((N, SEQS, 16)...  17 us
    ppermute x12, waiting for transfers between devices, along(): return lax.ppermute(value, 'loop', axis_shift(axis, step))  16 us
    ppermute x6, starting transfers between devices, across_heads(): return lax.ppermute(value, 'head', [(i, i ^ mask) for i in range(N)])  8.52 us
    ppermute x6, waiting for transfers between devices, across_heads(): return lax.ppermute(value, 'head', [(i, i ^ mask) for i in range(N)])  6.23 us
    ppermute x1, starting transfers between devices, swapped(): return lax.ppermute(value, ('loop', 'head'), swap_shift(step))  4.58 us
    ppermute x1, waiting for transfers between devices, swapped(): return lax.ppermute(value, ('loop', 'head'), swap_shift(step))  1.97 us
    pallas_call x1, Pallas kernels, rotated(): pl.pallas_call(rotate_kernel, out_shape=(jax.ShapeDtypeStruct((3, HEADS,...  1.82 us
  transfers between devices with their start and end apart: 19, of which 15 were waited for; matrix products, arithmetic and copies ran while one was open for 0% of the time, Pallas kernels for 0%

profile of v2, /device:TPU:1, one launch (start us, length us, event | category | flops | bytes accessed | tf_op | source)
XLA Modules:
  0.0 82.8 jit_solution(12763203552391425642)
XLA Ops:
  0.0 1.8 %shard_map.73 = (bf16[3,8,8,128]{3,2,1,0:T(8,128)(2,1)}, bf16[1,8,8,128]{3,2,1,0:T(8,128)(2,1)}) custom-call(bf16[1,8,8,128]{3,2,1,0:T(8,128)(2,1)} %query.1, bf16[1,8,1024]{2,1,0:T(8,128)(2,1)} %right.1, bf16[2,8,8,128]{3,2,1,0:T(8,128)(2,1)} %train.1, bf16[8,128,128]{2,1,0:T(8,128)(2,1)} %basis.1), custom_call_target="tpu_custom_call" | custom-call | tf_op jit(solution)/shard_map/pallas_call | solution.py:77
  1.8 4.6 %collective-permute-start = (bf16[3,8,8,128]{3,2,1,0:T(8,128)(2,1)}, bf16[3,8,8,128]{3,2,1,0:T(8,128)(2,1)S(1)}, u32[]{:S(2)}, u32[]{:S(2)}) collective-permute-start(bf16[3,8,8,128]{3,2,1,0:T(8,128)(2,1)} %get-tuple-element.13), channel_id=1, source_target_pairs={{0,0},{1,4},{2,8},{3,12},{4,1},{5,5},{6,9},{7,13},{8,2},{9,6},{10,... | collective-permute-start | bytes 147464 | tf_op jit(solution)/shard_map/ppermute | solution.py:54
  6.4 2.0 %collective-permute-done = bf16[3,8,8,128]{3,2,1,0:T(8,128)(2,1)S(1)} collective-permute-done((bf16[3,8,8,128]{3,2,1,0:T(8,128)(2,1)}, bf16[3,8,8,128]{3,2,1,0:T(8,128)(2,1)S(1)}, u32[]{:S(2)}, u32[]{:S(2)}) %collective-permute-start) | collective-permute-done | bytes 49184 | tf_op jit(solution)/shard_map/ppermute | solution.py:54
  9.1 3.0 %collective-permute-start.1 = (bf16[1,16,8,128]{3,2,1,0:T(8,128)(2,1)S(1)}, bf16[1,16,8,128]{3,2,1,0:T(8,128)(2,1)S(1)}, u32[]{:S(2)}, u32[]{:S(2)}) collective-permute-start(bf16[1,16,8,128]{3,2,1,0:T(8,128)(2,1)S(1)} %get-tuple-element.23), channel_id=1, source_target_pairs={{0,64},{4,68},{8,72},{12,76},{16,80},{20,84},{24,88},{28,92},{32,9... | collective-permute-start | bytes 98312 | tf_op jit(solution)/shard_map/ppermute | solution.py:50
  12.1 5.1 %collective-permute-start.2 = (bf16[1,16,8,128]{3,2,1,0:T(8,128)(2,1)S(1)}, bf16[1,16,8,128]{3,2,1,0:T(8,128)(2,1)S(1)}, u32[]{:S(2)}, u32[]{:S(2)}) collective-permute-start(bf16[1,16,8,128]{3,2,1,0:T(8,128)(2,1)S(1)} %get-tuple-element.23), channel_id=1, source_target_pairs={{0,128},{4,132},{8,136},{12,140},{16,144},{20,148},{24,152},{28,15... | collective-permute-start | bytes 98312 | tf_op jit(solution)/shard_map/ppermute | solution.py:50
  17.2 2.4 %collective-permute-start.3 = (bf16[1,16,8,128]{3,2,1,0:T(8,128)(2,1)S(1)}, bf16[1,16,8,128]{3,2,1,0:T(8,128)(2,1)S(1)}, u32[]{:S(2)}, u32[]{:S(2)}) collective-permute-start(bf16[1,16,8,128]{3,2,1,0:T(8,128)(2,1)S(1)} %get-tuple-element.23), channel_id=1, source_target_pairs={{0,192},{4,196},{8,200},{12,204},{16,208},{20,212},{24,216},{28,22... | collective-permute-start | bytes 98312 | tf_op jit(solution)/shard_map/ppermute | solution.py:50
  19.6 1.3 %collective-permute-done.3 = bf16[1,16,8,128]{3,2,1,0:T(8,128)(2,1)S(1)} collective-permute-done((bf16[1,16,8,128]{3,2,1,0:T(8,128)(2,1)S(1)}, bf16[1,16,8,128]{3,2,1,0:T(8,128)(2,1)S(1)}, u32[]{:S(2)}, u32[]{:S(2)}) %collective-permute-start.3) | collective-permute-done | bytes 32800 | tf_op jit(solution)/shard_map/ppermute | solution.py:50
  21.6 1.3 %collective-permute-start.4 = (bf16[4,16,8,128]{3,2,1,0:T(8,128)(2,1)S(1)}, bf16[4,16,8,128]{3,2,1,0:T(8,128)(2,1)S(1)}, u32[]{:S(2)}, u32[]{:S(2)}) collective-permute-start(bf16[4,16,8,128]{3,2,1,0:T(8,128)(2,1)S(1)} %pad_maximum_fusion.2), channel_id=1, source_target_pairs={{0,16},{4,20},{8,24},{12,28},{16,32},{20,36},{24,40},{28,44},{32,4... | collective-permute-start | bytes 393224 | tf_op jit(solution)/shard_map/ppermute | solution.py:50
  22.9 2.5 %collective-permute-start.5 = (bf16[4,16,8,128]{3,2,1,0:T(8,128)(2,1)S(1)}, bf16[4,16,8,128]{3,2,1,0:T(8,128)(2,1)S(1)}, u32[]{:S(2)}, u32[]{:S(2)}) collective-permute-start(bf16[4,16,8,128]{3,2,1,0:T(8,128)(2,1)S(1)} %pad_maximum_fusion.2), channel_id=1, source_target_pairs={{0,32},{4,36},{8,40},{12,44},{16,48},{20,52},{24,56},{28,60},{32,0... | collective-permute-start | bytes 393224 | tf_op jit(solution)/shard_map/ppermute | solution.py:50
  25.4 1.2 %collective-permute-start.6 = (bf16[4,16,8,128]{3,2,1,0:T(8,128)(2,1)S(1)}, bf16[4,16,8,128]{3,2,1,0:T(8,128)(2,1)S(1)}, u32[]{:S(2)}, u32[]{:S(2)}) collective-permute-start(bf16[4,16,8,128]{3,2,1,0:T(8,128)(2,1)S(1)} %pad_maximum_fusion.2), channel_id=1, source_target_pairs={{0,48},{4,52},{8,56},{12,60},{16,0},{20,4},{24,8},{28,12},{32,16},... | collective-permute-start | bytes 393224 | tf_op jit(solution)/shard_map/ppermute | solution.py:50
  27.6 2.9 %collective-permute-done.5 = bf16[4,16,8,128]{3,2,1,0:T(8,128)(2,1)S(1)} collective-permute-done((bf16[4,16,8,128]{3,2,1,0:T(8,128)(2,1)S(1)}, bf16[4,16,8,128]{3,2,1,0:T(8,128)(2,1)S(1)}, u32[]{:S(2)}, u32[]{:S(2)}) %collective-permute-start.5) | collective-permute-done | bytes 131104 | tf_op jit(solution)/shard_map/ppermute | solution.py:50
  31.4 4.6 %collective-permute-start.10 = (bf16[18,8,8,128]{3,2,1,0:T(8,128)(2,1)S(1)}, bf16[18,8,8,128]{3,2,1,0:T(8,128)(2,1)S(1)}, u32[]{:S(2)}, u32[]{:S(2)}) collective-permute-start(bf16[18,8,8,128]{3,2,1,0:T(8,128)(2,1)S(1)} %pad_maximum_fusion.1.refs_4_), channel_id=1, source_target_pairs={{0,12},{4,0},{8,4},{12,8},{16,28},{20,16},{24,20},{28,24},{32,44},... | collective-permute-start | bytes 884744 | tf_op jit(solution)/shard_map/ppermute | solution.py:50
  36.2 1.7 %collective-permute-start.9 = (bf16[18,8,8,128]{3,2,1,0:T(8,128)(2,1)S(1)}, bf16[18,8,8,128]{3,2,1,0:T(8,128)(2,1)S(1)}, u32[]{:S(2)}, u32[]{:S(2)}) collective-permute-start(bf16[18,8,8,128]{3,2,1,0:T(8,128)(2,1)S(1)} %pad_maximum_fusion.1.refs_4_), channel_id=1, source_target_pairs={{0,8},{4,12},{8,0},{12,4},{16,24},{20,28},{24,16},{28,20},{32,40},... | collective-permute-start | bytes 884744 | tf_op jit(solution)/shard_map/ppermute | solution.py:50
  38.0 1.7 %collective-permute-done.10.refs_7_ = bf16[18,8,8,128]{3,2,1,0:T(8,128)(2,1)S(1)} collective-permute-done((bf16[18,8,8,128]{3,2,1,0:T(8,128)(2,1)S(1)}, bf16[18,8,8,128]{3,2,1,0:T(8,128)(2,1)S(1)}, u32[]{:S(2)}, u32[]{:S(2)}) %collective-permute-start.10) | collective-permute-done | bytes 294944 | tf_op jit(solution)/shard_map/ppermute | solution.py:50
  39.7 2.0 %collective-permute-done.7.refs_2_ = bf16[18,8,8,128]{3,2,1,0:T(8,128)(2,1)S(1)} collective-permute-done((bf16[18,8,8,128]{3,2,1,0:T(8,128)(2,1)S(1)}, bf16[18,8,8,128]{3,2,1,0:T(8,128)(2,1)S(1)}, u32[]{:S(2)}, u32[]{:S(2)}) %collective-permute-start.7) | collective-permute-done | bytes 294944 | tf_op jit(solution)/shard_map/ppermute | solution.py:58
  41.7 5.0 %collective-permute-done.8.refs_5_ = bf16[18,8,8,128]{3,2,1,0:T(8,128)(2,1)S(1)} collective-permute-done((bf16[18,8,8,128]{3,2,1,0:T(8,128)(2,1)S(1)}, bf16[18,8,8,128]{3,2,1,0:T(8,128)(2,1)S(1)}, u32[]{:S(2)}, u32[]{:S(2)}) %collective-permute-start.8) | collective-permute-done | bytes 294944 | tf_op jit(solution)/shard_map/ppermute | solution.py:50
  47.2 6.0 %collective-permute-start.11 = (bf16[18,8,8,128]{3,2,1,0:T(8,128)(2,1)S(1)}, bf16[18,8,8,128]{3,2,1,0:T(8,128)(2,1)S(1)}, u32[]{:S(2)}, u32[]{:S(2)}) collective-permute-start(bf16[18,8,8,128]{3,2,1,0:T(8,128)(2,1)S(1)} %pad_maximum_fusion.refs_0_), channel_id=1, source_target_pairs={{0,1},{1,0},{2,3},{3,2},{4,5},{5,4},{6,7},{7,6},{8,9},{9,8},{10,11... | collective-permute-start | bytes 884744 | tf_op jit(solution)/shard_map/ppermute | solution.py:58
  53.2 1.1 %collective-permute-done.11.refs_1_ = bf16[18,8,8,128]{3,2,1,0:T(8,128)(2,1)S(1)} collective-permute-done((bf16[18,8,8,128]{3,2,1,0:T(8,128)(2,1)S(1)}, bf16[18,8,8,128]{3,2,1,0:T(8,128)(2,1)S(1)}, u32[]{:S(2)}, u32[]{:S(2)}) %collective-permute-start.11) | collective-permute-done | bytes 294944 | tf_op jit(solution)/shard_map/ppermute | solution.py:58
  54.8 17.0 %shard_map.74 = f32[4,8,16]{2,1,0:T(8,128)S(1)} custom-call(s32[4]{0:T(128)S(1)} %pad_add_fusion.place, bf16[18,8,8,128]{3,2,1,0:T(8,128)(2,1)S(1)} %pad_maximum_fusion.refs_0_, bf16[18,8,8,128]{3,2,1,0:T(8,128)(2,1)S(1)} %collective-permute-done.11.refs_1_, bf16[18,8,8,128]{3,2,1,0:T(8,128)(2,1)S(1)} %collective-permute-done.7.refs_2_, ...), custom_call_target="tpu_custom_call" | custom-call | tf_op jit(solution)/shard_map/pallas_call | solution.py:153
  72.5 1.4 %collective-permute-start.14 = (f32[8,16]{1,0:T(8,128)S(1)}, f32[8,16]{1,0:T(8,128)S(1)}, u32[]{:S(2)}, u32[]{:S(2)}) collective-permute-start(f32[8,16]{1,0:T(8,128)S(1)} %get-tuple-element.27), channel_id=1, source_target_pairs={{0,2},{1,3},{2,0},{3,1},{4,6},{5,7},{6,4},{7,5},{8,10},{9,11},{10,... | collective-permute-start | bytes 1544 | tf_op jit(solution)/shard_map/ppermute | solution.py:58
  74.9 2.0 %collective-permute-done.15 = f32[8,16]{1,0:T(8,128)S(1)} collective-permute-done((f32[8,16]{1,0:T(8,128)S(1)}, f32[8,16]{1,0:T(8,128)S(1)}, u32[]{:S(2)}, u32[]{:S(2)}) %collective-permute-start.15) | collective-permute-done | bytes 544 | tf_op jit(solution)/shard_map/ppermute | solution.py:58
  77.4 1.1 %collective-permute-start.18 = (f32[2,16]{1,0:T(2,128)S(1)}, f32[2,16]{1,0:T(2,128)S(1)}, u32[]{:S(2)}, u32[]{:S(2)}) collective-permute-start(f32[2,16]{1,0:T(2,128)S(1)} %get-tuple-element.29), channel_id=1, source_target_pairs={{0,4},{4,8},{8,12},{12,0},{16,20},{20,24},{24,28},{28,16},{32,36},... | collective-permute-start | bytes 392 | tf_op jit(solution)/shard_map/ppermute | solution.py:50
  79.4 1.6 %collective-permute-done.17 = f32[2,16]{1,0:T(2,128)S(1)} collective-permute-done((f32[2,16]{1,0:T(2,128)S(1)}, f32[2,16]{1,0:T(2,128)S(1)}, u32[]{:S(2)}, u32[]{:S(2)}) %collective-permute-start.17) | collective-permute-done | bytes 160 | tf_op jit(solution)/shard_map/ppermute | solution.py:50
  81.0 1.1 %collective-permute-done.18 = f32[2,16]{1,0:T(2,128)S(1)} collective-permute-done((f32[2,16]{1,0:T(2,128)S(1)}, f32[2,16]{1,0:T(2,128)S(1)}, u32[]{:S(2)}, u32[]{:S(2)}) %collective-permute-start.18) | collective-permute-done | bytes 160 | tf_op jit(solution)/shard_map/ppermute | solution.py:50
  (37 shorter events, 8.4 us)
Async XLA Ops:
  0.0 74.3 %copy-start = (s32[2]{0:T(128)S(1)}, s32[2]{0:T(128)}, u32[]{:S(2)}) copy-start(s32[2]{0:T(128)} %param.13) | copy-start | bytes 28
  1.8 6.6 %collective-permute-start = (bf16[3,8,8,128]{3,2,1,0:T(8,128)(2,1)}, bf16[3,8,8,128]{3,2,1,0:T(8,128)(2,1)S(1)}, u32[]{:S(2)}, u32[]{:S(2)}) collective-permute-start(bf16[3,8,8,128]{3,2,1,0:T(8,128)(2,1)} %get-tuple-element.13), channel_id=1, source_target_pairs={{0,0},{1,4},{2,8},{3,12},{4,1},{5,5},{6,9},{7,13},{8,2},{9,6},{10,... | collective-permute-start | bytes 147464 | tf_op jit(solution)/shard_map/ppermute | solution.py:54
  9.1 10.5 %collective-permute-start.1 = (bf16[1,16,8,128]{3,2,1,0:T(8,128)(2,1)S(1)}, bf16[1,16,8,128]{3,2,1,0:T(8,128)(2,1)S(1)}, u32[]{:S(2)}, u32[]{:S(2)}) collective-permute-start(bf16[1,16,8,128]{3,2,1,0:T(8,128)(2,1)S(1)} %get-tuple-element.23), channel_id=1, source_target_pairs={{0,64},{4,68},{8,72},{12,76},{16,80},{20,84},{24,88},{28,92},{32,9... | collective-permute-start | bytes 98312 | tf_op jit(solution)/shard_map/ppermute | solution.py:50
  12.1 7.5 %collective-permute-start.2 = (bf16[1,16,8,128]{3,2,1,0:T(8,128)(2,1)S(1)}, bf16[1,16,8,128]{3,2,1,0:T(8,128)(2,1)S(1)}, u32[]{:S(2)}, u32[]{:S(2)}) collective-permute-start(bf16[1,16,8,128]{3,2,1,0:T(8,128)(2,1)S(1)} %get-tuple-element.23), channel_id=1, source_target_pairs={{0,128},{4,132},{8,136},{12,140},{16,144},{20,148},{24,152},{28,15... | collective-permute-start | bytes 98312 | tf_op jit(solution)/shard_map/ppermute | solution.py:50
  17.2 3.7 %collective-permute-start.3 = (bf16[1,16,8,128]{3,2,1,0:T(8,128)(2,1)S(1)}, bf16[1,16,8,128]{3,2,1,0:T(8,128)(2,1)S(1)}, u32[]{:S(2)}, u32[]{:S(2)}) collective-permute-start(bf16[1,16,8,128]{3,2,1,0:T(8,128)(2,1)S(1)} %get-tuple-element.23), channel_id=1, source_target_pairs={{0,192},{4,196},{8,200},{12,204},{16,208},{20,212},{24,216},{28,22... | collective-permute-start | bytes 98312 | tf_op jit(solution)/shard_map/ppermute | solution.py:50
  21.6 6.0 %collective-permute-start.4 = (bf16[4,16,8,128]{3,2,1,0:T(8,128)(2,1)S(1)}, bf16[4,16,8,128]{3,2,1,0:T(8,128)(2,1)S(1)}, u32[]{:S(2)}, u32[]{:S(2)}) collective-permute-start(bf16[4,16,8,128]{3,2,1,0:T(8,128)(2,1)S(1)} %pad_maximum_fusion.2), channel_id=1, source_target_pairs={{0,16},{4,20},{8,24},{12,28},{16,32},{20,36},{24,40},{28,44},{32,4... | collective-permute-start | bytes 393224 | tf_op jit(solution)/shard_map/ppermute | solution.py:50
  22.9 7.6 %collective-permute-start.5 = (bf16[4,16,8,128]{3,2,1,0:T(8,128)(2,1)S(1)}, bf16[4,16,8,128]{3,2,1,0:T(8,128)(2,1)S(1)}, u32[]{:S(2)}, u32[]{:S(2)}) collective-permute-start(bf16[4,16,8,128]{3,2,1,0:T(8,128)(2,1)S(1)} %pad_maximum_fusion.2), channel_id=1, source_target_pairs={{0,32},{4,36},{8,40},{12,44},{16,48},{20,52},{24,56},{28,60},{32,0... | collective-permute-start | bytes 393224 | tf_op jit(solution)/shard_map/ppermute | solution.py:50
  25.4 5.1 %collective-permute-start.6 = (bf16[4,16,8,128]{3,2,1,0:T(8,128)(2,1)S(1)}, bf16[4,16,8,128]{3,2,1,0:T(8,128)(2,1)S(1)}, u32[]{:S(2)}, u32[]{:S(2)}) collective-permute-start(bf16[4,16,8,128]{3,2,1,0:T(8,128)(2,1)S(1)} %pad_maximum_fusion.2), channel_id=1, source_target_pairs={{0,48},{4,52},{8,56},{12,60},{16,0},{20,4},{24,8},{28,12},{32,16},... | collective-permute-start | bytes 393224 | tf_op jit(solution)/shard_map/ppermute | solution.py:50
  31.4 8.3 %collective-permute-start.10 = (bf16[18,8,8,128]{3,2,1,0:T(8,128)(2,1)S(1)}, bf16[18,8,8,128]{3,2,1,0:T(8,128)(2,1)S(1)}, u32[]{:S(2)}, u32[]{:S(2)}) collective-permute-start(bf16[18,8,8,128]{3,2,1,0:T(8,128)(2,1)S(1)} %pad_maximum_fusion.1.refs_4_), channel_id=1, source_target_pairs={{0,12},{4,0},{8,4},{12,8},{16,28},{20,16},{24,20},{28,24},{32,44},... | collective-permute-start | bytes 884744 | tf_op jit(solution)/shard_map/ppermute | solution.py:50
  36.0 5.7 %collective-permute-start.7 = (bf16[18,8,8,128]{3,2,1,0:T(8,128)(2,1)S(1)}, bf16[18,8,8,128]{3,2,1,0:T(8,128)(2,1)S(1)}, u32[]{:S(2)}, u32[]{:S(2)}) collective-permute-start(bf16[18,8,8,128]{3,2,1,0:T(8,128)(2,1)S(1)} %pad_maximum_fusion.refs_0_), channel_id=1, source_target_pairs={{0,2},{1,3},{2,0},{3,1},{4,6},{5,7},{6,4},{7,5},{8,10},{9,11},{10,... | collective-permute-start | bytes 884744 | tf_op jit(solution)/shard_map/ppermute | solution.py:58
  36.1 10.6 %collective-permute-start.8 = (bf16[18,8,8,128]{3,2,1,0:T(8,128)(2,1)S(1)}, bf16[18,8,8,128]{3,2,1,0:T(8,128)(2,1)S(1)}, u32[]{:S(2)}, u32[]{:S(2)}) collective-permute-start(bf16[18,8,8,128]{3,2,1,0:T(8,128)(2,1)S(1)} %pad_maximum_fusion.1.refs_4_), channel_id=1, source_target_pairs={{0,4},{4,8},{8,12},{12,0},{16,20},{20,24},{24,28},{28,16},{32,36},... | collective-permute-start | bytes 884744 | tf_op jit(solution)/shard_map/ppermute | solution.py:50
  36.2 10.9 %collective-permute-start.9 = (bf16[18,8,8,128]{3,2,1,0:T(8,128)(2,1)S(1)}, bf16[18,8,8,128]{3,2,1,0:T(8,128)(2,1)S(1)}, u32[]{:S(2)}, u32[]{:S(2)}) collective-permute-start(bf16[18,8,8,128]{3,2,1,0:T(8,128)(2,1)S(1)} %pad_maximum_fusion.1.refs_4_), channel_id=1, source_target_pairs={{0,8},{4,12},{8,0},{12,4},{16,24},{20,28},{24,16},{28,20},{32,40},... | collective-permute-start | bytes 884744 | tf_op jit(solution)/shard_map/ppermute | solution.py:50
  47.2 7.2 %collective-permute-start.11 = (bf16[18,8,8,128]{3,2,1,0:T(8,128)(2,1)S(1)}, bf16[18,8,8,128]{3,2,1,0:T(8,128)(2,1)S(1)}, u32[]{:S(2)}, u32[]{:S(2)}) collective-permute-start(bf16[18,8,8,128]{3,2,1,0:T(8,128)(2,1)S(1)} %pad_maximum_fusion.refs_0_), channel_id=1, source_target_pairs={{0,1},{1,0},{2,3},{3,2},{4,5},{5,4},{6,7},{7,6},{8,9},{9,8},{10,11... | collective-permute-start | bytes 884744 | tf_op jit(solution)/shard_map/ppermute | solution.py:58
  53.2 1.6 %collective-permute-start.12 = (bf16[18,8,8,128]{3,2,1,0:T(8,128)(2,1)S(1)}, bf16[18,8,8,128]{3,2,1,0:T(8,128)(2,1)S(1)}, u32[]{:S(2)}, u32[]{:S(2)}) collective-permute-start(bf16[18,8,8,128]{3,2,1,0:T(8,128)(2,1)S(1)} %collective-permute-done.7.refs_2_), channel_id=1, source_target_pairs={{0,1},{1,0},{2,3},{3,2},{4,5},{5,4},{6,7},{7,6},{8,9},{9,8},{10,11... | collective-permute-start | bytes 884744 | tf_op jit(solution)/shard_map/ppermute | solution.py:58
  71.8 2.4 %collective-permute-start.13 = (f32[8,16]{1,0:T(8,128)S(1)}, f32[8,16]{1,0:T(8,128)S(1)}, u32[]{:S(2)}, u32[]{:S(2)}) collective-permute-start(f32[8,16]{1,0:T(8,128)S(1)} %get-tuple-element.25), channel_id=1, source_target_pairs={{0,1},{1,0},{2,3},{3,2},{4,5},{5,4},{6,7},{7,6},{8,9},{9,8},{10,11... | collective-permute-start | bytes 1544 | tf_op jit(solution)/shard_map/ppermute | solution.py:58
  72.5 2.5 %collective-permute-start.14 = (f32[8,16]{1,0:T(8,128)S(1)}, f32[8,16]{1,0:T(8,128)S(1)}, u32[]{:S(2)}, u32[]{:S(2)}) collective-permute-start(f32[8,16]{1,0:T(8,128)S(1)} %get-tuple-element.27), channel_id=1, source_target_pairs={{0,2},{1,3},{2,0},{3,1},{4,6},{5,7},{6,4},{7,5},{8,10},{9,11},{10,... | collective-permute-start | bytes 1544 | tf_op jit(solution)/shard_map/ppermute | solution.py:58
  73.8 3.1 %collective-permute-start.15 = (f32[8,16]{1,0:T(8,128)S(1)}, f32[8,16]{1,0:T(8,128)S(1)}, u32[]{:S(2)}, u32[]{:S(2)}) collective-permute-start(f32[8,16]{1,0:T(8,128)S(1)} %get-tuple-element.26), channel_id=1, source_target_pairs={{0,3},{1,2},{2,1},{3,0},{4,7},{5,6},{6,5},{7,4},{8,11},{9,10},{10,... | collective-permute-start | bytes 1544 | tf_op jit(solution)/shard_map/ppermute | solution.py:58
  76.9 2.5 %collective-permute-start.16 = (f32[2,16]{1,0:T(2,128)S(1)}, f32[2,16]{1,0:T(2,128)S(1)}, u32[]{:S(2)}, u32[]{:S(2)}) collective-permute-start(f32[2,16]{1,0:T(2,128)S(1)} %get-tuple-element.28), channel_id=1, source_target_pairs={{0,12},{4,0},{8,4},{12,8},{16,28},{20,16},{24,20},{28,24},{32,44},... | collective-permute-start | bytes 392 | tf_op jit(solution)/shard_map/ppermute | solution.py:50
  77.0 4.0 %collective-permute-start.17 = (f32[2,16]{1,0:T(2,128)S(1)}, f32[2,16]{1,0:T(2,128)S(1)}, u32[]{:S(2)}, u32[]{:S(2)}) collective-permute-start(f32[2,16]{1,0:T(2,128)S(1)} %get-tuple-element.30), channel_id=1, source_target_pairs={{0,8},{4,12},{8,0},{12,4},{16,24},{20,28},{24,16},{28,20},{32,40},... | collective-permute-start | bytes 392 | tf_op jit(solution)/shard_map/ppermute | solution.py:50
  77.4 4.7 %collective-permute-start.18 = (f32[2,16]{1,0:T(2,128)S(1)}, f32[2,16]{1,0:T(2,128)S(1)}, u32[]{:S(2)}, u32[]{:S(2)}) collective-permute-start(f32[2,16]{1,0:T(2,128)S(1)} %get-tuple-element.29), channel_id=1, source_target_pairs={{0,4},{4,8},{8,12},{12,0},{16,20},{20,24},{24,28},{28,16},{32,36},... | collective-permute-start | bytes 392 | tf_op jit(solution)/shard_map/ppermute | solution.py:50

commit v3 on v2

v3 whole, which is shorter than its diff:
```python
import functools
import math

import jax
import jax.numpy as jnp
from jax import lax
from jax.experimental import pallas as pl
from jax.experimental.pallas import tpu as pltpu
from jax.sharding import PartitionSpec as P

HEAD_COUNT = 32
HEAD_DIM = 128
MODEL_DIM = 4096
GRAD_RANK = 8
QUERIES = 64
DAMPING = 0.1
FACTOR = 1.0 / (GRAD_RANK * math.sqrt(HEAD_COUNT * HEAD_DIM * MODEL_DIM))

N = 4
HEADS = 8
SEQS = 8
FEATURES = 1024
COLUMNS = QUERIES * GRAD_RANK
BLOCK = COLUMNS // N


def axis_shift(axis, step):
    pairs = []
    for z in range(N):
        for x in range(N):
            for y in range(N):
                to = {"z": z, "x": x, "y": y}
                to[axis] = (to[axis] + step) % N
                pairs.append((z * 16 + x * 4 + y, to["z"] * 16 + to["x"] * 4 + to["y"]))
    return pairs


def swap_shift(step):
    pairs = []
    for z in range(N):
        for x in range(N):
            for y in range(N):
                for g in range(N):
                    source = (z * 16 + x * 4 + y) * N + g
                    target = (((z + step) % N) * 16 + x * 4 + g) * N + y
                    pairs.append((source, target))
    return pairs


def along(axis, value, step):
    return lax.ppermute(value, "loop", axis_shift(axis, step))


def swapped(value, step):
    return lax.ppermute(value, ("loop", "head"), swap_shift(step))


def across_heads(value, mask):
    return lax.ppermute(value, "head", [(i, i ^ mask) for i in range(N)])


VMEM = pl.BlockSpec(memory_space=pltpu.VMEM)
SMEM = pl.BlockSpec(memory_space=pltpu.SMEM)
TILES = FEATURES // 128


def rotate_kernel(query, right, train, train_right, basis, left_out, right_out, train_right_out):
    for h in range(HEADS):
        left = jnp.concatenate([query[0, h], train[0, h], train[1, h]], axis=0)
        left = jnp.dot(left, basis[h], preferred_element_type=jnp.float32).astype(jnp.bfloat16)
        for n in range(3):
            left_out[n, h] = left[8 * n : 8 * (n + 1)]
    for j in range(TILES):
        tile = slice(128 * j, 128 * (j + 1))
        right_out[0, j] = right[0, :, tile]
        train_right_out[0, j] = train_right[0, :, tile]
        train_right_out[1, j] = train_right[1, :, tile]


def rotated(query_left, query_right, train_left, train_right, basis):
    return pl.pallas_call(
        rotate_kernel,
        out_shape=(
            pltpu.VMEM((3, HEADS, GRAD_RANK, HEAD_DIM), jnp.bfloat16),
            pltpu.VMEM((1, TILES, GRAD_RANK, 128), jnp.bfloat16),
            pltpu.VMEM((2, TILES, GRAD_RANK, 128), jnp.bfloat16),
        ),
    )(query_left, query_right, train_left, train_right, basis)


def inverse_kernel(place, eigen, inverse, fetched, sems):
    fetches = [
        pltpu.make_async_copy(eigen.at[HEADS * place[2] + h], fetched.at[h], sems.at[h]) for h in range(HEADS)
    ]
    for fetch in fetches:
        fetch.start()
    for h, fetch in enumerate(fetches):
        fetch.wait()
        inverse[h] = 1.0 / (fetched[h].astype(jnp.float32) + DAMPING)


def inverses(place, eigen):
    return pl.pallas_call(
        inverse_kernel,
        out_shape=pltpu.VMEM((HEADS, HEAD_DIM, FEATURES), jnp.float32),
        in_specs=[SMEM, pl.BlockSpec(memory_space=pltpu.HBM)],
        out_specs=VMEM,
        scratch_shapes=[
            pltpu.VMEM((HEADS, HEAD_DIM, FEATURES), jnp.bfloat16),
            pltpu.SemaphoreType.DMA((HEADS,)),
        ],
        compiler_params=pltpu.CompilerParams(vmem_limit_bytes=16 * 2**20),
        cost_estimate=pl.CostEstimate(flops=2**21, bytes_accessed=6 * 2**20, transcendentals=2**20),
    )(place, pltpu.with_memory_space_constraint(eigen, pltpu.HBM))


def scale_kernel(place, *refs):
    tl = refs[0:4]
    tr = refs[4:8]
    inverse, scaled, tl_all, tr_all = refs[8:]
    y, g = place[2], place[3]
    for m in range(N):
        tl_all[lax.rem(y - (g ^ m) + N, N)] = tl[m][...]
    for k in range(N):
        for j in range(TILES):
            tr_all[16 * k : 16 * (k + 1), 128 * j : 128 * (j + 1)] = tr[k][:, j].reshape(16, 128)

    @pl.loop(0, HEADS)
    def _(head):
        left = tl_all[:, :, head].reshape(SEQS * GRAD_RANK, HEAD_DIM)
        left = jnp.concatenate([left] * SEQS, axis=1)
        own = lax.broadcasted_iota(jnp.int32, left.shape, 0) // GRAD_RANK
        own = own == lax.broadcasted_iota(jnp.int32, left.shape, 1) // HEAD_DIM
        left = jnp.where(own, left, jnp.zeros_like(left))
        dense = lax.dot_general(left, tr_all[...], (((0,), (0,)), ((), ())), preferred_element_type=jnp.float32)
        dense = dense.reshape(SEQS, HEAD_DIM, FEATURES) * inverse[head][None]
        scaled[head] = dense.astype(jnp.bfloat16).reshape(SEQS * HEAD_DIM, FEATURES)


def scaled_heads(place, tl, tr, inverse):
    return pl.pallas_call(
        scale_kernel,
        out_shape=pltpu.VMEM((HEADS, SEQS * HEAD_DIM, FEATURES), jnp.bfloat16),
        in_specs=[SMEM] + [VMEM] * 9,
        out_specs=VMEM,
        scratch_shapes=[
            pltpu.VMEM((N, 2, HEADS, GRAD_RANK, HEAD_DIM), jnp.bfloat16),
            pltpu.VMEM((SEQS * GRAD_RANK, FEATURES), jnp.bfloat16),
        ],
        compiler_params=pltpu.CompilerParams(vmem_limit_bytes=16 * 2**20),
        cost_estimate=pl.CostEstimate(flops=2**32, bytes_accessed=2**20, transcendentals=0),
    )(place, *tl, *tr, inverse)


def product_kernel(steps, last, place, *refs):
    ql = refs[0:4]
    qr = refs[4 : 4 + len(steps)]
    scaled, *rest = refs[4 + len(steps) :]
    if last:
        before, out, ql_all, qr_all, ql_head, total = rest
    else:
        total, ql_all, qr_all, ql_head = rest
    z, x, y, g = (place[i] for i in range(4))

    total[...] = jnp.zeros_like(total)
    for n, k in enumerate(steps):
        for j in range(TILES):
            block = qr[n][:, j].reshape(BLOCK, 128)
            qr_all[128 * j : 128 * (j + 1), BLOCK * n : BLOCK * (n + 1)] = block.T
        for m in range(N):

            @pl.when((g ^ ((y - k) & 3)) == m)
            def _(n=n, m=m):
                ql_all[n] = ql[m][...]

    @pl.loop(0, HEADS)
    def _(head):
        for n in range(len(steps)):
            block = ql_all[n, :, head].reshape(BLOCK, HEAD_DIM)
            ql_head[:, BLOCK * n : BLOCK * (n + 1)] = block.astype(jnp.float32).T
        product = jnp.dot(scaled[head], qr_all[...], preferred_element_type=jnp.float32)
        product = product.reshape(SEQS, HEAD_DIM, BLOCK * len(steps)) * ql_head[...][None]
        total[...] += jnp.sum(product, axis=1)

    if last:
        column = lax.broadcasted_iota(jnp.int32, (COLUMNS, QUERIES), 0)
        target = lax.broadcasted_iota(jnp.int32, (COLUMNS, QUERIES), 1)
        block = column // BLOCK
        yq = (y - 2 * block + (block // 2) * 3) & 3
        xq = (x - (column // 32) % N) & 3
        zq = (z - (column // 8) % N) & 3
        pick = ((g ^ zq) * 16 + xq * 4 + yq == target).astype(jnp.float32)
        both = jnp.concatenate([before[...], total[...]], axis=1)
        picked = lax.dot_general(
            both, pick, (((1,), (0,)), ((), ())),
            preferred_element_type=jnp.float32, precision=lax.Precision.HIGHEST,
        )
        for m in range(N):
            out[m] = picked[:, 16 * m : 16 * (m + 1)]


def products(place, steps, ql, qr, scaled, before=None):
    columns = BLOCK * len(steps)
    last = before is not None
    operands = [place, *ql, *qr, scaled] + ([before] if last else [])
    out = (N, SEQS, 16) if last else (SEQS, columns)
    scratch = [
        pltpu.VMEM((len(steps), 16, HEADS, GRAD_RANK, HEAD_DIM), jnp.bfloat16),
        pltpu.VMEM((FEATURES, columns), jnp.bfloat16),
        pltpu.VMEM((HEAD_DIM, columns), jnp.float32),
    ]
    return pl.pallas_call(
        functools.partial(product_kernel, steps, last),
        out_shape=jax.ShapeDtypeStruct(out, jnp.float32),
        in_specs=[SMEM] + [VMEM] * (len(operands) - 1),
        out_specs=VMEM,
        scratch_shapes=scratch + ([pltpu.VMEM((SEQS, columns), jnp.float32)] if last else []),
        compiler_params=pltpu.CompilerParams(vmem_limit_bytes=16 * 2**20),
        cost_estimate=pl.CostEstimate(flops=2**20, bytes_accessed=2**12, transcendentals=0),
    )(*operands)


def on_device(query_left, query_right, train_left, train_right, basis, eigen, counts):
    loop, g = lax.axis_index("loop"), lax.axis_index("head")
    place = jnp.stack([loop // 16, loop // 4 % 4, loop % 4, g]).astype(jnp.int32)

    left, right, train_right = rotated(query_left, query_right, train_left, train_right, basis)
    left = swapped(left, 0)

    both = jnp.concatenate([left[:1], right], 1)
    both = jnp.concatenate([both] + [along("z", both, s) for s in range(1, N)], 0)

    over_x = [along("x", both, s) for s in range(1, N)]
    tr = [train_right] + [along("y", train_right, k) for k in range(1, N)]
    pair = [left[1:], across_heads(left[1:], 2)]
    tl = [pair[0], across_heads(pair[0], 1), pair[1], across_heads(pair[1], 1)]
    inverse = inverses(place, eigen)
    both, over_x, tr, tl, inverse = lax.optimization_barrier((both, over_x, tr, tl, inverse))
    both = jnp.concatenate([both, *over_x], 0)

    scaled = scaled_heads(place, tl, tr, inverse)
    right = both[:, HEADS:]
    qr = [right] + [along("y", right, k) for k in range(1, N)]
    pair = [both[:, :HEADS], across_heads(both[:, :HEADS], 2)]
    pair, qr[2], scaled = lax.optimization_barrier((pair, qr[2], scaled))
    ql = [pair[0], across_heads(pair[0], 1), pair[1], across_heads(pair[1], 1)]
    first = products(place, (0, 2), ql, qr[0::2], scaled)
    partial = products(place, (1, 3), ql, qr[1::2], scaled, first)

    summed = sum([across_heads(partial[m], m) for m in range(1, N)], partial[0])
    summed = sum([along("y", summed[2 * k : 2 * k + 2], -k) for k in range(1, N)], summed[:2])
    weights = counts.astype(jnp.float32) / 2048.0
    return (summed * weights[:, None] * FACTOR).T


def solution(mesh):
    placed = (
        P("loop", "head", None, None),
        P("loop", None, "head"),
        P("loop", "head", None, None),
        P("loop", None, "head"),
        P("head", None, None),
        P(None, None, "head"),
        P("loop"),
    )
    return jax.shard_map(
        on_device, mesh=mesh, in_specs=placed, out_specs=P("head", "loop"), check_vma=False
    )
```

time: 83.1 us -> 76.6 us (0.922)
  waiting for transfers between devices: 24.2 us -> 8.04 us
  starting transfers between devices: 36.5 us -> 43.8 us
  Pallas kernels: 18.8 us -> 23.6 us
  other arithmetic: 3 us -> 0.75 us
    ppermute x12 -> x15, waiting for transfers between devices: 16 us -> 4.7 us  [along(): return lax.ppermute(value, 'loop', axis_shift(axis, step))]
    pallas_call x2 -> x5, Pallas kernels: 18.8 us -> 23.6 us  [the longest x2 13.7 us: products(): pl.pallas_call(functools.partial(product_kernel, steps, last), out_shape=...]
    ppermute x6 -> x9, waiting for transfers between devices: 6.23 us -> 1.59 us  [across_heads(): return lax.ppermute(value, 'head', [(i, i ^ mask) for i in range(N)])]
    ppermute x12 -> x15, starting transfers between devices: 23.4 us -> 27.4 us  [along(): return lax.ppermute(value, 'loop', axis_shift(axis, step))]
    ppermute x6 -> x9, starting transfers between devices: 8.52 us -> 11.8 us  [across_heads(): return lax.ppermute(value, 'head', [(i, i ^ mask) for i in range(N)])]
  transfers between devices with their start and end apart: 19 -> 25, of which waited for: 15 -> 5; matrix products, arithmetic and copies ran while one was open for 0% -> 0% of each run, Pallas kernels for 0% -> 20%
where the time goes in v3:
time: 76.6 us; the launch traced here: 76.4 us
  starting transfers between devices  43.8 us (57%)
  Pallas kernels  23.6 us (31%)
  waiting for transfers between devices  8.04 us (10%)
    ppermute x15, starting transfers between devices, along(): return lax.ppermute(value, 'loop', axis_shift(axis, step))  27.4 us
    pallas_call x2, Pallas kernels, products(): pl.pallas_call(functools.partial(product_kernel, steps, last), out_shape=...  13.7 us
    ppermute x9, starting transfers between devices, across_heads(): return lax.ppermute(value, 'head', [(i, i ^ mask) for i in range(N)])  11.8 us
    pallas_call x1, Pallas kernels, scaled_heads(): pl.pallas_call(scale_kernel, out_shape=pltpu.VMEM((HEADS, SEQS * HEAD_DIM...  6.48 us
    ppermute x15, waiting for transfers between devices, along(): return lax.ppermute(value, 'loop', axis_shift(axis, step))  4.7 us
    ppermute x1, starting transfers between devices, swapped(): return lax.ppermute(value, ('loop', 'head'), swap_shift(step))  4.59 us
    pallas_call x1, Pallas kernels, inverses(): pl.pallas_call(inverse_kernel, out_shape=pltpu.VMEM((HEADS, HEAD_DIM, FEA...  2.19 us
    ppermute x1, waiting for transfers between devices, swapped(): return lax.ppermute(value, ('loop', 'head'), swap_shift(step))  1.76 us
  transfers between devices with their start and end apart: 25, of which 5 were waited for; matrix products, arithmetic and copies ran while one was open for 0% of the time, Pallas kernels for 20%

profile of v3, /device:TPU:1, one launch (start us, length us, event | category | flops | bytes accessed | tf_op | source)
XLA Modules:
  0.0 76.4 jit_solution(9499945506274000294)
XLA Ops:
  0.0 1.2 %shard_map.73 = (bf16[3,8,8,128]{3,2,1,0:T(8,128)(2,1)S(1)}, bf16[1,8,8,128]{3,2,1,0:T(8,128)(2,1)S(1)}, bf16[2,8,8,128]{3,2,1,0:T(8,128)(2,1)S(1)}) custom-call(bf16[1,8,8,128]{3,2,1,0:T(8,128)(2,1)} %query.1, bf16[1,8,1024]{2,1,0:T(8,128)(2,1)} %right.1, bf16[2,8,8,128]{3,2,1,0:T(8,128)(2,1)} %train.1, bf16[2,8,1024]{2,1,0:T(8,128)(2,1)} %train_right.1, ...), custom_call_target="tpu_custom_call" | custom-call | tf_op jit(solution)/shard_map/pallas_call | solution.py:81
  1.2 4.6 %collective-permute-start = (bf16[3,8,8,128]{3,2,1,0:T(8,128)(2,1)S(1)}, bf16[3,8,8,128]{3,2,1,0:T(8,128)(2,1)S(1)}, u32[]{:S(2)}, u32[]{:S(2)}) collective-permute-start(bf16[3,8,8,128]{3,2,1,0:T(8,128)(2,1)S(1)} %get-tuple-element.25), channel_id=1, source_target_pairs={{0,0},{1,4},{2,8},{3,12},{4,1},{5,5},{6,9},{7,13},{8,2},{9,6},{10,... | collective-permute-start | bytes 147464 | tf_op jit(solution)/shard_map/ppermute | solution.py:55
  5.8 1.8 %collective-permute-done = bf16[3,8,8,128]{3,2,1,0:T(8,128)(2,1)S(1)} collective-permute-done((bf16[3,8,8,128]{3,2,1,0:T(8,128)(2,1)S(1)}, bf16[3,8,8,128]{3,2,1,0:T(8,128)(2,1)S(1)}, u32[]{:S(2)}, u32[]{:S(2)}) %collective-permute-start) | collective-permute-done | bytes 49184 | tf_op jit(solution)/shard_map/ppermute | solution.py:55
  7.6 3.4 %collective-permute-start.1 = (bf16[1,16,8,128]{3,2,1,0:T(8,128)(2,1)S(1)}, bf16[1,16,8,128]{3,2,1,0:T(8,128)(2,1)S(1)}, u32[]{:S(2)}, u32[]{:S(2)}) collective-permute-start(bf16[1,16,8,128]{3,2,1,0:T(8,128)(2,1)S(1)} %pad_maximum_fusion.1), channel_id=1, source_target_pairs={{0,64},{4,68},{8,72},{12,76},{16,80},{20,84},{24,88},{28,92},{32,9... | collective-permute-start | bytes 98312 | tf_op jit(solution)/shard_map/ppermute | solution.py:51
  10.9 5.1 %collective-permute-start.2 = (bf16[1,16,8,128]{3,2,1,0:T(8,128)(2,1)S(1)}, bf16[1,16,8,128]{3,2,1,0:T(8,128)(2,1)S(1)}, u32[]{:S(2)}, u32[]{:S(2)}) collective-permute-start(bf16[1,16,8,128]{3,2,1,0:T(8,128)(2,1)S(1)} %pad_maximum_fusion.1), channel_id=1, source_target_pairs={{0,128},{4,132},{8,136},{12,140},{16,144},{20,148},{24,152},{28,15... | collective-permute-start | bytes 98312 | tf_op jit(solution)/shard_map/ppermute | solution.py:51
  16.0 2.1 %collective-permute-start.3 = (bf16[1,16,8,128]{3,2,1,0:T(8,128)(2,1)S(1)}, bf16[1,16,8,128]{3,2,1,0:T(8,128)(2,1)S(1)}, u32[]{:S(2)}, u32[]{:S(2)}) collective-permute-start(bf16[1,16,8,128]{3,2,1,0:T(8,128)(2,1)S(1)} %pad_maximum_fusion.1), channel_id=1, source_target_pairs={{0,192},{4,196},{8,200},{12,204},{16,208},{20,212},{24,216},{28,22... | collective-permute-start | bytes 98312 | tf_op jit(solution)/shard_map/ppermute | solution.py:51
  18.1 6.3 %collective-permute-start.8 = (bf16[2,8,8,128]{3,2,1,0:T(8,128)(2,1)S(1)}, bf16[2,8,8,128]{3,2,1,0:T(8,128)(2,1)S(1)}, u32[]{:S(2)}, u32[]{:S(2)}) collective-permute-start(bf16[2,8,8,128]{3,2,1,0:T(8,128)(2,1)S(1)} %get-tuple-element.36.refs_4_), channel_id=1, source_target_pairs={{0,8},{4,12},{8,0},{12,4},{16,24},{20,28},{24,16},{28,20},{32,40},... | collective-permute-start | bytes 98312 | tf_op jit(solution)/shard_map/ppermute | solution.py:51
  24.8 1.3 %collective-permute-start.4 = (bf16[4,16,8,128]{3,2,1,0:T(8,128)(2,1)S(1)}, bf16[4,16,8,128]{3,2,1,0:T(8,128)(2,1)S(1)}, u32[]{:S(2)}, u32[]{:S(2)}) collective-permute-start(bf16[4,16,8,128]{3,2,1,0:T(8,128)(2,1)S(1)} %pad_maximum_fusion), channel_id=1, source_target_pairs={{0,16},{4,20},{8,24},{12,28},{16,32},{20,36},{24,40},{28,44},{32,4... | collective-permute-start | bytes 393224 | tf_op jit(solution)/shard_map/ppermute | solution.py:51
  26.0 2.5 %collective-permute-start.5 = (bf16[4,16,8,128]{3,2,1,0:T(8,128)(2,1)S(1)}, bf16[4,16,8,128]{3,2,1,0:T(8,128)(2,1)S(1)}, u32[]{:S(2)}, u32[]{:S(2)}) collective-permute-start(bf16[4,16,8,128]{3,2,1,0:T(8,128)(2,1)S(1)} %pad_maximum_fusion), channel_id=1, source_target_pairs={{0,32},{4,36},{8,40},{12,44},{16,48},{20,52},{24,56},{28,60},{32,0... | collective-permute-start | bytes 393224 | tf_op jit(solution)/shard_map/ppermute | solution.py:51
  28.5 1.2 %collective-permute-start.6 = (bf16[4,16,8,128]{3,2,1,0:T(8,128)(2,1)S(1)}, bf16[4,16,8,128]{3,2,1,0:T(8,128)(2,1)S(1)}, u32[]{:S(2)}, u32[]{:S(2)}) collective-permute-start(bf16[4,16,8,128]{3,2,1,0:T(8,128)(2,1)S(1)} %pad_maximum_fusion), channel_id=1, source_target_pairs={{0,48},{4,52},{8,56},{12,60},{16,0},{20,4},{24,8},{28,12},{32,16},... | collective-permute-start | bytes 393224 | tf_op jit(solution)/shard_map/ppermute | solution.py:51
  29.7 4.5 %collective-permute-start.10 = (bf16[2,8,8,128]{3,2,1,0:T(8,128)(2,1)S(1)}, bf16[2,8,8,128]{3,2,1,0:T(8,128)(2,1)S(1)}, u32[]{:S(2)}, u32[]{:S(2)}) collective-permute-start(bf16[2,8,8,128]{3,2,1,0:T(8,128)(2,1)S(1)} %slice.51.refs_0_), channel_id=1, source_target_pairs={{0,1},{1,0},{2,3},{3,2},{4,5},{5,4},{6,7},{7,6},{8,9},{9,8},{10,11... | collective-permute-start | bytes 98312 | tf_op jit(solution)/shard_map/ppermute | solution.py:59
  34.3 2.2 %shard_map.74.refs_8_ = f32[8,128,1024]{2,1,0:T(8,128)S(1)} custom-call(s32[4]{0:T(128)S(1)} %pad_add_fusion.place, bf16[32,128,1024]{2,1,0:T(8,128)(2,1)} %eigen.1), custom_call_target="tpu_custom_call" | custom-call | flops 2097152 | bytes 6291456 | tf_op jit(solution)/shard_map/pallas_call | solution.py:103
  36.7 1.8 %collective-permute-start.13 = (bf16[16,8,8,128]{3,2,1,0:T(8,128)(2,1)S(1)}, bf16[16,8,8,128]{3,2,1,0:T(8,128)(2,1)S(1)}, u32[]{:S(2)}, u32[]{:S(2)}) collective-permute-start(bf16[16,8,8,128]{3,2,1,0:T(8,128)(2,1)S(1)} %get-tuple-element.41.refs_0_), channel_id=1, source_target_pairs={{0,2},{1,3},{2,0},{3,1},{4,6},{5,7},{6,4},{7,5},{8,10},{9,11},{10,... | collective-permute-start | bytes 786440 | tf_op jit(solution)/shard_map/ppermute | solution.py:59
  38.5 6.5 %shard_map.75.refs_6_ = bf16[8,1024,1024]{2,1,0:T(8,128)(2,1)S(1)} custom-call(s32[4]{0:T(128)S(1)} %pad_add_fusion.place, bf16[2,8,8,128]{3,2,1,0:T(8,128)(2,1)S(1)} %slice.51.refs_0_, bf16[2,8,8,128]{3,2,1,0:T(8,128)(2,1)S(1)} %collective-permute-done.10.refs_1_, bf16[2,8,8,128]{3,2,1,0:T(8,128)(2,1)S(1)} %collective-permute-done.11.refs_2_, ...), custom_call_target="tpu_custom_call" | custom-call | flops 4294967296 | bytes 1048576 | tf_op jit(solution)/shard_map/pallas_call | solution.py:141
  45.0 1.4 %collective-permute-done.14.refs_5_ = bf16[16,8,8,128]{3,2,1,0:T(8,128)(2,1)S(1)} collective-permute-done((bf16[16,8,8,128]{3,2,1,0:T(8,128)(2,1)S(1)}, bf16[16,8,8,128]{3,2,1,0:T(8,128)(2,1)S(1)}, u32[]{:S(2)}, u32[]{:S(2)}) %collective-permute-start.14) | collective-permute-done | bytes 262176 | tf_op jit(solution)/shard_map/ppermute | solution.py:51
  46.4 2.3 %collective-permute-start.15 = (bf16[16,8,8,128]{3,2,1,0:T(8,128)(2,1)S(1)}, bf16[16,8,8,128]{3,2,1,0:T(8,128)(2,1)S(1)}, u32[]{:S(2)}, u32[]{:S(2)}) collective-permute-start(bf16[16,8,8,128]{3,2,1,0:T(8,128)(2,1)S(1)} %get-tuple-element.41.refs_0_), channel_id=1, source_target_pairs={{0,1},{1,0},{2,3},{3,2},{4,5},{5,4},{6,7},{7,6},{8,9},{9,8},{10,11... | collective-permute-start | bytes 786440 | tf_op jit(solution)/shard_map/ppermute | solution.py:59
  48.8 2.7 %collective-permute-start.18 = (bf16[16,8,8,128]{3,2,1,0:T(8,128)(2,1)S(1)}, bf16[16,8,8,128]{3,2,1,0:T(8,128)(2,1)S(1)}, u32[]{:S(2)}, u32[]{:S(2)}) collective-permute-start(bf16[16,8,8,128]{3,2,1,0:T(8,128)(2,1)S(1)} %get-tuple-element.45.refs_4_), channel_id=1, source_target_pairs={{0,12},{4,0},{8,4},{12,8},{16,28},{20,16},{24,20},{28,24},{32,44},... | collective-permute-start | bytes 786440 | tf_op jit(solution)/shard_map/ppermute | solution.py:51
  51.4 6.6 %shard_map.76.refs_7_ = f32[8,256]{1,0:T(8,128)S(1)} custom-call(s32[4]{0:T(128)S(1)} %pad_add_fusion.place, bf16[16,8,8,128]{3,2,1,0:T(8,128)(2,1)S(1)} %get-tuple-element.41.refs_0_, bf16[16,8,8,128]{3,2,1,0:T(8,128)(2,1)S(1)} %collective-permute-done.15.refs_1_, bf16[16,8,8,128]{3,2,1,0:T(8,128)(2,1)S(1)} %collective-permute-done.13.refs_2_, ...), custom_call_target="tpu_custom_call" | custom-call | flops 1048576 | bytes 4096 | tf_op jit(solution)/shard_map/pallas_call | solution.py:212
  58.1 7.1 %shard_map.77 = f32[4,8,16]{2,1,0:T(8,128)S(1)} custom-call(s32[4]{0:T(128)S(1)} %pad_add_fusion.place, bf16[16,8,8,128]{3,2,1,0:T(8,128)(2,1)S(1)} %get-tuple-element.41.refs_0_, bf16[16,8,8,128]{3,2,1,0:T(8,128)(2,1)S(1)} %collective-permute-done.15.refs_1_, bf16[16,8,8,128]{3,2,1,0:T(8,128)(2,1)S(1)} %collective-permute-done.13.refs_2_, ...), custom_call_target="tpu_custom_call" | custom-call | flops 1048576 | bytes 4096 | tf_op jit(solution)/shard_map/pallas_call | solution.py:212
  65.2 1.1 %collective-permute-start.19 = (f32[8,16]{1,0:T(8,128)S(1)}, f32[8,16]{1,0:T(8,128)S(1)}, u32[]{:S(2)}, u32[]{:S(2)}) collective-permute-start(f32[8,16]{1,0:T(8,128)S(1)} %get-tuple-element.47), channel_id=1, source_target_pairs={{0,1},{1,0},{2,3},{3,2},{4,5},{5,4},{6,7},{7,6},{8,9},{9,8},{10,11... | collective-permute-start | bytes 1544 | tf_op jit(solution)/shard_map/ppermute | solution.py:59
  66.4 1.6 %collective-permute-start.21 = (f32[8,16]{1,0:T(8,128)S(1)}, f32[8,16]{1,0:T(8,128)S(1)}, u32[]{:S(2)}, u32[]{:S(2)}) collective-permute-start(f32[8,16]{1,0:T(8,128)S(1)} %get-tuple-element.48), channel_id=1, source_target_pairs={{0,3},{1,2},{2,1},{3,0},{4,7},{5,6},{6,5},{7,4},{8,11},{9,10},{10,... | collective-permute-start | bytes 1544 | tf_op jit(solution)/shard_map/ppermute | solution.py:59
  68.8 0.8 %collective-permute-done.21 = f32[8,16]{1,0:T(8,128)S(1)} collective-permute-done((f32[8,16]{1,0:T(8,128)S(1)}, f32[8,16]{1,0:T(8,128)S(1)}, u32[]{:S(2)}, u32[]{:S(2)}) %collective-permute-start.21) | collective-permute-done | bytes 544 | tf_op jit(solution)/shard_map/ppermute | solution.py:59
  69.6 2.3 %collective-permute-start.22 = (f32[2,16]{1,0:T(2,128)S(1)}, f32[2,16]{1,0:T(2,128)S(1)}, u32[]{:S(2)}, u32[]{:S(2)}) collective-permute-start(f32[2,16]{1,0:T(2,128)S(1)} %get-tuple-element.50), channel_id=1, source_target_pairs={{0,12},{4,0},{8,4},{12,8},{16,28},{20,16},{24,20},{28,24},{32,44},... | collective-permute-start | bytes 392 | tf_op jit(solution)/shard_map/ppermute | solution.py:51
  72.6 3.2 %collective-permute-done.23 = f32[2,16]{1,0:T(2,128)S(1)} collective-permute-done((f32[2,16]{1,0:T(2,128)S(1)}, f32[2,16]{1,0:T(2,128)S(1)}, u32[]{:S(2)}, u32[]{:S(2)}) %collective-permute-start.23) | collective-permute-done | bytes 160 | tf_op jit(solution)/shard_map/ppermute | solution.py:51
  (48 shorter events, 2.9 us)
Async XLA Ops:
  1.2 6.4 %collective-permute-start = (bf16[3,8,8,128]{3,2,1,0:T(8,128)(2,1)S(1)}, bf16[3,8,8,128]{3,2,1,0:T(8,128)(2,1)S(1)}, u32[]{:S(2)}, u32[]{:S(2)}) collective-permute-start(bf16[3,8,8,128]{3,2,1,0:T(8,128)(2,1)S(1)} %get-tuple-element.25), channel_id=1, source_target_pairs={{0,0},{1,4},{2,8},{3,12},{4,1},{5,5},{6,9},{7,13},{8,2},{9,6},{10,... | collective-permute-start | bytes 147464 | tf_op jit(solution)/shard_map/ppermute | solution.py:55
  7.6 16.9 %collective-permute-start.1 = (bf16[1,16,8,128]{3,2,1,0:T(8,128)(2,1)S(1)}, bf16[1,16,8,128]{3,2,1,0:T(8,128)(2,1)S(1)}, u32[]{:S(2)}, u32[]{:S(2)}) collective-permute-start(bf16[1,16,8,128]{3,2,1,0:T(8,128)(2,1)S(1)} %pad_maximum_fusion.1), channel_id=1, source_target_pairs={{0,64},{4,68},{8,72},{12,76},{16,80},{20,84},{24,88},{28,92},{32,9... | collective-permute-start | bytes 98312 | tf_op jit(solution)/shard_map/ppermute | solution.py:51
  10.9 13.5 %collective-permute-start.2 = (bf16[1,16,8,128]{3,2,1,0:T(8,128)(2,1)S(1)}, bf16[1,16,8,128]{3,2,1,0:T(8,128)(2,1)S(1)}, u32[]{:S(2)}, u32[]{:S(2)}) collective-permute-start(bf16[1,16,8,128]{3,2,1,0:T(8,128)(2,1)S(1)} %pad_maximum_fusion.1), channel_id=1, source_target_pairs={{0,128},{4,132},{8,136},{12,140},{16,144},{20,148},{24,152},{28,15... | collective-permute-start | bytes 98312 | tf_op jit(solution)/shard_map/ppermute | solution.py:51
  16.0 8.7 %collective-permute-start.3 = (bf16[1,16,8,128]{3,2,1,0:T(8,128)(2,1)S(1)}, bf16[1,16,8,128]{3,2,1,0:T(8,128)(2,1)S(1)}, u32[]{:S(2)}, u32[]{:S(2)}) collective-permute-start(bf16[1,16,8,128]{3,2,1,0:T(8,128)(2,1)S(1)} %pad_maximum_fusion.1), channel_id=1, source_target_pairs={{0,192},{4,196},{8,200},{12,204},{16,208},{20,212},{24,216},{28,22... | collective-permute-start | bytes 98312 | tf_op jit(solution)/shard_map/ppermute | solution.py:51
  18.1 7.9 %collective-permute-start.7 = (bf16[2,8,8,128]{3,2,1,0:T(8,128)(2,1)S(1)}, bf16[2,8,8,128]{3,2,1,0:T(8,128)(2,1)S(1)}, u32[]{:S(2)}, u32[]{:S(2)}) collective-permute-start(bf16[2,8,8,128]{3,2,1,0:T(8,128)(2,1)S(1)} %get-tuple-element.36.refs_4_), channel_id=1, source_target_pairs={{0,4},{4,8},{8,12},{12,0},{16,20},{20,24},{24,28},{28,16},{32,36},... | collective-permute-start | bytes 98312 | tf_op jit(solution)/shard_map/ppermute | solution.py:51
  18.1 10.4 %collective-permute-start.8 = (bf16[2,8,8,128]{3,2,1,0:T(8,128)(2,1)S(1)}, bf16[2,8,8,128]{3,2,1,0:T(8,128)(2,1)S(1)}, u32[]{:S(2)}, u32[]{:S(2)}) collective-permute-start(bf16[2,8,8,128]{3,2,1,0:T(8,128)(2,1)S(1)} %get-tuple-element.36.refs_4_), channel_id=1, source_target_pairs={{0,8},{4,12},{8,0},{12,4},{16,24},{20,28},{24,16},{28,20},{32,40},... | collective-permute-start | bytes 98312 | tf_op jit(solution)/shard_map/ppermute | solution.py:51
  24.4 5.2 %collective-permute-start.9 = (bf16[2,8,8,128]{3,2,1,0:T(8,128)(2,1)S(1)}, bf16[2,8,8,128]{3,2,1,0:T(8,128)(2,1)S(1)}, u32[]{:S(2)}, u32[]{:S(2)}) collective-permute-start(bf16[2,8,8,128]{3,2,1,0:T(8,128)(2,1)S(1)} %get-tuple-element.36.refs_4_), channel_id=1, source_target_pairs={{0,12},{4,0},{8,4},{12,8},{16,28},{20,16},{24,20},{28,24},{32,44},... | collective-permute-start | bytes 98312 | tf_op jit(solution)/shard_map/ppermute | solution.py:51
  24.4 9.7 %collective-permute-start.11 = (bf16[2,8,8,128]{3,2,1,0:T(8,128)(2,1)S(1)}, bf16[2,8,8,128]{3,2,1,0:T(8,128)(2,1)S(1)}, u32[]{:S(2)}, u32[]{:S(2)}) collective-permute-start(bf16[2,8,8,128]{3,2,1,0:T(8,128)(2,1)S(1)} %slice.51.refs_0_), channel_id=1, source_target_pairs={{0,2},{1,3},{2,0},{3,1},{4,6},{5,7},{6,4},{7,5},{8,10},{9,11},{10,... | collective-permute-start | bytes 98312 | tf_op jit(solution)/shard_map/ppermute | solution.py:59
  24.8 11.8 %collective-permute-start.4 = (bf16[4,16,8,128]{3,2,1,0:T(8,128)(2,1)S(1)}, bf16[4,16,8,128]{3,2,1,0:T(8,128)(2,1)S(1)}, u32[]{:S(2)}, u32[]{:S(2)}) collective-permute-start(bf16[4,16,8,128]{3,2,1,0:T(8,128)(2,1)S(1)} %pad_maximum_fusion), channel_id=1, source_target_pairs={{0,16},{4,20},{8,24},{12,28},{16,32},{20,36},{24,40},{28,44},{32,4... | collective-permute-start | bytes 393224 | tf_op jit(solution)/shard_map/ppermute | solution.py:51
  26.0 10.5 %collective-permute-start.5 = (bf16[4,16,8,128]{3,2,1,0:T(8,128)(2,1)S(1)}, bf16[4,16,8,128]{3,2,1,0:T(8,128)(2,1)S(1)}, u32[]{:S(2)}, u32[]{:S(2)}) collective-permute-start(bf16[4,16,8,128]{3,2,1,0:T(8,128)(2,1)S(1)} %pad_maximum_fusion), channel_id=1, source_target_pairs={{0,32},{4,36},{8,40},{12,44},{16,48},{20,52},{24,56},{28,60},{32,0... | collective-permute-start | bytes 393224 | tf_op jit(solution)/shard_map/ppermute | solution.py:51
  28.5 8.0 %collective-permute-start.6 = (bf16[4,16,8,128]{3,2,1,0:T(8,128)(2,1)S(1)}, bf16[4,16,8,128]{3,2,1,0:T(8,128)(2,1)S(1)}, u32[]{:S(2)}, u32[]{:S(2)}) collective-permute-start(bf16[4,16,8,128]{3,2,1,0:T(8,128)(2,1)S(1)} %pad_maximum_fusion), channel_id=1, source_target_pairs={{0,48},{4,52},{8,56},{12,60},{16,0},{20,4},{24,8},{28,12},{32,16},... | collective-permute-start | bytes 393224 | tf_op jit(solution)/shard_map/ppermute | solution.py:51
  29.7 6.8 %collective-permute-start.10 = (bf16[2,8,8,128]{3,2,1,0:T(8,128)(2,1)S(1)}, bf16[2,8,8,128]{3,2,1,0:T(8,128)(2,1)S(1)}, u32[]{:S(2)}, u32[]{:S(2)}) collective-permute-start(bf16[2,8,8,128]{3,2,1,0:T(8,128)(2,1)S(1)} %slice.51.refs_0_), channel_id=1, source_target_pairs={{0,1},{1,0},{2,3},{3,2},{4,5},{5,4},{6,7},{7,6},{8,9},{9,8},{10,11... | collective-permute-start | bytes 98312 | tf_op jit(solution)/shard_map/ppermute | solution.py:59
  36.7 8.3 %collective-permute-start.13 = (bf16[16,8,8,128]{3,2,1,0:T(8,128)(2,1)S(1)}, bf16[16,8,8,128]{3,2,1,0:T(8,128)(2,1)S(1)}, u32[]{:S(2)}, u32[]{:S(2)}) collective-permute-start(bf16[16,8,8,128]{3,2,1,0:T(8,128)(2,1)S(1)} %get-tuple-element.41.refs_0_), channel_id=1, source_target_pairs={{0,2},{1,3},{2,0},{3,1},{4,6},{5,7},{6,4},{7,5},{8,10},{9,11},{10,... | collective-permute-start | bytes 786440 | tf_op jit(solution)/shard_map/ppermute | solution.py:59
  38.5 7.9 %collective-permute-start.14 = (bf16[16,8,8,128]{3,2,1,0:T(8,128)(2,1)S(1)}, bf16[16,8,8,128]{3,2,1,0:T(8,128)(2,1)S(1)}, u32[]{:S(2)}, u32[]{:S(2)}) collective-permute-start(bf16[16,8,8,128]{3,2,1,0:T(8,128)(2,1)S(1)} %get-tuple-element.45.refs_4_), channel_id=1, source_target_pairs={{0,8},{4,12},{8,0},{12,4},{16,24},{20,28},{24,16},{28,20},{32,40},... | collective-permute-start | bytes 786440 | tf_op jit(solution)/shard_map/ppermute | solution.py:51
  46.4 5.0 %collective-permute-start.15 = (bf16[16,8,8,128]{3,2,1,0:T(8,128)(2,1)S(1)}, bf16[16,8,8,128]{3,2,1,0:T(8,128)(2,1)S(1)}, u32[]{:S(2)}, u32[]{:S(2)}) collective-permute-start(bf16[16,8,8,128]{3,2,1,0:T(8,128)(2,1)S(1)} %get-tuple-element.41.refs_0_), channel_id=1, source_target_pairs={{0,1},{1,0},{2,3},{3,2},{4,5},{5,4},{6,7},{7,6},{8,9},{9,8},{10,11... | collective-permute-start | bytes 786440 | tf_op jit(solution)/shard_map/ppermute | solution.py:59
  48.7 2.7 %collective-permute-start.16 = (bf16[16,8,8,128]{3,2,1,0:T(8,128)(2,1)S(1)}, bf16[16,8,8,128]{3,2,1,0:T(8,128)(2,1)S(1)}, u32[]{:S(2)}, u32[]{:S(2)}) collective-permute-start(bf16[16,8,8,128]{3,2,1,0:T(8,128)(2,1)S(1)} %collective-permute-done.13.refs_2_), channel_id=1, source_target_pairs={{0,1},{1,0},{2,3},{3,2},{4,5},{5,4},{6,7},{7,6},{8,9},{9,8},{10,11... | collective-permute-start | bytes 786440 | tf_op jit(solution)/shard_map/ppermute | solution.py:59
  48.8 9.3 %collective-permute-start.17 = (bf16[16,8,8,128]{3,2,1,0:T(8,128)(2,1)S(1)}, bf16[16,8,8,128]{3,2,1,0:T(8,128)(2,1)S(1)}, u32[]{:S(2)}, u32[]{:S(2)}) collective-permute-start(bf16[16,8,8,128]{3,2,1,0:T(8,128)(2,1)S(1)} %get-tuple-element.45.refs_4_), channel_id=1, source_target_pairs={{0,4},{4,8},{8,12},{12,0},{16,20},{20,24},{24,28},{28,16},{32,36},... | collective-permute-start | bytes 786440 | tf_op jit(solution)/shard_map/ppermute | solution.py:51
  48.8 9.3 %collective-permute-start.18 = (bf16[16,8,8,128]{3,2,1,0:T(8,128)(2,1)S(1)}, bf16[16,8,8,128]{3,2,1,0:T(8,128)(2,1)S(1)}, u32[]{:S(2)}, u32[]{:S(2)}) collective-permute-start(bf16[16,8,8,128]{3,2,1,0:T(8,128)(2,1)S(1)} %get-tuple-element.45.refs_4_), channel_id=1, source_target_pairs={{0,12},{4,0},{8,4},{12,8},{16,28},{20,16},{24,20},{28,24},{32,44},... | collective-permute-start | bytes 786440 | tf_op jit(solution)/shard_map/ppermute | solution.py:51
  65.2 2.8 %collective-permute-start.19 = (f32[8,16]{1,0:T(8,128)S(1)}, f32[8,16]{1,0:T(8,128)S(1)}, u32[]{:S(2)}, u32[]{:S(2)}) collective-permute-start(f32[8,16]{1,0:T(8,128)S(1)} %get-tuple-element.47), channel_id=1, source_target_pairs={{0,1},{1,0},{2,3},{3,2},{4,5},{5,4},{6,7},{7,6},{8,9},{9,8},{10,11... | collective-permute-start | bytes 1544 | tf_op jit(solution)/shard_map/ppermute | solution.py:59
  66.3 2.5 %collective-permute-start.20 = (f32[8,16]{1,0:T(8,128)S(1)}, f32[8,16]{1,0:T(8,128)S(1)}, u32[]{:S(2)}, u32[]{:S(2)}) collective-permute-start(f32[8,16]{1,0:T(8,128)S(1)} %get-tuple-element.49), channel_id=1, source_target_pairs={{0,2},{1,3},{2,0},{3,1},{4,6},{5,7},{6,4},{7,5},{8,10},{9,11},{10,... | collective-permute-start | bytes 1544 | tf_op jit(solution)/shard_map/ppermute | solution.py:59
  66.4 3.2 %collective-permute-start.21 = (f32[8,16]{1,0:T(8,128)S(1)}, f32[8,16]{1,0:T(8,128)S(1)}, u32[]{:S(2)}, u32[]{:S(2)}) collective-permute-start(f32[8,16]{1,0:T(8,128)S(1)} %get-tuple-element.48), channel_id=1, source_target_pairs={{0,3},{1,2},{2,1},{3,0},{4,7},{5,6},{6,5},{7,4},{8,11},{9,10},{10,... | collective-permute-start | bytes 1544 | tf_op jit(solution)/shard_map/ppermute | solution.py:59
  69.6 3.0 %collective-permute-start.22 = (f32[2,16]{1,0:T(2,128)S(1)}, f32[2,16]{1,0:T(2,128)S(1)}, u32[]{:S(2)}, u32[]{:S(2)}) collective-permute-start(f32[2,16]{1,0:T(2,128)S(1)} %get-tuple-element.50), channel_id=1, source_target_pairs={{0,12},{4,0},{8,4},{12,8},{16,28},{20,16},{24,20},{28,24},{32,44},... | collective-permute-start | bytes 392 | tf_op jit(solution)/shard_map/ppermute | solution.py:51
  71.9 3.9 %collective-permute-start.23 = (f32[2,16]{1,0:T(2,128)S(1)}, f32[2,16]{1,0:T(2,128)S(1)}, u32[]{:S(2)}, u32[]{:S(2)}) collective-permute-start(f32[2,16]{1,0:T(2,128)S(1)} %get-tuple-element.52), channel_id=1, source_target_pairs={{0,8},{4,12},{8,0},{12,4},{16,24},{20,28},{24,16},{28,20},{32,40},... | collective-permute-start | bytes 392 | tf_op jit(solution)/shard_map/ppermute | solution.py:51
  71.9 3.9 %collective-permute-start.24 = (f32[2,16]{1,0:T(2,128)S(1)}, f32[2,16]{1,0:T(2,128)S(1)}, u32[]{:S(2)}, u32[]{:S(2)}) collective-permute-start(f32[2,16]{1,0:T(2,128)S(1)} %get-tuple-element.51), channel_id=1, source_target_pairs={{0,4},{4,8},{8,12},{12,0},{16,20},{20,24},{24,28},{28,16},{32,36},... | collective-permute-start | bytes 392 | tf_op jit(solution)/shard_map/ppermute | solution.py:51
  (2 other events, 12.3 us)

commit v4 on v3

--- a/solution.py
+++ b/solution.py
@@ -18,6 +18,7 @@
 
 N = 4
 HEADS = 8
+AT_ONCE = 4
 SEQS = 8
 FEATURES = 1024
 COLUMNS = QUERIES * GRAD_RANK
@@ -60,7 +61,6 @@
 
 
 VMEM = pl.BlockSpec(memory_space=pltpu.VMEM)
-SMEM = pl.BlockSpec(memory_space=pltpu.SMEM)
 TILES = FEATURES // 128
 
 
@@ -88,10 +88,14 @@
     )(query_left, query_right, train_left, train_right, basis)
 
 
-def inverse_kernel(place, eigen, inverse, fetched, sems):
-    fetches = [
-        pltpu.make_async_copy(eigen.at[HEADS * place[2] + h], fetched.at[h], sems.at[h]) for h in range(HEADS)
-    ]
+def place():
+    loop = lax.axis_index("loop")
+    return loop // 16, loop // 4 % 4, loop % 4, lax.axis_index("head")
+
+
+def inverse_kernel(eigen, inverse, fetched, sems):
+    _, _, y, _ = place()
+    fetches = [pltpu.make_async_copy(eigen.at[HEADS * y + h], fetched.at[h], sems.at[h]) for h in range(HEADS)]
     for fetch in fetches:
         fetch.start()
     for h, fetch in enumerate(fetches):
@@ -99,11 +103,11 @@
         inverse[h] = 1.0 / (fetched[h].astype(jnp.float32) + DAMPING)
 
 
-def inverses(place, eigen):
+def inverses(eigen):
     return pl.pallas_call(
         inverse_kernel,
         out_shape=pltpu.VMEM((HEADS, HEAD_DIM, FEATURES), jnp.float32),
-        in_specs=[SMEM, pl.BlockSpec(memory_space=pltpu.HBM)],
+        in_specs=[pl.BlockSpec(memory_space=pltpu.HBM)],
         out_specs=VMEM,
         scratch_shapes=[
             pltpu.VMEM((HEADS, HEAD_DIM, FEATURES), jnp.bfloat16),
@@ -111,48 +115,51 @@
         ],
         compiler_params=pltpu.CompilerParams(vmem_limit_bytes=16 * 2**20),
         cost_estimate=pl.CostEstimate(flops=2**21, bytes_accessed=6 * 2**20, transcendentals=2**20),
-    )(place, pltpu.with_memory_space_constraint(eigen, pltpu.HBM))
-
-
-def scale_kernel(place, *refs):
+    )(pltpu.with_memory_space_constraint(eigen, pltpu.HBM))
+
+
+def scale_kernel(*refs):
     tl = refs[0:4]
     tr = refs[4:8]
     inverse, scaled, tl_all, tr_all = refs[8:]
-    y, g = place[2], place[3]
+    _, _, y, g = place()
     for m in range(N):
         tl_all[lax.rem(y - (g ^ m) + N, N)] = tl[m][...]
     for k in range(N):
         for j in range(TILES):
             tr_all[16 * k : 16 * (k + 1), 128 * j : 128 * (j + 1)] = tr[k][:, j].reshape(16, 128)
 
-    @pl.loop(0, HEADS)
+    @pl.loop(0, HEADS, step=AT_ONCE)
     def _(head):
-        left = tl_all[:, :, head].reshape(SEQS * GRAD_RANK, HEAD_DIM)
-        left = jnp.concatenate([left] * SEQS, axis=1)
-        own = lax.broadcasted_iota(jnp.int32, left.shape, 0) // GRAD_RANK
-        own = own == lax.broadcasted_iota(jnp.int32, left.shape, 1) // HEAD_DIM
-        left = jnp.where(own, left, jnp.zeros_like(left))
+        lefts = []
+        for h in range(AT_ONCE):
+            left = tl_all[:, :, head + h].reshape(SEQS * GRAD_RANK, HEAD_DIM)
+            left = jnp.concatenate([left] * SEQS, axis=1)
+            own = lax.broadcasted_iota(jnp.int32, left.shape, 0) // GRAD_RANK
+            own = own == lax.broadcasted_iota(jnp.int32, left.shape, 1) // HEAD_DIM
+            lefts.append(jnp.where(own, left, jnp.zeros_like(left)))
+        left = jnp.concatenate(lefts, axis=1)
         dense = lax.dot_general(left, tr_all[...], (((0,), (0,)), ((), ())), preferred_element_type=jnp.float32)
-        dense = dense.reshape(SEQS, HEAD_DIM, FEATURES) * inverse[head][None]
-        scaled[head] = dense.astype(jnp.bfloat16).reshape(SEQS * HEAD_DIM, FEATURES)
-
-
-def scaled_heads(place, tl, tr, inverse):
+        dense = dense.reshape(AT_ONCE, SEQS, HEAD_DIM, FEATURES) * inverse[pl.ds(head, AT_ONCE)][:, None]
+        scaled[pl.ds(head, AT_ONCE)] = dense.astype(jnp.bfloat16).reshape(AT_ONCE, SEQS * HEAD_DIM, FEATURES)
+
+
+def scaled_heads(tl, tr, inverse):
     return pl.pallas_call(
         scale_kernel,
         out_shape=pltpu.VMEM((HEADS, SEQS * HEAD_DIM, FEATURES), jnp.bfloat16),
-        in_specs=[SMEM] + [VMEM] * 9,
+        in_specs=[VMEM] * 9,
         out_specs=VMEM,
         scratch_shapes=[
             pltpu.VMEM((N, 2, HEADS, GRAD_RANK, HEAD_DIM), jnp.bfloat16),
             pltpu.VMEM((SEQS * GRAD_RANK, FEATURES), jnp.bfloat16),
         ],
-        compiler_params=pltpu.CompilerParams(vmem_limit_bytes=16 * 2**20),
+        compiler_params=pltpu.CompilerParams(vmem_limit_bytes=30 * 2**20),
         cost_estimate=pl.CostEstimate(flops=2**32, bytes_accessed=2**20, transcendentals=0),
-    )(place, *tl, *tr, inverse)
-
-
-def product_kernel(steps, last, place, *refs):
+    )(*tl, *tr, inverse)
+
+
+def product_kernel(steps, last, *refs):
     ql = refs[0:4]
     qr = refs[4 : 4 + len(steps)]
     scaled, *rest = refs[4 + len(steps) :]
@@ -160,7 +167,7 @@
         before, out, ql_all, qr_all, ql_head, total = rest
     else:
         total, ql_all, qr_all, ql_head = rest
-    z, x, y, g = (place[i] for i in range(4))
+    z, x, y, g = place()
 
     total[...] = jnp.zeros_like(total)
     for n, k in enumerate(steps):
@@ -173,14 +180,16 @@
             def _(n=n, m=m):
                 ql_all[n] = ql[m][...]
 
-    @pl.loop(0, HEADS)
+    @pl.loop(0, HEADS, step=AT_ONCE)
     def _(head):
-        for n in range(len(steps)):
-            block = ql_all[n, :, head].reshape(BLOCK, HEAD_DIM)
-            ql_head[:, BLOCK * n : BLOCK * (n + 1)] = block.astype(jnp.float32).T
-        product = jnp.dot(scaled[head], qr_all[...], preferred_element_type=jnp.float32)
-        product = product.reshape(SEQS, HEAD_DIM, BLOCK * len(steps)) * ql_head[...][None]
-        total[...] += jnp.sum(product, axis=1)
+        for h in range(AT_ONCE):
+            for n in range(len(steps)):
+                block = ql_all[n, :, head + h].reshape(BLOCK, HEAD_DIM)
+                ql_head[h, :, BLOCK * n : BLOCK * (n + 1)] = block.astype(jnp.float32).T
+        rows = scaled[pl.ds(head, AT_ONCE)].reshape(AT_ONCE * SEQS * HEAD_DIM, FEATURES)
+        product = jnp.dot(rows, qr_all[...], preferred_element_type=jnp.float32)
+        product = product.reshape(AT_ONCE, SEQS, HEAD_DIM, BLOCK * len(steps)) * ql_head[...][:, None]
+        total[...] += jnp.sum(product, axis=(0, 2))
 
     if last:
         column = lax.broadcasted_iota(jnp.int32, (COLUMNS, QUERIES), 0)
@@ -199,20 +208,20 @@
             out[m] = picked[:, 16 * m : 16 * (m + 1)]
 
 
-def products(place, steps, ql, qr, scaled, before=None):
+def products(steps, ql, qr, scaled, before=None):
     columns = BLOCK * len(steps)
     last = before is not None
-    operands = [place, *ql, *qr, scaled] + ([before] if last else [])
+    operands = [*ql, *qr, scaled] + ([before] if last else [])
     out = (N, SEQS, 16) if last else (SEQS, columns)
     scratch = [
         pltpu.VMEM((len(steps), 16, HEADS, GRAD_RANK, HEAD_DIM), jnp.bfloat16),
         pltpu.VMEM((FEATURES, columns), jnp.bfloat16),
-        pltpu.VMEM((HEAD_DIM, columns), jnp.float32),
+        pltpu.VMEM((AT_ONCE, HEAD_DIM, columns), jnp.float32),
     ]
     return pl.pallas_call(
         functools.partial(product_kernel, steps, last),
         out_shape=jax.ShapeDtypeStruct(out, jnp.float32),
-        in_specs=[SMEM] + [VMEM] * (len(operands) - 1),
+        in_specs=[VMEM] * len(operands),
         out_specs=VMEM,
         scratch_shapes=scratch + ([pltpu.VMEM((SEQS, columns), jnp.float32)] if last else []),
         compiler_params=pltpu.CompilerParams(vmem_limit_bytes=16 * 2**20),
@@ -221,31 +230,29 @@
 
 
 def on_device(query_left, query_right, train_left, train_right, basis, eigen, counts):
-    loop, g = lax.axis_index("loop"), lax.axis_index("head")
-    place = jnp.stack([loop // 16, loop // 4 % 4, loop % 4, g]).astype(jnp.int32)
-
     left, right, train_right = rotated(query_left, query_right, train_left, train_right, basis)
-    left = swapped(left, 0)
+    left, train_right, inverse = lax.optimization_barrier((swapped(left, 0), train_right, inverses(eigen)))
 
     both = jnp.concatenate([left[:1], right], 1)
-    both = jnp.concatenate([both] + [along("z", both, s) for s in range(1, N)], 0)
-
-    over_x = [along("x", both, s) for s in range(1, N)]
+    over_z = [along("z", both, s) for s in range(1, N)]
     tr = [train_right] + [along("y", train_right, k) for k in range(1, N)]
     pair = [left[1:], across_heads(left[1:], 2)]
+    over_z, tr[2], pair = lax.optimization_barrier((over_z, tr[2], pair))
+    both = jnp.concatenate([both, *over_z], 0)
+
+    over_x = [along("x", both, s) for s in range(1, N)]
     tl = [pair[0], across_heads(pair[0], 1), pair[1], across_heads(pair[1], 1)]
-    inverse = inverses(place, eigen)
-    both, over_x, tr, tl, inverse = lax.optimization_barrier((both, over_x, tr, tl, inverse))
+    over_x, tl, tr = lax.optimization_barrier((over_x, tl, tr))
     both = jnp.concatenate([both, *over_x], 0)
 
-    scaled = scaled_heads(place, tl, tr, inverse)
+    scaled = scaled_heads(tl, tr, inverse)
     right = both[:, HEADS:]
     qr = [right] + [along("y", right, k) for k in range(1, N)]
     pair = [both[:, :HEADS], across_heads(both[:, :HEADS], 2)]
-    pair, qr[2], scaled = lax.optimization_barrier((pair, qr[2], scaled))
+    pair, scaled = lax.optimization_barrier((pair, scaled))
     ql = [pair[0], across_heads(pair[0], 1), pair[1], across_heads(pair[1], 1)]
-    first = products(place, (0, 2), ql, qr[0::2], scaled)
-    partial = products(place, (1, 3), ql, qr[1::2], scaled, first)
+    first = products((0, 2), ql, qr[0::2], scaled)
+    partial = products((1, 3), ql, qr[1::2], scaled, first)
 
     summed = sum([across_heads(partial[m], m) for m in range(1, N)], partial[0])
     summed = sum([along("y", summed[2 * k : 2 * k + 2], -k) for k in range(1, N)], summed[:2])

time: 76.6 us -> 72.6 us (0.948)
  Pallas kernels: 23.6 us -> 18.1 us
  starting transfers between devices: 43.8 us -> 46.4 us
  waiting for transfers between devices: 8.04 us -> 6.8 us
    pallas_call x2, Pallas kernels: 13.7 us -> 10.5 us  [products(): pl.pallas_call(functools.partial(product_kernel, steps, last), out_shape=...]
    ppermute x15, starting transfers between devices: 27.4 us -> 29.3 us  [along(): return lax.ppermute(value, 'loop', axis_shift(axis, step))]
    ppermute x9, waiting for transfers between devices: 1.59 us -> 3.31 us  [across_heads(): return lax.ppermute(value, 'head', [(i, i ^ mask) for i in range(N)])]
    pallas_call x1, Pallas kernels: 6.48 us -> 4.77 us  [scaled_heads(): pl.pallas_call(scale_kernel, out_shape=pltpu.VMEM((HEADS, SEQS * HEAD_DIM...]
    ppermute x1, waiting for transfers between devices: 1.76 us -> 0.09 us  [swapped(): return lax.ppermute(value, ('loop', 'head'), swap_shift(step))]
    ppermute x15, waiting for transfers between devices: 4.7 us -> 3.4 us  [along(): return lax.ppermute(value, 'loop', axis_shift(axis, step))]
  transfers between devices with their start and end apart: 25 -> 25, of which waited for: 5 -> 9; matrix products, arithmetic and copies ran while one was open for 0% -> 0% of each run, Pallas kernels for 20% -> 16%
where the time goes in v4:
time: 72.6 us; the launch traced here: 72.3 us
  starting transfers between devices  46.4 us (64%)
  Pallas kernels  18.1 us (25%)
  waiting for transfers between devices  6.8 us (9%)
    ppermute x15, starting transfers between devices, along(): return lax.ppermute(value, 'loop', axis_shift(axis, step))  29.3 us
    ppermute x9, starting transfers between devices, across_heads(): return lax.ppermute(value, 'head', [(i, i ^ mask) for i in range(N)])  12.5 us
    pallas_call x2, Pallas kernels, products(): pl.pallas_call(functools.partial(product_kernel, steps, last), out_shape=...  10.5 us
    pallas_call x1, Pallas kernels, scaled_heads(): pl.pallas_call(scale_kernel, out_shape=pltpu.VMEM((HEADS, SEQS * HEAD_DIM...  4.77 us
    ppermute x1, starting transfers between devices, swapped(): return lax.ppermute(value, ('loop', 'head'), swap_shift(step))  4.59 us
    ppermute x15, waiting for transfers between devices, along(): return lax.ppermute(value, 'loop', axis_shift(axis, step))  3.4 us
    ppermute x9, waiting for transfers between devices, across_heads(): return lax.ppermute(value, 'head', [(i, i ^ mask) for i in range(N)])  3.31 us
    pallas_call x1, Pallas kernels, inverses(): pl.pallas_call(inverse_kernel, out_shape=pltpu.VMEM((HEADS, HEAD_DIM, FEA...  1.66 us
  transfers between devices with their start and end apart: 25, of which 9 were waited for; matrix products, arithmetic and copies ran while one was open for 0% of the time, Pallas kernels for 16%

profile of v4, /device:TPU:1, one launch (start us, length us, event | category | flops | bytes accessed | tf_op | source)
XLA Modules:
  0.0 72.3 jit_solution(4272137083534365321)
XLA Ops:
  0.0 1.2 %shard_map.73 = (bf16[3,8,8,128]{3,2,1,0:T(8,128)(2,1)S(1)}, bf16[1,8,8,128]{3,2,1,0:T(8,128)(2,1)S(1)}, bf16[2,8,8,128]{3,2,1,0:T(8,128)(2,1)S(1)}) custom-call(bf16[1,8,8,128]{3,2,1,0:T(8,128)(2,1)} %query.1, bf16[1,8,1024]{2,1,0:T(8,128)(2,1)} %right.1, bf16[2,8,8,128]{3,2,1,0:T(8,128)(2,1)} %train.1, bf16[2,8,1024]{2,1,0:T(8,128)(2,1)} %train_right.1, ...), custom_call_target="tpu_custom_call" | custom-call | tf_op jit(solution)/shard_map/pallas_call | solution.py:81
  1.2 4.6 %collective-permute-start = (bf16[3,8,8,128]{3,2,1,0:T(8,128)(2,1)S(1)}, bf16[3,8,8,128]{3,2,1,0:T(8,128)(2,1)S(1)}, u32[]{:S(2)}, u32[]{:S(2)}) collective-permute-start(bf16[3,8,8,128]{3,2,1,0:T(8,128)(2,1)S(1)} %get-tuple-element.31), channel_id=1, source_target_pairs={{0,0},{1,4},{2,8},{3,12},{4,1},{5,5},{6,9},{7,13},{8,2},{9,6},{10,... | collective-permute-start | bytes 147464 | tf_op jit(solution)/shard_map/ppermute | solution.py:56
  5.8 1.7 %shard_map.74.refs_8_ = f32[8,128,1024]{2,1,0:T(8,128)S(1)} custom-call(bf16[32,128,1024]{2,1,0:T(8,128)(2,1)} %eigen.1), custom_call_target="tpu_custom_call" | custom-call | flops 2097152 | bytes 6291456 | tf_op jit(solution)/shard_map/pallas_call | solution.py:107
  7.6 3.1 %collective-permute-start.1 = (bf16[1,16,8,128]{3,2,1,0:T(8,128)(2,1)S(1)}, bf16[1,16,8,128]{3,2,1,0:T(8,128)(2,1)S(1)}, u32[]{:S(2)}, u32[]{:S(2)}) collective-permute-start(bf16[1,16,8,128]{3,2,1,0:T(8,128)(2,1)S(1)} %get-tuple-element.59), channel_id=1, source_target_pairs={{0,64},{4,68},{8,72},{12,76},{16,80},{20,84},{24,88},{28,92},{32,9... | collective-permute-start | bytes 98312 | tf_op jit(solution)/shard_map/ppermute | solution.py:52
  10.6 5.1 %collective-permute-start.2 = (bf16[1,16,8,128]{3,2,1,0:T(8,128)(2,1)S(1)}, bf16[1,16,8,128]{3,2,1,0:T(8,128)(2,1)S(1)}, u32[]{:S(2)}, u32[]{:S(2)}) collective-permute-start(bf16[1,16,8,128]{3,2,1,0:T(8,128)(2,1)S(1)} %get-tuple-element.59), channel_id=1, source_target_pairs={{0,128},{4,132},{8,136},{12,140},{16,144},{20,148},{24,152},{28,15... | collective-permute-start | bytes 98312 | tf_op jit(solution)/shard_map/ppermute | solution.py:52
  15.8 2.4 %collective-permute-start.3 = (bf16[1,16,8,128]{3,2,1,0:T(8,128)(2,1)S(1)}, bf16[1,16,8,128]{3,2,1,0:T(8,128)(2,1)S(1)}, u32[]{:S(2)}, u32[]{:S(2)}) collective-permute-start(bf16[1,16,8,128]{3,2,1,0:T(8,128)(2,1)S(1)} %get-tuple-element.59), channel_id=1, source_target_pairs={{0,192},{4,196},{8,200},{12,204},{16,208},{20,212},{24,216},{28,22... | collective-permute-start | bytes 98312 | tf_op jit(solution)/shard_map/ppermute | solution.py:52
  18.1 4.1 %collective-permute-start.4 = (bf16[2,8,8,128]{3,2,1,0:T(8,128)(2,1)S(1)}, bf16[2,8,8,128]{3,2,1,0:T(8,128)(2,1)S(1)}, u32[]{:S(2)}, u32[]{:S(2)}) collective-permute-start(bf16[2,8,8,128]{3,2,1,0:T(8,128)(2,1)S(1)} %get-tuple-element.49.refs_4_), channel_id=1, source_target_pairs={{0,8},{4,12},{8,0},{12,4},{16,24},{20,28},{24,16},{28,20},{32,40},... | collective-permute-start | bytes 98312 | tf_op jit(solution)/shard_map/ppermute | solution.py:52
  22.2 1.6 %collective-permute-start.11 = (bf16[2,8,8,128]{3,2,1,0:T(8,128)(2,1)S(1)}, bf16[2,8,8,128]{3,2,1,0:T(8,128)(2,1)S(1)}, u32[]{:S(2)}, u32[]{:S(2)}) collective-permute-start(bf16[2,8,8,128]{3,2,1,0:T(8,128)(2,1)S(1)} %get-tuple-element.49.refs_4_), channel_id=1, source_target_pairs={{0,4},{4,8},{8,12},{12,0},{16,20},{20,24},{24,28},{28,16},{32,36},... | collective-permute-start | bytes 98312 | tf_op jit(solution)/shard_map/ppermute | solution.py:52
  23.8 1.1 %collective-permute-start.12 = (bf16[2,8,8,128]{3,2,1,0:T(8,128)(2,1)S(1)}, bf16[2,8,8,128]{3,2,1,0:T(8,128)(2,1)S(1)}, u32[]{:S(2)}, u32[]{:S(2)}) collective-permute-start(bf16[2,8,8,128]{3,2,1,0:T(8,128)(2,1)S(1)} %get-tuple-element.49.refs_4_), channel_id=1, source_target_pairs={{0,12},{4,0},{8,4},{12,8},{16,28},{20,16},{24,20},{28,24},{32,44},... | collective-permute-start | bytes 98312 | tf_op jit(solution)/shard_map/ppermute | solution.py:52
  25.2 1.3 %collective-permute-start.6 = (bf16[4,16,8,128]{3,2,1,0:T(8,128)(2,1)S(1)}, bf16[4,16,8,128]{3,2,1,0:T(8,128)(2,1)S(1)}, u32[]{:S(2)}, u32[]{:S(2)}) collective-permute-start(bf16[4,16,8,128]{3,2,1,0:T(8,128)(2,1)S(1)} %pad_maximum_fusion), channel_id=1, source_target_pairs={{0,16},{4,20},{8,24},{12,28},{16,32},{20,36},{24,40},{28,44},{32,4... | collective-permute-start | bytes 393224 | tf_op jit(solution)/shard_map/ppermute | solution.py:52
  26.5 2.5 %collective-permute-start.7 = (bf16[4,16,8,128]{3,2,1,0:T(8,128)(2,1)S(1)}, bf16[4,16,8,128]{3,2,1,0:T(8,128)(2,1)S(1)}, u32[]{:S(2)}, u32[]{:S(2)}) collective-permute-start(bf16[4,16,8,128]{3,2,1,0:T(8,128)(2,1)S(1)} %pad_maximum_fusion), channel_id=1, source_target_pairs={{0,32},{4,36},{8,40},{12,44},{16,48},{20,52},{24,56},{28,60},{32,0... | collective-permute-start | bytes 393224 | tf_op jit(solution)/shard_map/ppermute | solution.py:52
  28.9 1.2 %collective-permute-start.8 = (bf16[4,16,8,128]{3,2,1,0:T(8,128)(2,1)S(1)}, bf16[4,16,8,128]{3,2,1,0:T(8,128)(2,1)S(1)}, u32[]{:S(2)}, u32[]{:S(2)}) collective-permute-start(bf16[4,16,8,128]{3,2,1,0:T(8,128)(2,1)S(1)} %pad_maximum_fusion), channel_id=1, source_target_pairs={{0,48},{4,52},{8,56},{12,60},{16,0},{20,4},{24,8},{28,12},{32,16},... | collective-permute-start | bytes 393224 | tf_op jit(solution)/shard_map/ppermute | solution.py:52
  30.1 5.4 %collective-permute-start.9 = (bf16[2,8,8,128]{3,2,1,0:T(8,128)(2,1)S(1)}, bf16[2,8,8,128]{3,2,1,0:T(8,128)(2,1)S(1)}, u32[]{:S(2)}, u32[]{:S(2)}) collective-permute-start(bf16[2,8,8,128]{3,2,1,0:T(8,128)(2,1)S(1)} %slice.39.refs_0_), channel_id=1, source_target_pairs={{0,1},{1,0},{2,3},{3,2},{4,5},{5,4},{6,7},{7,6},{8,9},{9,8},{10,11... | collective-permute-start | bytes 98312 | tf_op jit(solution)/shard_map/ppermute | solution.py:60
  36.8 1.2 %collective-permute-start.13 = (bf16[16,8,8,128]{3,2,1,0:T(8,128)(2,1)S(1)}, bf16[16,8,8,128]{3,2,1,0:T(8,128)(2,1)S(1)}, u32[]{:S(2)}, u32[]{:S(2)}) collective-permute-start(bf16[16,8,8,128]{3,2,1,0:T(8,128)(2,1)S(1)} %get-tuple-element.54.refs_0_), channel_id=1, source_target_pairs={{0,2},{1,3},{2,0},{3,1},{4,6},{5,7},{6,4},{7,5},{8,10},{9,11},{10,... | collective-permute-start | bytes 786440 | tf_op jit(solution)/shard_map/ppermute | solution.py:60
  38.5 4.8 %shard_map.75.refs_6_ = bf16[8,1024,1024]{2,1,0:T(8,128)(2,1)S(1)} custom-call(bf16[2,8,8,128]{3,2,1,0:T(8,128)(2,1)S(1)} %slice.39.refs_0_, bf16[2,8,8,128]{3,2,1,0:T(8,128)(2,1)S(1)} %collective-permute-done.9.refs_1_, bf16[2,8,8,128]{3,2,1,0:T(8,128)(2,1)S(1)} %collective-permute-done.5.refs_2_, ...), custom_call_target="tpu_custom_call" | custom-call | flops 4294967296 | bytes 1048576 | tf_op jit(solution)/shard_map/pallas_call | solution.py:148
  43.3 2.6 %collective-permute-start.14 = (bf16[16,8,8,128]{3,2,1,0:T(8,128)(2,1)S(1)}, bf16[16,8,8,128]{3,2,1,0:T(8,128)(2,1)S(1)}, u32[]{:S(2)}, u32[]{:S(2)}) collective-permute-start(bf16[16,8,8,128]{3,2,1,0:T(8,128)(2,1)S(1)} %get-tuple-element.54.refs_0_), channel_id=1, source_target_pairs={{0,1},{1,0},{2,3},{3,2},{4,5},{5,4},{6,7},{7,6},{8,9},{9,8},{10,11... | collective-permute-start | bytes 786440 | tf_op jit(solution)/shard_map/ppermute | solution.py:60
  46.1 2.6 %collective-permute-start.17 = (bf16[16,8,8,128]{3,2,1,0:T(8,128)(2,1)S(1)}, bf16[16,8,8,128]{3,2,1,0:T(8,128)(2,1)S(1)}, u32[]{:S(2)}, u32[]{:S(2)}) collective-permute-start(bf16[16,8,8,128]{3,2,1,0:T(8,128)(2,1)S(1)} %get-tuple-element.57.refs_4_), channel_id=1, source_target_pairs={{0,12},{4,0},{8,4},{12,8},{16,28},{20,16},{24,20},{28,24},{32,44},... | collective-permute-start | bytes 786440 | tf_op jit(solution)/shard_map/ppermute | solution.py:52
  48.7 5.0 %shard_map.76.refs_7_ = f32[8,256]{1,0:T(8,128)S(1)} custom-call(bf16[16,8,8,128]{3,2,1,0:T(8,128)(2,1)S(1)} %get-tuple-element.54.refs_0_, bf16[16,8,8,128]{3,2,1,0:T(8,128)(2,1)S(1)} %collective-permute-done.14.refs_1_, bf16[16,8,8,128]{3,2,1,0:T(8,128)(2,1)S(1)} %collective-permute-done.13.refs_2_, ...), custom_call_target="tpu_custom_call" | custom-call | flops 1048576 | bytes 4096 | tf_op jit(solution)/shard_map/pallas_call | solution.py:221
  54.7 5.5 %shard_map.77 = f32[4,8,16]{2,1,0:T(8,128)S(1)} custom-call(bf16[16,8,8,128]{3,2,1,0:T(8,128)(2,1)S(1)} %get-tuple-element.54.refs_0_, bf16[16,8,8,128]{3,2,1,0:T(8,128)(2,1)S(1)} %collective-permute-done.14.refs_1_, bf16[16,8,8,128]{3,2,1,0:T(8,128)(2,1)S(1)} %collective-permute-done.13.refs_2_, ...), custom_call_target="tpu_custom_call" | custom-call | flops 1048576 | bytes 4096 | tf_op jit(solution)/shard_map/pallas_call | solution.py:221
  60.2 2.6 %collective-permute-start.21 = (f32[8,16]{1,0:T(8,128)S(1)}, f32[8,16]{1,0:T(8,128)S(1)}, u32[]{:S(2)}, u32[]{:S(2)}) collective-permute-start(f32[8,16]{1,0:T(8,128)S(1)} %get-tuple-element.62), channel_id=1, source_target_pairs={{0,3},{1,2},{2,1},{3,0},{4,7},{5,6},{6,5},{7,4},{8,11},{9,10},{10,... | collective-permute-start | bytes 1544 | tf_op jit(solution)/shard_map/ppermute | solution.py:60
  64.1 1.2 %collective-permute-done.20 = f32[8,16]{1,0:T(8,128)S(1)} collective-permute-done((f32[8,16]{1,0:T(8,128)S(1)}, f32[8,16]{1,0:T(8,128)S(1)}, u32[]{:S(2)}, u32[]{:S(2)}) %collective-permute-start.20) | collective-permute-done | bytes 544 | tf_op jit(solution)/shard_map/ppermute | solution.py:60
  65.4 3.8 %collective-permute-start.23 = (f32[2,16]{1,0:T(2,128)S(1)}, f32[2,16]{1,0:T(2,128)S(1)}, u32[]{:S(2)}, u32[]{:S(2)}) collective-permute-start(f32[2,16]{1,0:T(2,128)S(1)} %get-tuple-element.66), channel_id=1, source_target_pairs={{0,8},{4,12},{8,0},{12,4},{16,24},{20,28},{24,16},{28,20},{32,40},... | collective-permute-start | bytes 392 | tf_op jit(solution)/shard_map/ppermute | solution.py:52
  69.2 1.0 %collective-permute-done.23 = f32[2,16]{1,0:T(2,128)S(1)} collective-permute-done((f32[2,16]{1,0:T(2,128)S(1)}, f32[2,16]{1,0:T(2,128)S(1)}, u32[]{:S(2)}, u32[]{:S(2)}) %collective-permute-start.23) | collective-permute-done | bytes 160 | tf_op jit(solution)/shard_map/ppermute | solution.py:52
  70.2 1.5 %collective-permute-done.22 = f32[2,16]{1,0:T(2,128)S(1)} collective-permute-done((f32[2,16]{1,0:T(2,128)S(1)}, f32[2,16]{1,0:T(2,128)S(1)}, u32[]{:S(2)}, u32[]{:S(2)}) %collective-permute-start.22) | collective-permute-done | bytes 160 | tf_op jit(solution)/shard_map/ppermute | solution.py:52
  (49 shorter events, 5.5 us)
Async XLA Ops:
  1.2 6.4 %collective-permute-start = (bf16[3,8,8,128]{3,2,1,0:T(8,128)(2,1)S(1)}, bf16[3,8,8,128]{3,2,1,0:T(8,128)(2,1)S(1)}, u32[]{:S(2)}, u32[]{:S(2)}) collective-permute-start(bf16[3,8,8,128]{3,2,1,0:T(8,128)(2,1)S(1)} %get-tuple-element.31), channel_id=1, source_target_pairs={{0,0},{1,4},{2,8},{3,12},{4,1},{5,5},{6,9},{7,13},{8,2},{9,6},{10,... | collective-permute-start | bytes 147464 | tf_op jit(solution)/shard_map/ppermute | solution.py:56
  7.6 14.6 %collective-permute-start.1 = (bf16[1,16,8,128]{3,2,1,0:T(8,128)(2,1)S(1)}, bf16[1,16,8,128]{3,2,1,0:T(8,128)(2,1)S(1)}, u32[]{:S(2)}, u32[]{:S(2)}) collective-permute-start(bf16[1,16,8,128]{3,2,1,0:T(8,128)(2,1)S(1)} %get-tuple-element.59), channel_id=1, source_target_pairs={{0,64},{4,68},{8,72},{12,76},{16,80},{20,84},{24,88},{28,92},{32,9... | collective-permute-start | bytes 98312 | tf_op jit(solution)/shard_map/ppermute | solution.py:52
  10.6 13.2 %collective-permute-start.2 = (bf16[1,16,8,128]{3,2,1,0:T(8,128)(2,1)S(1)}, bf16[1,16,8,128]{3,2,1,0:T(8,128)(2,1)S(1)}, u32[]{:S(2)}, u32[]{:S(2)}) collective-permute-start(bf16[1,16,8,128]{3,2,1,0:T(8,128)(2,1)S(1)} %get-tuple-element.59), channel_id=1, source_target_pairs={{0,128},{4,132},{8,136},{12,140},{16,144},{20,148},{24,152},{28,15... | collective-permute-start | bytes 98312 | tf_op jit(solution)/shard_map/ppermute | solution.py:52
  15.8 9.1 %collective-permute-start.3 = (bf16[1,16,8,128]{3,2,1,0:T(8,128)(2,1)S(1)}, bf16[1,16,8,128]{3,2,1,0:T(8,128)(2,1)S(1)}, u32[]{:S(2)}, u32[]{:S(2)}) collective-permute-start(bf16[1,16,8,128]{3,2,1,0:T(8,128)(2,1)S(1)} %get-tuple-element.59), channel_id=1, source_target_pairs={{0,192},{4,196},{8,200},{12,204},{16,208},{20,212},{24,216},{28,22... | collective-permute-start | bytes 98312 | tf_op jit(solution)/shard_map/ppermute | solution.py:52
  18.1 6.8 %collective-permute-start.4 = (bf16[2,8,8,128]{3,2,1,0:T(8,128)(2,1)S(1)}, bf16[2,8,8,128]{3,2,1,0:T(8,128)(2,1)S(1)}, u32[]{:S(2)}, u32[]{:S(2)}) collective-permute-start(bf16[2,8,8,128]{3,2,1,0:T(8,128)(2,1)S(1)} %get-tuple-element.49.refs_4_), channel_id=1, source_target_pairs={{0,8},{4,12},{8,0},{12,4},{16,24},{20,28},{24,16},{28,20},{32,40},... | collective-permute-start | bytes 98312 | tf_op jit(solution)/shard_map/ppermute | solution.py:52
  22.2 2.9 %collective-permute-start.5 = (bf16[2,8,8,128]{3,2,1,0:T(8,128)(2,1)S(1)}, bf16[2,8,8,128]{3,2,1,0:T(8,128)(2,1)S(1)}, u32[]{:S(2)}, u32[]{:S(2)}) collective-permute-start(bf16[2,8,8,128]{3,2,1,0:T(8,128)(2,1)S(1)} %slice.39.refs_0_), channel_id=1, source_target_pairs={{0,2},{1,3},{2,0},{3,1},{4,6},{5,7},{6,4},{7,5},{8,10},{9,11},{10,... | collective-permute-start | bytes 98312 | tf_op jit(solution)/shard_map/ppermute | solution.py:60
  22.2 7.9 %collective-permute-start.11 = (bf16[2,8,8,128]{3,2,1,0:T(8,128)(2,1)S(1)}, bf16[2,8,8,128]{3,2,1,0:T(8,128)(2,1)S(1)}, u32[]{:S(2)}, u32[]{:S(2)}) collective-permute-start(bf16[2,8,8,128]{3,2,1,0:T(8,128)(2,1)S(1)} %get-tuple-element.49.refs_4_), channel_id=1, source_target_pairs={{0,4},{4,8},{8,12},{12,0},{16,20},{20,24},{24,28},{28,16},{32,36},... | collective-permute-start | bytes 98312 | tf_op jit(solution)/shard_map/ppermute | solution.py:52
  23.8 11.7 %collective-permute-start.12 = (bf16[2,8,8,128]{3,2,1,0:T(8,128)(2,1)S(1)}, bf16[2,8,8,128]{3,2,1,0:T(8,128)(2,1)S(1)}, u32[]{:S(2)}, u32[]{:S(2)}) collective-permute-start(bf16[2,8,8,128]{3,2,1,0:T(8,128)(2,1)S(1)} %get-tuple-element.49.refs_4_), channel_id=1, source_target_pairs={{0,12},{4,0},{8,4},{12,8},{16,28},{20,16},{24,20},{28,24},{32,44},... | collective-permute-start | bytes 98312 | tf_op jit(solution)/shard_map/ppermute | solution.py:52
  25.2 11.5 %collective-permute-start.6 = (bf16[4,16,8,128]{3,2,1,0:T(8,128)(2,1)S(1)}, bf16[4,16,8,128]{3,2,1,0:T(8,128)(2,1)S(1)}, u32[]{:S(2)}, u32[]{:S(2)}) collective-permute-start(bf16[4,16,8,128]{3,2,1,0:T(8,128)(2,1)S(1)} %pad_maximum_fusion), channel_id=1, source_target_pairs={{0,16},{4,20},{8,24},{12,28},{16,32},{20,36},{24,40},{28,44},{32,4... | collective-permute-start | bytes 393224 | tf_op jit(solution)/shard_map/ppermute | solution.py:52
  26.5 10.3 %collective-permute-start.7 = (bf16[4,16,8,128]{3,2,1,0:T(8,128)(2,1)S(1)}, bf16[4,16,8,128]{3,2,1,0:T(8,128)(2,1)S(1)}, u32[]{:S(2)}, u32[]{:S(2)}) collective-permute-start(bf16[4,16,8,128]{3,2,1,0:T(8,128)(2,1)S(1)} %pad_maximum_fusion), channel_id=1, source_target_pairs={{0,32},{4,36},{8,40},{12,44},{16,48},{20,52},{24,56},{28,60},{32,0... | collective-permute-start | bytes 393224 | tf_op jit(solution)/shard_map/ppermute | solution.py:52
  28.9 7.8 %collective-permute-start.8 = (bf16[4,16,8,128]{3,2,1,0:T(8,128)(2,1)S(1)}, bf16[4,16,8,128]{3,2,1,0:T(8,128)(2,1)S(1)}, u32[]{:S(2)}, u32[]{:S(2)}) collective-permute-start(bf16[4,16,8,128]{3,2,1,0:T(8,128)(2,1)S(1)} %pad_maximum_fusion), channel_id=1, source_target_pairs={{0,48},{4,52},{8,56},{12,60},{16,0},{20,4},{24,8},{28,12},{32,16},... | collective-permute-start | bytes 393224 | tf_op jit(solution)/shard_map/ppermute | solution.py:52
  30.1 6.3 %collective-permute-start.9 = (bf16[2,8,8,128]{3,2,1,0:T(8,128)(2,1)S(1)}, bf16[2,8,8,128]{3,2,1,0:T(8,128)(2,1)S(1)}, u32[]{:S(2)}, u32[]{:S(2)}) collective-permute-start(bf16[2,8,8,128]{3,2,1,0:T(8,128)(2,1)S(1)} %slice.39.refs_0_), channel_id=1, source_target_pairs={{0,1},{1,0},{2,3},{3,2},{4,5},{5,4},{6,7},{7,6},{8,9},{9,8},{10,11... | collective-permute-start | bytes 98312 | tf_op jit(solution)/shard_map/ppermute | solution.py:60
  36.8 6.5 %collective-permute-start.13 = (bf16[16,8,8,128]{3,2,1,0:T(8,128)(2,1)S(1)}, bf16[16,8,8,128]{3,2,1,0:T(8,128)(2,1)S(1)}, u32[]{:S(2)}, u32[]{:S(2)}) collective-permute-start(bf16[16,8,8,128]{3,2,1,0:T(8,128)(2,1)S(1)} %get-tuple-element.54.refs_0_), channel_id=1, source_target_pairs={{0,2},{1,3},{2,0},{3,1},{4,6},{5,7},{6,4},{7,5},{8,10},{9,11},{10,... | collective-permute-start | bytes 786440 | tf_op jit(solution)/shard_map/ppermute | solution.py:60
  38.0 10.6 %collective-permute-start.18 = (bf16[16,8,8,128]{3,2,1,0:T(8,128)(2,1)S(1)}, bf16[16,8,8,128]{3,2,1,0:T(8,128)(2,1)S(1)}, u32[]{:S(2)}, u32[]{:S(2)}) collective-permute-start(bf16[16,8,8,128]{3,2,1,0:T(8,128)(2,1)S(1)} %get-tuple-element.57.refs_4_), channel_id=1, source_target_pairs={{0,8},{4,12},{8,0},{12,4},{16,24},{20,28},{24,16},{28,20},{32,40},... | collective-permute-start | bytes 786440 | tf_op jit(solution)/shard_map/ppermute | solution.py:52
  43.3 5.3 %collective-permute-start.14 = (bf16[16,8,8,128]{3,2,1,0:T(8,128)(2,1)S(1)}, bf16[16,8,8,128]{3,2,1,0:T(8,128)(2,1)S(1)}, u32[]{:S(2)}, u32[]{:S(2)}) collective-permute-start(bf16[16,8,8,128]{3,2,1,0:T(8,128)(2,1)S(1)} %get-tuple-element.54.refs_0_), channel_id=1, source_target_pairs={{0,1},{1,0},{2,3},{3,2},{4,5},{5,4},{6,7},{7,6},{8,9},{9,8},{10,11... | collective-permute-start | bytes 786440 | tf_op jit(solution)/shard_map/ppermute | solution.py:60
  45.9 2.8 %collective-permute-start.15 = (bf16[16,8,8,128]{3,2,1,0:T(8,128)(2,1)S(1)}, bf16[16,8,8,128]{3,2,1,0:T(8,128)(2,1)S(1)}, u32[]{:S(2)}, u32[]{:S(2)}) collective-permute-start(bf16[16,8,8,128]{3,2,1,0:T(8,128)(2,1)S(1)} %collective-permute-done.13.refs_2_), channel_id=1, source_target_pairs={{0,1},{1,0},{2,3},{3,2},{4,5},{5,4},{6,7},{7,6},{8,9},{9,8},{10,11... | collective-permute-start | bytes 786440 | tf_op jit(solution)/shard_map/ppermute | solution.py:60
  46.0 8.7 %collective-permute-start.16 = (bf16[16,8,8,128]{3,2,1,0:T(8,128)(2,1)S(1)}, bf16[16,8,8,128]{3,2,1,0:T(8,128)(2,1)S(1)}, u32[]{:S(2)}, u32[]{:S(2)}) collective-permute-start(bf16[16,8,8,128]{3,2,1,0:T(8,128)(2,1)S(1)} %get-tuple-element.57.refs_4_), channel_id=1, source_target_pairs={{0,4},{4,8},{8,12},{12,0},{16,20},{20,24},{24,28},{28,16},{32,36},... | collective-permute-start | bytes 786440 | tf_op jit(solution)/shard_map/ppermute | solution.py:52
  46.1 8.6 %collective-permute-start.17 = (bf16[16,8,8,128]{3,2,1,0:T(8,128)(2,1)S(1)}, bf16[16,8,8,128]{3,2,1,0:T(8,128)(2,1)S(1)}, u32[]{:S(2)}, u32[]{:S(2)}) collective-permute-start(bf16[16,8,8,128]{3,2,1,0:T(8,128)(2,1)S(1)} %get-tuple-element.57.refs_4_), channel_id=1, source_target_pairs={{0,12},{4,0},{8,4},{12,8},{16,28},{20,16},{24,20},{28,24},{32,44},... | collective-permute-start | bytes 786440 | tf_op jit(solution)/shard_map/ppermute | solution.py:52
  60.2 3.9 %collective-permute-start.21 = (f32[8,16]{1,0:T(8,128)S(1)}, f32[8,16]{1,0:T(8,128)S(1)}, u32[]{:S(2)}, u32[]{:S(2)}) collective-permute-start(f32[8,16]{1,0:T(8,128)S(1)} %get-tuple-element.62), channel_id=1, source_target_pairs={{0,3},{1,2},{2,1},{3,0},{4,7},{5,6},{6,5},{7,4},{8,11},{9,10},{10,... | collective-permute-start | bytes 1544 | tf_op jit(solution)/shard_map/ppermute | solution.py:60
  62.8 2.5 %collective-permute-start.20 = (f32[8,16]{1,0:T(8,128)S(1)}, f32[8,16]{1,0:T(8,128)S(1)}, u32[]{:S(2)}, u32[]{:S(2)}) collective-permute-start(f32[8,16]{1,0:T(8,128)S(1)} %get-tuple-element.63), channel_id=1, source_target_pairs={{0,2},{1,3},{2,0},{3,1},{4,6},{5,7},{6,4},{7,5},{8,10},{9,11},{10,... | collective-permute-start | bytes 1544 | tf_op jit(solution)/shard_map/ppermute | solution.py:60
  62.8 2.4 %collective-permute-start.19 = (f32[8,16]{1,0:T(8,128)S(1)}, f32[8,16]{1,0:T(8,128)S(1)}, u32[]{:S(2)}, u32[]{:S(2)}) collective-permute-start(f32[8,16]{1,0:T(8,128)S(1)} %get-tuple-element.61), channel_id=1, source_target_pairs={{0,1},{1,0},{2,3},{3,2},{4,5},{5,4},{6,7},{7,6},{8,9},{9,8},{10,11... | collective-permute-start | bytes 1544 | tf_op jit(solution)/shard_map/ppermute | solution.py:60
  65.3 3.9 %collective-permute-start.24 = (f32[2,16]{1,0:T(2,128)S(1)}, f32[2,16]{1,0:T(2,128)S(1)}, u32[]{:S(2)}, u32[]{:S(2)}) collective-permute-start(f32[2,16]{1,0:T(2,128)S(1)} %get-tuple-element.65), channel_id=1, source_target_pairs={{0,4},{4,8},{8,12},{12,0},{16,20},{20,24},{24,28},{28,16},{32,36},... | collective-permute-start | bytes 392 | tf_op jit(solution)/shard_map/ppermute | solution.py:52
  65.4 4.7 %collective-permute-start.23 = (f32[2,16]{1,0:T(2,128)S(1)}, f32[2,16]{1,0:T(2,128)S(1)}, u32[]{:S(2)}, u32[]{:S(2)}) collective-permute-start(f32[2,16]{1,0:T(2,128)S(1)} %get-tuple-element.66), channel_id=1, source_target_pairs={{0,8},{4,12},{8,0},{12,4},{16,24},{20,28},{24,16},{28,20},{32,40},... | collective-permute-start | bytes 392 | tf_op jit(solution)/shard_map/ppermute | solution.py:52
  69.2 2.4 %collective-permute-start.22 = (f32[2,16]{1,0:T(2,128)S(1)}, f32[2,16]{1,0:T(2,128)S(1)}, u32[]{:S(2)}, u32[]{:S(2)}) collective-permute-start(f32[2,16]{1,0:T(2,128)S(1)} %get-tuple-element.64), channel_id=1, source_target_pairs={{0,12},{4,0},{8,4},{12,8},{16,28},{20,16},{24,20},{28,24},{32,44},... | collective-permute-start | bytes 392 | tf_op jit(solution)/shard_map/ppermute | solution.py:52
  (2 other events, 10.8 us)

commit v5 on v4

--- a/solution.py
+++ b/solution.py
@@ -249,7 +249,6 @@
     right = both[:, HEADS:]
     qr = [right] + [along("y", right, k) for k in range(1, N)]
     pair = [both[:, :HEADS], across_heads(both[:, :HEADS], 2)]
-    pair, scaled = lax.optimization_barrier((pair, scaled))
     ql = [pair[0], across_heads(pair[0], 1), pair[1], across_heads(pair[1], 1)]
     first = products((0, 2), ql, qr[0::2], scaled)
     partial = products((1, 3), ql, qr[1::2], scaled, first)

time: 72.6 us -> 71.9 us (level)
  starting transfers between devices: 46.4 us -> 45.5 us
    ppermute x15, starting transfers between devices: 29.3 us -> 26.9 us  [along(): return lax.ppermute(value, 'loop', axis_shift(axis, step))]
    ppermute x9, starting transfers between devices: 12.5 us -> 14 us  [across_heads(): return lax.ppermute(value, 'head', [(i, i ^ mask) for i in range(N)])]
where the time goes in v5:
time: 71.9 us; the launch traced here: 71.6 us
  starting transfers between devices  45.5 us (63%)
  Pallas kernels  18.1 us (25%)
  waiting for transfers between devices  6.98 us (10%)
    ppermute x15, starting transfers between devices, along(): return lax.ppermute(value, 'loop', axis_shift(axis, step))  26.9 us
    ppermute x9, starting transfers between devices, across_heads(): return lax.ppermute(value, 'head', [(i, i ^ mask) for i in range(N)])  14 us
    pallas_call x2, Pallas kernels, products(): pl.pallas_call(functools.partial(product_kernel, steps, last), out_shape=...  10.5 us
    pallas_call x1, Pallas kernels, scaled_heads(): pl.pallas_call(scale_kernel, out_shape=pltpu.VMEM((HEADS, SEQS * HEAD_DIM...  4.77 us
    ppermute x1, starting transfers between devices, swapped(): return lax.ppermute(value, ('loop', 'head'), swap_shift(step))  4.59 us
    ppermute x9, waiting for transfers between devices, across_heads(): return lax.ppermute(value, 'head', [(i, i ^ mask) for i in range(N)])  3.46 us
    ppermute x15, waiting for transfers between devices, along(): return lax.ppermute(value, 'loop', axis_shift(axis, step))  3.42 us
    pallas_call x1, Pallas kernels, inverses(): pl.pallas_call(inverse_kernel, out_shape=pltpu.VMEM((HEADS, HEAD_DIM, FEA...  1.66 us
  transfers between devices with their start and end apart: 25, of which 9 were waited for; matrix products, arithmetic and copies ran while one was open for 0% of the time, Pallas kernels for 16%

profile of v5, /device:TPU:1, one launch (start us, length us, event | category | flops | bytes accessed | tf_op | source)
XLA Modules:
  0.0 71.6 jit_solution(594279341231083597)
XLA Ops:
  0.0 1.2 %shard_map.73 = (bf16[3,8,8,128]{3,2,1,0:T(8,128)(2,1)S(1)}, bf16[1,8,8,128]{3,2,1,0:T(8,128)(2,1)S(1)}, bf16[2,8,8,128]{3,2,1,0:T(8,128)(2,1)S(1)}) custom-call(bf16[1,8,8,128]{3,2,1,0:T(8,128)(2,1)} %query.1, bf16[1,8,1024]{2,1,0:T(8,128)(2,1)} %right.1, bf16[2,8,8,128]{3,2,1,0:T(8,128)(2,1)} %train.1, bf16[2,8,1024]{2,1,0:T(8,128)(2,1)} %train_right.1, ...), custom_call_target="tpu_custom_call" | custom-call | tf_op jit(solution)/shard_map/pallas_call | solution.py:81
  1.2 4.6 %collective-permute-start = (bf16[3,8,8,128]{3,2,1,0:T(8,128)(2,1)S(1)}, bf16[3,8,8,128]{3,2,1,0:T(8,128)(2,1)S(1)}, u32[]{:S(2)}, u32[]{:S(2)}) collective-permute-start(bf16[3,8,8,128]{3,2,1,0:T(8,128)(2,1)S(1)} %get-tuple-element.28), channel_id=1, source_target_pairs={{0,0},{1,4},{2,8},{3,12},{4,1},{5,5},{6,9},{7,13},{8,2},{9,6},{10,... | collective-permute-start | bytes 147464 | tf_op jit(solution)/shard_map/ppermute | solution.py:56
  5.8 1.7 %shard_map.74.refs_8_ = f32[8,128,1024]{2,1,0:T(8,128)S(1)} custom-call(bf16[32,128,1024]{2,1,0:T(8,128)(2,1)} %eigen.1), custom_call_target="tpu_custom_call" | custom-call | flops 2097152 | bytes 6291456 | tf_op jit(solution)/shard_map/pallas_call | solution.py:107
  7.6 3.1 %collective-permute-start.1 = (bf16[1,16,8,128]{3,2,1,0:T(8,128)(2,1)S(1)}, bf16[1,16,8,128]{3,2,1,0:T(8,128)(2,1)S(1)}, u32[]{:S(2)}, u32[]{:S(2)}) collective-permute-start(bf16[1,16,8,128]{3,2,1,0:T(8,128)(2,1)S(1)} %get-tuple-element.53), channel_id=1, source_target_pairs={{0,64},{4,68},{8,72},{12,76},{16,80},{20,84},{24,88},{28,92},{32,9... | collective-permute-start | bytes 98312 | tf_op jit(solution)/shard_map/ppermute | solution.py:52
  10.6 5.1 %collective-permute-start.2 = (bf16[1,16,8,128]{3,2,1,0:T(8,128)(2,1)S(1)}, bf16[1,16,8,128]{3,2,1,0:T(8,128)(2,1)S(1)}, u32[]{:S(2)}, u32[]{:S(2)}) collective-permute-start(bf16[1,16,8,128]{3,2,1,0:T(8,128)(2,1)S(1)} %get-tuple-element.53), channel_id=1, source_target_pairs={{0,128},{4,132},{8,136},{12,140},{16,144},{20,148},{24,152},{28,15... | collective-permute-start | bytes 98312 | tf_op jit(solution)/shard_map/ppermute | solution.py:52
  15.8 2.4 %collective-permute-start.3 = (bf16[1,16,8,128]{3,2,1,0:T(8,128)(2,1)S(1)}, bf16[1,16,8,128]{3,2,1,0:T(8,128)(2,1)S(1)}, u32[]{:S(2)}, u32[]{:S(2)}) collective-permute-start(bf16[1,16,8,128]{3,2,1,0:T(8,128)(2,1)S(1)} %get-tuple-element.53), channel_id=1, source_target_pairs={{0,192},{4,196},{8,200},{12,204},{16,208},{20,212},{24,216},{28,22... | collective-permute-start | bytes 98312 | tf_op jit(solution)/shard_map/ppermute | solution.py:52
  18.1 4.1 %collective-permute-start.4 = (bf16[2,8,8,128]{3,2,1,0:T(8,128)(2,1)S(1)}, bf16[2,8,8,128]{3,2,1,0:T(8,128)(2,1)S(1)}, u32[]{:S(2)}, u32[]{:S(2)}) collective-permute-start(bf16[2,8,8,128]{3,2,1,0:T(8,128)(2,1)S(1)} %get-tuple-element.46.refs_4_), channel_id=1, source_target_pairs={{0,8},{4,12},{8,0},{12,4},{16,24},{20,28},{24,16},{28,20},{32,40},... | collective-permute-start | bytes 98312 | tf_op jit(solution)/shard_map/ppermute | solution.py:52
  22.2 1.6 %collective-permute-start.11 = (bf16[2,8,8,128]{3,2,1,0:T(8,128)(2,1)S(1)}, bf16[2,8,8,128]{3,2,1,0:T(8,128)(2,1)S(1)}, u32[]{:S(2)}, u32[]{:S(2)}) collective-permute-start(bf16[2,8,8,128]{3,2,1,0:T(8,128)(2,1)S(1)} %get-tuple-element.46.refs_4_), channel_id=1, source_target_pairs={{0,4},{4,8},{8,12},{12,0},{16,20},{20,24},{24,28},{28,16},{32,36},... | collective-permute-start | bytes 98312 | tf_op jit(solution)/shard_map/ppermute | solution.py:52
  25.2 1.3 %collective-permute-start.6 = (bf16[4,16,8,128]{3,2,1,0:T(8,128)(2,1)S(1)}, bf16[4,16,8,128]{3,2,1,0:T(8,128)(2,1)S(1)}, u32[]{:S(2)}, u32[]{:S(2)}) collective-permute-start(bf16[4,16,8,128]{3,2,1,0:T(8,128)(2,1)S(1)} %pad_maximum_fusion), channel_id=1, source_target_pairs={{0,16},{4,20},{8,24},{12,28},{16,32},{20,36},{24,40},{28,44},{32,4... | collective-permute-start | bytes 393224 | tf_op jit(solution)/shard_map/ppermute | solution.py:52
  26.5 2.5 %collective-permute-start.7 = (bf16[4,16,8,128]{3,2,1,0:T(8,128)(2,1)S(1)}, bf16[4,16,8,128]{3,2,1,0:T(8,128)(2,1)S(1)}, u32[]{:S(2)}, u32[]{:S(2)}) collective-permute-start(bf16[4,16,8,128]{3,2,1,0:T(8,128)(2,1)S(1)} %pad_maximum_fusion), channel_id=1, source_target_pairs={{0,32},{4,36},{8,40},{12,44},{16,48},{20,52},{24,56},{28,60},{32,0... | collective-permute-start | bytes 393224 | tf_op jit(solution)/shard_map/ppermute | solution.py:52
  28.9 1.2 %collective-permute-start.8 = (bf16[4,16,8,128]{3,2,1,0:T(8,128)(2,1)S(1)}, bf16[4,16,8,128]{3,2,1,0:T(8,128)(2,1)S(1)}, u32[]{:S(2)}, u32[]{:S(2)}) collective-permute-start(bf16[4,16,8,128]{3,2,1,0:T(8,128)(2,1)S(1)} %pad_maximum_fusion), channel_id=1, source_target_pairs={{0,48},{4,52},{8,56},{12,60},{16,0},{20,4},{24,8},{28,12},{32,16},... | collective-permute-start | bytes 393224 | tf_op jit(solution)/shard_map/ppermute | solution.py:52
  30.1 5.4 %collective-permute-start.10 = (bf16[2,8,8,128]{3,2,1,0:T(8,128)(2,1)S(1)}, bf16[2,8,8,128]{3,2,1,0:T(8,128)(2,1)S(1)}, u32[]{:S(2)}, u32[]{:S(2)}) collective-permute-start(bf16[2,8,8,128]{3,2,1,0:T(8,128)(2,1)S(1)} %collective-permute-done.5.refs_2_), channel_id=1, source_target_pairs={{0,1},{1,0},{2,3},{3,2},{4,5},{5,4},{6,7},{7,6},{8,9},{9,8},{10,11... | collective-permute-start | bytes 98312 | tf_op jit(solution)/shard_map/ppermute | solution.py:60
  36.8 1.2 %collective-permute-start.14 = (bf16[16,8,8,128]{3,2,1,0:T(8,128)(2,1)S(1)}, bf16[16,8,8,128]{3,2,1,0:T(8,128)(2,1)S(1)}, u32[]{:S(2)}, u32[]{:S(2)}) collective-permute-start(bf16[16,8,8,128]{3,2,1,0:T(8,128)(2,1)S(1)} %get-tuple-element.52.refs_0_), channel_id=1, source_target_pairs={{0,2},{1,3},{2,0},{3,1},{4,6},{5,7},{6,4},{7,5},{8,10},{9,11},{10,... | collective-permute-start | bytes 786440 | tf_op jit(solution)/shard_map/ppermute | solution.py:60
  38.0 2.5 %collective-permute-start.13 = (bf16[16,8,8,128]{3,2,1,0:T(8,128)(2,1)S(1)}, bf16[16,8,8,128]{3,2,1,0:T(8,128)(2,1)S(1)}, u32[]{:S(2)}, u32[]{:S(2)}) collective-permute-start(bf16[16,8,8,128]{3,2,1,0:T(8,128)(2,1)S(1)} %get-tuple-element.52.refs_0_), channel_id=1, source_target_pairs={{0,1},{1,0},{2,3},{3,2},{4,5},{5,4},{6,7},{7,6},{8,9},{9,8},{10,11... | collective-permute-start | bytes 786440 | tf_op jit(solution)/shard_map/ppermute | solution.py:60
  40.8 2.4 %collective-permute-start.17 = (bf16[16,8,8,128]{3,2,1,0:T(8,128)(2,1)S(1)}, bf16[16,8,8,128]{3,2,1,0:T(8,128)(2,1)S(1)}, u32[]{:S(2)}, u32[]{:S(2)}) collective-permute-start(bf16[16,8,8,128]{3,2,1,0:T(8,128)(2,1)S(1)} %get-tuple-element.51.refs_4_), channel_id=1, source_target_pairs={{0,12},{4,0},{8,4},{12,8},{16,28},{20,16},{24,20},{28,24},{32,44},... | collective-permute-start | bytes 786440 | tf_op jit(solution)/shard_map/ppermute | solution.py:52
  43.3 2.4 %collective-permute-start.15 = (bf16[16,8,8,128]{3,2,1,0:T(8,128)(2,1)S(1)}, bf16[16,8,8,128]{3,2,1,0:T(8,128)(2,1)S(1)}, u32[]{:S(2)}, u32[]{:S(2)}) collective-permute-start(bf16[16,8,8,128]{3,2,1,0:T(8,128)(2,1)S(1)} %collective-permute-done.14.refs_2_), channel_id=1, source_target_pairs={{0,1},{1,0},{2,3},{3,2},{4,5},{5,4},{6,7},{7,6},{8,9},{9,8},{10,11... | collective-permute-start | bytes 786440 | tf_op jit(solution)/shard_map/ppermute | solution.py:60
  45.7 4.8 %shard_map.75.refs_6_ = bf16[8,1024,1024]{2,1,0:T(8,128)(2,1)S(1)} custom-call(bf16[2,8,8,128]{3,2,1,0:T(8,128)(2,1)S(1)} %slice.39.refs_0_, bf16[2,8,8,128]{3,2,1,0:T(8,128)(2,1)S(1)} %collective-permute-done.9.refs_1_, bf16[2,8,8,128]{3,2,1,0:T(8,128)(2,1)S(1)} %collective-permute-done.5.refs_2_, ...), custom_call_target="tpu_custom_call" | custom-call | flops 4294967296 | bytes 1048576 | tf_op jit(solution)/shard_map/pallas_call | solution.py:148
  50.5 5.0 %shard_map.76.refs_7_ = f32[8,256]{1,0:T(8,128)S(1)} custom-call(bf16[16,8,8,128]{3,2,1,0:T(8,128)(2,1)S(1)} %get-tuple-element.52.refs_0_, bf16[16,8,8,128]{3,2,1,0:T(8,128)(2,1)S(1)} %collective-permute-done.13.refs_1_, bf16[16,8,8,128]{3,2,1,0:T(8,128)(2,1)S(1)} %collective-permute-done.14.refs_2_, ...), custom_call_target="tpu_custom_call" | custom-call | flops 1048576 | bytes 4096 | tf_op jit(solution)/shard_map/pallas_call | solution.py:221
  55.5 5.5 %shard_map.77 = f32[4,8,16]{2,1,0:T(8,128)S(1)} custom-call(bf16[16,8,8,128]{3,2,1,0:T(8,128)(2,1)S(1)} %get-tuple-element.52.refs_0_, bf16[16,8,8,128]{3,2,1,0:T(8,128)(2,1)S(1)} %collective-permute-done.13.refs_1_, bf16[16,8,8,128]{3,2,1,0:T(8,128)(2,1)S(1)} %collective-permute-done.14.refs_2_, ...), custom_call_target="tpu_custom_call" | custom-call | flops 1048576 | bytes 4096 | tf_op jit(solution)/shard_map/pallas_call | solution.py:221
  62.2 1.2 %collective-permute-start.21 = (f32[8,16]{1,0:T(8,128)S(1)}, f32[8,16]{1,0:T(8,128)S(1)}, u32[]{:S(2)}, u32[]{:S(2)}) collective-permute-start(f32[8,16]{1,0:T(8,128)S(1)} %get-tuple-element.56), channel_id=1, source_target_pairs={{0,3},{1,2},{2,1},{3,0},{4,7},{5,6},{6,5},{7,4},{8,11},{9,10},{10,... | collective-permute-start | bytes 1544 | tf_op jit(solution)/shard_map/ppermute | solution.py:60
  64.2 1.4 %collective-permute-done.21 = f32[8,16]{1,0:T(8,128)S(1)} collective-permute-done((f32[8,16]{1,0:T(8,128)S(1)}, f32[8,16]{1,0:T(8,128)S(1)}, u32[]{:S(2)}, u32[]{:S(2)}) %collective-permute-start.21) | collective-permute-done | bytes 544 | tf_op jit(solution)/shard_map/ppermute | solution.py:60
  65.8 1.2 %collective-permute-start.23 = (f32[2,16]{1,0:T(2,128)S(1)}, f32[2,16]{1,0:T(2,128)S(1)}, u32[]{:S(2)}, u32[]{:S(2)}) collective-permute-start(f32[2,16]{1,0:T(2,128)S(1)} %get-tuple-element.60), channel_id=1, source_target_pairs={{0,8},{4,12},{8,0},{12,4},{16,24},{20,28},{24,16},{28,20},{32,40},... | collective-permute-start | bytes 392 | tf_op jit(solution)/shard_map/ppermute | solution.py:52
  68.1 1.6 %collective-permute-done.23 = f32[2,16]{1,0:T(2,128)S(1)} collective-permute-done((f32[2,16]{1,0:T(2,128)S(1)}, f32[2,16]{1,0:T(2,128)S(1)}, u32[]{:S(2)}, u32[]{:S(2)}) %collective-permute-start.23) | collective-permute-done | bytes 160 | tf_op jit(solution)/shard_map/ppermute | solution.py:52
  69.7 1.2 %collective-permute-done.24 = f32[2,16]{1,0:T(2,128)S(1)} collective-permute-done((f32[2,16]{1,0:T(2,128)S(1)}, f32[2,16]{1,0:T(2,128)S(1)}, u32[]{:S(2)}, u32[]{:S(2)}) %collective-permute-start.24) | collective-permute-done | bytes 160 | tf_op jit(solution)/shard_map/ppermute | solution.py:52
  (49 shorter events, 7.0 us)
Async XLA Ops:
  1.2 6.4 %collective-permute-start = (bf16[3,8,8,128]{3,2,1,0:T(8,128)(2,1)S(1)}, bf16[3,8,8,128]{3,2,1,0:T(8,128)(2,1)S(1)}, u32[]{:S(2)}, u32[]{:S(2)}) collective-permute-start(bf16[3,8,8,128]{3,2,1,0:T(8,128)(2,1)S(1)} %get-tuple-element.28), channel_id=1, source_target_pairs={{0,0},{1,4},{2,8},{3,12},{4,1},{5,5},{6,9},{7,13},{8,2},{9,6},{10,... | collective-permute-start | bytes 147464 | tf_op jit(solution)/shard_map/ppermute | solution.py:56
  7.6 14.6 %collective-permute-start.1 = (bf16[1,16,8,128]{3,2,1,0:T(8,128)(2,1)S(1)}, bf16[1,16,8,128]{3,2,1,0:T(8,128)(2,1)S(1)}, u32[]{:S(2)}, u32[]{:S(2)}) collective-permute-start(bf16[1,16,8,128]{3,2,1,0:T(8,128)(2,1)S(1)} %get-tuple-element.53), channel_id=1, source_target_pairs={{0,64},{4,68},{8,72},{12,76},{16,80},{20,84},{24,88},{28,92},{32,9... | collective-permute-start | bytes 98312 | tf_op jit(solution)/shard_map/ppermute | solution.py:52
  10.6 13.2 %collective-permute-start.2 = (bf16[1,16,8,128]{3,2,1,0:T(8,128)(2,1)S(1)}, bf16[1,16,8,128]{3,2,1,0:T(8,128)(2,1)S(1)}, u32[]{:S(2)}, u32[]{:S(2)}) collective-permute-start(bf16[1,16,8,128]{3,2,1,0:T(8,128)(2,1)S(1)} %get-tuple-element.53), channel_id=1, source_target_pairs={{0,128},{4,132},{8,136},{12,140},{16,144},{20,148},{24,152},{28,15... | collective-permute-start | bytes 98312 | tf_op jit(solution)/shard_map/ppermute | solution.py:52
  15.8 9.1 %collective-permute-start.3 = (bf16[1,16,8,128]{3,2,1,0:T(8,128)(2,1)S(1)}, bf16[1,16,8,128]{3,2,1,0:T(8,128)(2,1)S(1)}, u32[]{:S(2)}, u32[]{:S(2)}) collective-permute-start(bf16[1,16,8,128]{3,2,1,0:T(8,128)(2,1)S(1)} %get-tuple-element.53), channel_id=1, source_target_pairs={{0,192},{4,196},{8,200},{12,204},{16,208},{20,212},{24,216},{28,22... | collective-permute-start | bytes 98312 | tf_op jit(solution)/shard_map/ppermute | solution.py:52
  18.1 6.8 %collective-permute-start.4 = (bf16[2,8,8,128]{3,2,1,0:T(8,128)(2,1)S(1)}, bf16[2,8,8,128]{3,2,1,0:T(8,128)(2,1)S(1)}, u32[]{:S(2)}, u32[]{:S(2)}) collective-permute-start(bf16[2,8,8,128]{3,2,1,0:T(8,128)(2,1)S(1)} %get-tuple-element.46.refs_4_), channel_id=1, source_target_pairs={{0,8},{4,12},{8,0},{12,4},{16,24},{20,28},{24,16},{28,20},{32,40},... | collective-permute-start | bytes 98312 | tf_op jit(solution)/shard_map/ppermute | solution.py:52
  22.2 2.9 %collective-permute-start.5 = (bf16[2,8,8,128]{3,2,1,0:T(8,128)(2,1)S(1)}, bf16[2,8,8,128]{3,2,1,0:T(8,128)(2,1)S(1)}, u32[]{:S(2)}, u32[]{:S(2)}) collective-permute-start(bf16[2,8,8,128]{3,2,1,0:T(8,128)(2,1)S(1)} %slice.39.refs_0_), channel_id=1, source_target_pairs={{0,2},{1,3},{2,0},{3,1},{4,6},{5,7},{6,4},{7,5},{8,10},{9,11},{10,... | collective-permute-start | bytes 98312 | tf_op jit(solution)/shard_map/ppermute | solution.py:60
  22.2 7.9 %collective-permute-start.11 = (bf16[2,8,8,128]{3,2,1,0:T(8,128)(2,1)S(1)}, bf16[2,8,8,128]{3,2,1,0:T(8,128)(2,1)S(1)}, u32[]{:S(2)}, u32[]{:S(2)}) collective-permute-start(bf16[2,8,8,128]{3,2,1,0:T(8,128)(2,1)S(1)} %get-tuple-element.46.refs_4_), channel_id=1, source_target_pairs={{0,4},{4,8},{8,12},{12,0},{16,20},{20,24},{24,28},{28,16},{32,36},... | collective-permute-start | bytes 98312 | tf_op jit(solution)/shard_map/ppermute | solution.py:52
  23.8 11.7 %collective-permute-start.12 = (bf16[2,8,8,128]{3,2,1,0:T(8,128)(2,1)S(1)}, bf16[2,8,8,128]{3,2,1,0:T(8,128)(2,1)S(1)}, u32[]{:S(2)}, u32[]{:S(2)}) collective-permute-start(bf16[2,8,8,128]{3,2,1,0:T(8,128)(2,1)S(1)} %get-tuple-element.46.refs_4_), channel_id=1, source_target_pairs={{0,12},{4,0},{8,4},{12,8},{16,28},{20,16},{24,20},{28,24},{32,44},... | collective-permute-start | bytes 98312 | tf_op jit(solution)/shard_map/ppermute | solution.py:52
  25.2 11.5 %collective-permute-start.6 = (bf16[4,16,8,128]{3,2,1,0:T(8,128)(2,1)S(1)}, bf16[4,16,8,128]{3,2,1,0:T(8,128)(2,1)S(1)}, u32[]{:S(2)}, u32[]{:S(2)}) collective-permute-start(bf16[4,16,8,128]{3,2,1,0:T(8,128)(2,1)S(1)} %pad_maximum_fusion), channel_id=1, source_target_pairs={{0,16},{4,20},{8,24},{12,28},{16,32},{20,36},{24,40},{28,44},{32,4... | collective-permute-start | bytes 393224 | tf_op jit(solution)/shard_map/ppermute | solution.py:52
  26.5 10.3 %collective-permute-start.7 = (bf16[4,16,8,128]{3,2,1,0:T(8,128)(2,1)S(1)}, bf16[4,16,8,128]{3,2,1,0:T(8,128)(2,1)S(1)}, u32[]{:S(2)}, u32[]{:S(2)}) collective-permute-start(bf16[4,16,8,128]{3,2,1,0:T(8,128)(2,1)S(1)} %pad_maximum_fusion), channel_id=1, source_target_pairs={{0,32},{4,36},{8,40},{12,44},{16,48},{20,52},{24,56},{28,60},{32,0... | collective-permute-start | bytes 393224 | tf_op jit(solution)/shard_map/ppermute | solution.py:52
  28.9 7.8 %collective-permute-start.8 = (bf16[4,16,8,128]{3,2,1,0:T(8,128)(2,1)S(1)}, bf16[4,16,8,128]{3,2,1,0:T(8,128)(2,1)S(1)}, u32[]{:S(2)}, u32[]{:S(2)}) collective-permute-start(bf16[4,16,8,128]{3,2,1,0:T(8,128)(2,1)S(1)} %pad_maximum_fusion), channel_id=1, source_target_pairs={{0,48},{4,52},{8,56},{12,60},{16,0},{20,4},{24,8},{28,12},{32,16},... | collective-permute-start | bytes 393224 | tf_op jit(solution)/shard_map/ppermute | solution.py:52
  30.1 6.3 %collective-permute-start.10 = (bf16[2,8,8,128]{3,2,1,0:T(8,128)(2,1)S(1)}, bf16[2,8,8,128]{3,2,1,0:T(8,128)(2,1)S(1)}, u32[]{:S(2)}, u32[]{:S(2)}) collective-permute-start(bf16[2,8,8,128]{3,2,1,0:T(8,128)(2,1)S(1)} %collective-permute-done.5.refs_2_), channel_id=1, source_target_pairs={{0,1},{1,0},{2,3},{3,2},{4,5},{5,4},{6,7},{7,6},{8,9},{9,8},{10,11... | collective-permute-start | bytes 98312 | tf_op jit(solution)/shard_map/ppermute | solution.py:60
  36.8 6.4 %collective-permute-start.14 = (bf16[16,8,8,128]{3,2,1,0:T(8,128)(2,1)S(1)}, bf16[16,8,8,128]{3,2,1,0:T(8,128)(2,1)S(1)}, u32[]{:S(2)}, u32[]{:S(2)}) collective-permute-start(bf16[16,8,8,128]{3,2,1,0:T(8,128)(2,1)S(1)} %get-tuple-element.52.refs_0_), channel_id=1, source_target_pairs={{0,2},{1,3},{2,0},{3,1},{4,6},{5,7},{6,4},{7,5},{8,10},{9,11},{10,... | collective-permute-start | bytes 786440 | tf_op jit(solution)/shard_map/ppermute | solution.py:60
  38.0 12.4 %collective-permute-start.13 = (bf16[16,8,8,128]{3,2,1,0:T(8,128)(2,1)S(1)}, bf16[16,8,8,128]{3,2,1,0:T(8,128)(2,1)S(1)}, u32[]{:S(2)}, u32[]{:S(2)}) collective-permute-start(bf16[16,8,8,128]{3,2,1,0:T(8,128)(2,1)S(1)} %get-tuple-element.52.refs_0_), channel_id=1, source_target_pairs={{0,1},{1,0},{2,3},{3,2},{4,5},{5,4},{6,7},{7,6},{8,9},{9,8},{10,11... | collective-permute-start | bytes 786440 | tf_op jit(solution)/shard_map/ppermute | solution.py:60
  40.5 9.9 %collective-permute-start.18 = (bf16[16,8,8,128]{3,2,1,0:T(8,128)(2,1)S(1)}, bf16[16,8,8,128]{3,2,1,0:T(8,128)(2,1)S(1)}, u32[]{:S(2)}, u32[]{:S(2)}) collective-permute-start(bf16[16,8,8,128]{3,2,1,0:T(8,128)(2,1)S(1)} %get-tuple-element.51.refs_4_), channel_id=1, source_target_pairs={{0,8},{4,12},{8,0},{12,4},{16,24},{20,28},{24,16},{28,20},{32,40},... | collective-permute-start | bytes 786440 | tf_op jit(solution)/shard_map/ppermute | solution.py:52
  40.6 14.9 %collective-permute-start.16 = (bf16[16,8,8,128]{3,2,1,0:T(8,128)(2,1)S(1)}, bf16[16,8,8,128]{3,2,1,0:T(8,128)(2,1)S(1)}, u32[]{:S(2)}, u32[]{:S(2)}) collective-permute-start(bf16[16,8,8,128]{3,2,1,0:T(8,128)(2,1)S(1)} %get-tuple-element.51.refs_4_), channel_id=1, source_target_pairs={{0,4},{4,8},{8,12},{12,0},{16,20},{20,24},{24,28},{28,16},{32,36},... | collective-permute-start | bytes 786440 | tf_op jit(solution)/shard_map/ppermute | solution.py:52
  40.8 14.7 %collective-permute-start.17 = (bf16[16,8,8,128]{3,2,1,0:T(8,128)(2,1)S(1)}, bf16[16,8,8,128]{3,2,1,0:T(8,128)(2,1)S(1)}, u32[]{:S(2)}, u32[]{:S(2)}) collective-permute-start(bf16[16,8,8,128]{3,2,1,0:T(8,128)(2,1)S(1)} %get-tuple-element.51.refs_4_), channel_id=1, source_target_pairs={{0,12},{4,0},{8,4},{12,8},{16,28},{20,16},{24,20},{28,24},{32,44},... | collective-permute-start | bytes 786440 | tf_op jit(solution)/shard_map/ppermute | solution.py:52
  43.3 7.2 %collective-permute-start.15 = (bf16[16,8,8,128]{3,2,1,0:T(8,128)(2,1)S(1)}, bf16[16,8,8,128]{3,2,1,0:T(8,128)(2,1)S(1)}, u32[]{:S(2)}, u32[]{:S(2)}) collective-permute-start(bf16[16,8,8,128]{3,2,1,0:T(8,128)(2,1)S(1)} %collective-permute-done.14.refs_2_), channel_id=1, source_target_pairs={{0,1},{1,0},{2,3},{3,2},{4,5},{5,4},{6,7},{7,6},{8,9},{9,8},{10,11... | collective-permute-start | bytes 786440 | tf_op jit(solution)/shard_map/ppermute | solution.py:60
  61.0 2.5 %collective-permute-start.19 = (f32[8,16]{1,0:T(8,128)S(1)}, f32[8,16]{1,0:T(8,128)S(1)}, u32[]{:S(2)}, u32[]{:S(2)}) collective-permute-start(f32[8,16]{1,0:T(8,128)S(1)} %get-tuple-element.55), channel_id=1, source_target_pairs={{0,1},{1,0},{2,3},{3,2},{4,5},{5,4},{6,7},{7,6},{8,9},{9,8},{10,11... | collective-permute-start | bytes 1544 | tf_op jit(solution)/shard_map/ppermute | solution.py:60
  61.7 2.5 %collective-permute-start.20 = (f32[8,16]{1,0:T(8,128)S(1)}, f32[8,16]{1,0:T(8,128)S(1)}, u32[]{:S(2)}, u32[]{:S(2)}) collective-permute-start(f32[8,16]{1,0:T(8,128)S(1)} %get-tuple-element.57), channel_id=1, source_target_pairs={{0,2},{1,3},{2,0},{3,1},{4,6},{5,7},{6,4},{7,5},{8,10},{9,11},{10,... | collective-permute-start | bytes 1544 | tf_op jit(solution)/shard_map/ppermute | solution.py:60
  62.2 3.4 %collective-permute-start.21 = (f32[8,16]{1,0:T(8,128)S(1)}, f32[8,16]{1,0:T(8,128)S(1)}, u32[]{:S(2)}, u32[]{:S(2)}) collective-permute-start(f32[8,16]{1,0:T(8,128)S(1)} %get-tuple-element.56), channel_id=1, source_target_pairs={{0,3},{1,2},{2,1},{3,0},{4,7},{5,6},{6,5},{7,4},{8,11},{9,10},{10,... | collective-permute-start | bytes 1544 | tf_op jit(solution)/shard_map/ppermute | solution.py:60
  65.6 2.5 %collective-permute-start.22 = (f32[2,16]{1,0:T(2,128)S(1)}, f32[2,16]{1,0:T(2,128)S(1)}, u32[]{:S(2)}, u32[]{:S(2)}) collective-permute-start(f32[2,16]{1,0:T(2,128)S(1)} %get-tuple-element.58), channel_id=1, source_target_pairs={{0,12},{4,0},{8,4},{12,8},{16,28},{20,16},{24,20},{28,24},{32,44},... | collective-permute-start | bytes 392 | tf_op jit(solution)/shard_map/ppermute | solution.py:52
  65.8 3.9 %collective-permute-start.23 = (f32[2,16]{1,0:T(2,128)S(1)}, f32[2,16]{1,0:T(2,128)S(1)}, u32[]{:S(2)}, u32[]{:S(2)}) collective-permute-start(f32[2,16]{1,0:T(2,128)S(1)} %get-tuple-element.60), channel_id=1, source_target_pairs={{0,8},{4,12},{8,0},{12,4},{16,24},{20,28},{24,16},{28,20},{32,40},... | collective-permute-start | bytes 392 | tf_op jit(solution)/shard_map/ppermute | solution.py:52
  67.0 3.9 %collective-permute-start.24 = (f32[2,16]{1,0:T(2,128)S(1)}, f32[2,16]{1,0:T(2,128)S(1)}, u32[]{:S(2)}, u32[]{:S(2)}) collective-permute-start(f32[2,16]{1,0:T(2,128)S(1)} %get-tuple-element.59), channel_id=1, source_target_pairs={{0,4},{4,8},{8,12},{12,0},{16,20},{20,24},{24,28},{28,16},{32,36},... | collective-permute-start | bytes 392 | tf_op jit(solution)/shard_map/ppermute | solution.py:52
  (2 other events, 9.2 us)

commit v6 on v5

--- a/solution.py
+++ b/solution.py
@@ -200,10 +200,10 @@
         zq = (z - (column // 8) % N) & 3
         pick = ((g ^ zq) * 16 + xq * 4 + yq == target).astype(jnp.float32)
         both = jnp.concatenate([before[...], total[...]], axis=1)
-        picked = lax.dot_general(
-            both, pick, (((1,), (0,)), ((), ())),
-            preferred_element_type=jnp.float32, precision=lax.Precision.HIGHEST,
-        )
+        high = both.astype(jnp.bfloat16).astype(jnp.float32)
+        terms = jnp.concatenate([high, both - high], axis=0).astype(jnp.bfloat16)
+        picked = jnp.dot(terms, pick.astype(jnp.bfloat16), preferred_element_type=jnp.float32)
+        picked = picked[:SEQS] + picked[SEQS:]
         for m in range(N):
             out[m] = picked[:, 16 * m : 16 * (m + 1)]
 

time: 71.9 us -> 71.8 us (level)
  no operation moved by 1% of the time
where the time goes in v6:
time: 71.8 us; the launch traced here: 71.5 us
  starting transfers between devices  45.5 us (63%)
  Pallas kernels  18.1 us (25%)
  waiting for transfers between devices  6.98 us (10%)
    ppermute x15, starting transfers between devices, along(): return lax.ppermute(value, 'loop', axis_shift(axis, step))  26.9 us
    ppermute x9, starting transfers between devices, across_heads(): return lax.ppermute(value, 'head', [(i, i ^ mask) for i in range(N)])  14 us
    pallas_call x2, Pallas kernels, products(): pl.pallas_call(functools.partial(product_kernel, steps, last), out_shape=...  10.4 us
    pallas_call x1, Pallas kernels, scaled_heads(): pl.pallas_call(scale_kernel, out_shape=pltpu.VMEM((HEADS, SEQS * HEAD_DIM...  4.77 us
    ppermute x1, starting transfers between devices, swapped(): return lax.ppermute(value, ('loop', 'head'), swap_shift(step))  4.59 us
    ppermute x9, waiting for transfers between devices, across_heads(): return lax.ppermute(value, 'head', [(i, i ^ mask) for i in range(N)])  3.46 us
    ppermute x15, waiting for transfers between devices, along(): return lax.ppermute(value, 'loop', axis_shift(axis, step))  3.42 us
    pallas_call x1, Pallas kernels, inverses(): pl.pallas_call(inverse_kernel, out_shape=pltpu.VMEM((HEADS, HEAD_DIM, FEA...  1.66 us
  transfers between devices with their start and end apart: 25, of which 9 were waited for; matrix products, arithmetic and copies ran while one was open for 0% of the time, Pallas kernels for 16%

profile of v6, /device:TPU:1, one launch (start us, length us, event | category | flops | bytes accessed | tf_op | source)
XLA Modules:
  0.0 71.5 jit_solution(7269092690648627565)
XLA Ops:
  0.0 1.2 %shard_map.73 = (bf16[3,8,8,128]{3,2,1,0:T(8,128)(2,1)S(1)}, bf16[1,8,8,128]{3,2,1,0:T(8,128)(2,1)S(1)}, bf16[2,8,8,128]{3,2,1,0:T(8,128)(2,1)S(1)}) custom-call(bf16[1,8,8,128]{3,2,1,0:T(8,128)(2,1)} %query.1, bf16[1,8,1024]{2,1,0:T(8,128)(2,1)} %right.1, bf16[2,8,8,128]{3,2,1,0:T(8,128)(2,1)} %train.1, bf16[2,8,1024]{2,1,0:T(8,128)(2,1)} %train_right.1, ...), custom_call_target="tpu_custom_call" | custom-call | tf_op jit(solution)/shard_map/pallas_call | solution.py:81
  1.2 4.6 %collective-permute-start = (bf16[3,8,8,128]{3,2,1,0:T(8,128)(2,1)S(1)}, bf16[3,8,8,128]{3,2,1,0:T(8,128)(2,1)S(1)}, u32[]{:S(2)}, u32[]{:S(2)}) collective-permute-start(bf16[3,8,8,128]{3,2,1,0:T(8,128)(2,1)S(1)} %get-tuple-element.28), channel_id=1, source_target_pairs={{0,0},{1,4},{2,8},{3,12},{4,1},{5,5},{6,9},{7,13},{8,2},{9,6},{10,... | collective-permute-start | bytes 147464 | tf_op jit(solution)/shard_map/ppermute | solution.py:56
  5.8 1.7 %shard_map.74.refs_8_ = f32[8,128,1024]{2,1,0:T(8,128)S(1)} custom-call(bf16[32,128,1024]{2,1,0:T(8,128)(2,1)} %eigen.1), custom_call_target="tpu_custom_call" | custom-call | flops 2097152 | bytes 6291456 | tf_op jit(solution)/shard_map/pallas_call | solution.py:107
  7.6 3.1 %collective-permute-start.1 = (bf16[1,16,8,128]{3,2,1,0:T(8,128)(2,1)S(1)}, bf16[1,16,8,128]{3,2,1,0:T(8,128)(2,1)S(1)}, u32[]{:S(2)}, u32[]{:S(2)}) collective-permute-start(bf16[1,16,8,128]{3,2,1,0:T(8,128)(2,1)S(1)} %get-tuple-element.53), channel_id=1, source_target_pairs={{0,64},{4,68},{8,72},{12,76},{16,80},{20,84},{24,88},{28,92},{32,9... | collective-permute-start | bytes 98312 | tf_op jit(solution)/shard_map/ppermute | solution.py:52
  10.6 5.1 %collective-permute-start.2 = (bf16[1,16,8,128]{3,2,1,0:T(8,128)(2,1)S(1)}, bf16[1,16,8,128]{3,2,1,0:T(8,128)(2,1)S(1)}, u32[]{:S(2)}, u32[]{:S(2)}) collective-permute-start(bf16[1,16,8,128]{3,2,1,0:T(8,128)(2,1)S(1)} %get-tuple-element.53), channel_id=1, source_target_pairs={{0,128},{4,132},{8,136},{12,140},{16,144},{20,148},{24,152},{28,15... | collective-permute-start | bytes 98312 | tf_op jit(solution)/shard_map/ppermute | solution.py:52
  15.8 2.4 %collective-permute-start.3 = (bf16[1,16,8,128]{3,2,1,0:T(8,128)(2,1)S(1)}, bf16[1,16,8,128]{3,2,1,0:T(8,128)(2,1)S(1)}, u32[]{:S(2)}, u32[]{:S(2)}) collective-permute-start(bf16[1,16,8,128]{3,2,1,0:T(8,128)(2,1)S(1)} %get-tuple-element.53), channel_id=1, source_target_pairs={{0,192},{4,196},{8,200},{12,204},{16,208},{20,212},{24,216},{28,22... | collective-permute-start | bytes 98312 | tf_op jit(solution)/shard_map/ppermute | solution.py:52
  18.1 4.1 %collective-permute-start.4 = (bf16[2,8,8,128]{3,2,1,0:T(8,128)(2,1)S(1)}, bf16[2,8,8,128]{3,2,1,0:T(8,128)(2,1)S(1)}, u32[]{:S(2)}, u32[]{:S(2)}) collective-permute-start(bf16[2,8,8,128]{3,2,1,0:T(8,128)(2,1)S(1)} %get-tuple-element.46.refs_4_), channel_id=1, source_target_pairs={{0,8},{4,12},{8,0},{12,4},{16,24},{20,28},{24,16},{28,20},{32,40},... | collective-permute-start | bytes 98312 | tf_op jit(solution)/shard_map/ppermute | solution.py:52
  22.2 1.6 %collective-permute-start.11 = (bf16[2,8,8,128]{3,2,1,0:T(8,128)(2,1)S(1)}, bf16[2,8,8,128]{3,2,1,0:T(8,128)(2,1)S(1)}, u32[]{:S(2)}, u32[]{:S(2)}) collective-permute-start(bf16[2,8,8,128]{3,2,1,0:T(8,128)(2,1)S(1)} %get-tuple-element.46.refs_4_), channel_id=1, source_target_pairs={{0,4},{4,8},{8,12},{12,0},{16,20},{20,24},{24,28},{28,16},{32,36},... | collective-permute-start | bytes 98312 | tf_op jit(solution)/shard_map/ppermute | solution.py:52
  25.2 1.3 %collective-permute-start.6 = (bf16[4,16,8,128]{3,2,1,0:T(8,128)(2,1)S(1)}, bf16[4,16,8,128]{3,2,1,0:T(8,128)(2,1)S(1)}, u32[]{:S(2)}, u32[]{:S(2)}) collective-permute-start(bf16[4,16,8,128]{3,2,1,0:T(8,128)(2,1)S(1)} %pad_maximum_fusion), channel_id=1, source_target_pairs={{0,16},{4,20},{8,24},{12,28},{16,32},{20,36},{24,40},{28,44},{32,4... | collective-permute-start | bytes 393224 | tf_op jit(solution)/shard_map/ppermute | solution.py:52
  26.5 2.5 %collective-permute-start.7 = (bf16[4,16,8,128]{3,2,1,0:T(8,128)(2,1)S(1)}, bf16[4,16,8,128]{3,2,1,0:T(8,128)(2,1)S(1)}, u32[]{:S(2)}, u32[]{:S(2)}) collective-permute-start(bf16[4,16,8,128]{3,2,1,0:T(8,128)(2,1)S(1)} %pad_maximum_fusion), channel_id=1, source_target_pairs={{0,32},{4,36},{8,40},{12,44},{16,48},{20,52},{24,56},{28,60},{32,0... | collective-permute-start | bytes 393224 | tf_op jit(solution)/shard_map/ppermute | solution.py:52
  28.9 1.2 %collective-permute-start.8 = (bf16[4,16,8,128]{3,2,1,0:T(8,128)(2,1)S(1)}, bf16[4,16,8,128]{3,2,1,0:T(8,128)(2,1)S(1)}, u32[]{:S(2)}, u32[]{:S(2)}) collective-permute-start(bf16[4,16,8,128]{3,2,1,0:T(8,128)(2,1)S(1)} %pad_maximum_fusion), channel_id=1, source_target_pairs={{0,48},{4,52},{8,56},{12,60},{16,0},{20,4},{24,8},{28,12},{32,16},... | collective-permute-start | bytes 393224 | tf_op jit(solution)/shard_map/ppermute | solution.py:52
  30.1 5.4 %collective-permute-start.10 = (bf16[2,8,8,128]{3,2,1,0:T(8,128)(2,1)S(1)}, bf16[2,8,8,128]{3,2,1,0:T(8,128)(2,1)S(1)}, u32[]{:S(2)}, u32[]{:S(2)}) collective-permute-start(bf16[2,8,8,128]{3,2,1,0:T(8,128)(2,1)S(1)} %collective-permute-done.5.refs_2_), channel_id=1, source_target_pairs={{0,1},{1,0},{2,3},{3,2},{4,5},{5,4},{6,7},{7,6},{8,9},{9,8},{10,11... | collective-permute-start | bytes 98312 | tf_op jit(solution)/shard_map/ppermute | solution.py:60
  36.8 1.2 %collective-permute-start.14 = (bf16[16,8,8,128]{3,2,1,0:T(8,128)(2,1)S(1)}, bf16[16,8,8,128]{3,2,1,0:T(8,128)(2,1)S(1)}, u32[]{:S(2)}, u32[]{:S(2)}) collective-permute-start(bf16[16,8,8,128]{3,2,1,0:T(8,128)(2,1)S(1)} %get-tuple-element.52.refs_0_), channel_id=1, source_target_pairs={{0,2},{1,3},{2,0},{3,1},{4,6},{5,7},{6,4},{7,5},{8,10},{9,11},{10,... | collective-permute-start | bytes 786440 | tf_op jit(solution)/shard_map/ppermute | solution.py:60
  38.0 2.5 %collective-permute-start.13 = (bf16[16,8,8,128]{3,2,1,0:T(8,128)(2,1)S(1)}, bf16[16,8,8,128]{3,2,1,0:T(8,128)(2,1)S(1)}, u32[]{:S(2)}, u32[]{:S(2)}) collective-permute-start(bf16[16,8,8,128]{3,2,1,0:T(8,128)(2,1)S(1)} %get-tuple-element.52.refs_0_), channel_id=1, source_target_pairs={{0,1},{1,0},{2,3},{3,2},{4,5},{5,4},{6,7},{7,6},{8,9},{9,8},{10,11... | collective-permute-start | bytes 786440 | tf_op jit(solution)/shard_map/ppermute | solution.py:60
  40.8 2.4 %collective-permute-start.17 = (bf16[16,8,8,128]{3,2,1,0:T(8,128)(2,1)S(1)}, bf16[16,8,8,128]{3,2,1,0:T(8,128)(2,1)S(1)}, u32[]{:S(2)}, u32[]{:S(2)}) collective-permute-start(bf16[16,8,8,128]{3,2,1,0:T(8,128)(2,1)S(1)} %get-tuple-element.51.refs_4_), channel_id=1, source_target_pairs={{0,12},{4,0},{8,4},{12,8},{16,28},{20,16},{24,20},{28,24},{32,44},... | collective-permute-start | bytes 786440 | tf_op jit(solution)/shard_map/ppermute | solution.py:52
  43.3 2.4 %collective-permute-start.15 = (bf16[16,8,8,128]{3,2,1,0:T(8,128)(2,1)S(1)}, bf16[16,8,8,128]{3,2,1,0:T(8,128)(2,1)S(1)}, u32[]{:S(2)}, u32[]{:S(2)}) collective-permute-start(bf16[16,8,8,128]{3,2,1,0:T(8,128)(2,1)S(1)} %collective-permute-done.14.refs_2_), channel_id=1, source_target_pairs={{0,1},{1,0},{2,3},{3,2},{4,5},{5,4},{6,7},{7,6},{8,9},{9,8},{10,11... | collective-permute-start | bytes 786440 | tf_op jit(solution)/shard_map/ppermute | solution.py:60
  45.7 4.8 %shard_map.75.refs_6_ = bf16[8,1024,1024]{2,1,0:T(8,128)(2,1)S(1)} custom-call(bf16[2,8,8,128]{3,2,1,0:T(8,128)(2,1)S(1)} %slice.39.refs_0_, bf16[2,8,8,128]{3,2,1,0:T(8,128)(2,1)S(1)} %collective-permute-done.9.refs_1_, bf16[2,8,8,128]{3,2,1,0:T(8,128)(2,1)S(1)} %collective-permute-done.5.refs_2_, ...), custom_call_target="tpu_custom_call" | custom-call | flops 4294967296 | bytes 1048576 | tf_op jit(solution)/shard_map/pallas_call | solution.py:148
  50.5 5.0 %shard_map.76.refs_7_ = f32[8,256]{1,0:T(8,128)S(1)} custom-call(bf16[16,8,8,128]{3,2,1,0:T(8,128)(2,1)S(1)} %get-tuple-element.52.refs_0_, bf16[16,8,8,128]{3,2,1,0:T(8,128)(2,1)S(1)} %collective-permute-done.13.refs_1_, bf16[16,8,8,128]{3,2,1,0:T(8,128)(2,1)S(1)} %collective-permute-done.14.refs_2_, ...), custom_call_target="tpu_custom_call" | custom-call | flops 1048576 | bytes 4096 | tf_op jit(solution)/shard_map/pallas_call | solution.py:221
  55.5 5.4 %shard_map.77 = f32[4,8,16]{2,1,0:T(8,128)S(1)} custom-call(bf16[16,8,8,128]{3,2,1,0:T(8,128)(2,1)S(1)} %get-tuple-element.52.refs_0_, bf16[16,8,8,128]{3,2,1,0:T(8,128)(2,1)S(1)} %collective-permute-done.13.refs_1_, bf16[16,8,8,128]{3,2,1,0:T(8,128)(2,1)S(1)} %collective-permute-done.14.refs_2_, ...), custom_call_target="tpu_custom_call" | custom-call | flops 1048576 | bytes 4096 | tf_op jit(solution)/shard_map/pallas_call | solution.py:221
  62.1 1.2 %collective-permute-start.21 = (f32[8,16]{1,0:T(8,128)S(1)}, f32[8,16]{1,0:T(8,128)S(1)}, u32[]{:S(2)}, u32[]{:S(2)}) collective-permute-start(f32[8,16]{1,0:T(8,128)S(1)} %get-tuple-element.56), channel_id=1, source_target_pairs={{0,3},{1,2},{2,1},{3,0},{4,7},{5,6},{6,5},{7,4},{8,11},{9,10},{10,... | collective-permute-start | bytes 1544 | tf_op jit(solution)/shard_map/ppermute | solution.py:60
  64.1 1.4 %collective-permute-done.21 = f32[8,16]{1,0:T(8,128)S(1)} collective-permute-done((f32[8,16]{1,0:T(8,128)S(1)}, f32[8,16]{1,0:T(8,128)S(1)}, u32[]{:S(2)}, u32[]{:S(2)}) %collective-permute-start.21) | collective-permute-done | bytes 544 | tf_op jit(solution)/shard_map/ppermute | solution.py:60
  65.7 1.2 %collective-permute-start.23 = (f32[2,16]{1,0:T(2,128)S(1)}, f32[2,16]{1,0:T(2,128)S(1)}, u32[]{:S(2)}, u32[]{:S(2)}) collective-permute-start(f32[2,16]{1,0:T(2,128)S(1)} %get-tuple-element.60), channel_id=1, source_target_pairs={{0,8},{4,12},{8,0},{12,4},{16,24},{20,28},{24,16},{28,20},{32,40},... | collective-permute-start | bytes 392 | tf_op jit(solution)/shard_map/ppermute | solution.py:52
  68.0 1.6 %collective-permute-done.23 = f32[2,16]{1,0:T(2,128)S(1)} collective-permute-done((f32[2,16]{1,0:T(2,128)S(1)}, f32[2,16]{1,0:T(2,128)S(1)}, u32[]{:S(2)}, u32[]{:S(2)}) %collective-permute-start.23) | collective-permute-done | bytes 160 | tf_op jit(solution)/shard_map/ppermute | solution.py:52
  69.7 1.2 %collective-permute-done.24 = f32[2,16]{1,0:T(2,128)S(1)} collective-permute-done((f32[2,16]{1,0:T(2,128)S(1)}, f32[2,16]{1,0:T(2,128)S(1)}, u32[]{:S(2)}, u32[]{:S(2)}) %collective-permute-start.24) | collective-permute-done | bytes 160 | tf_op jit(solution)/shard_map/ppermute | solution.py:52
  (49 shorter events, 7.0 us)
Async XLA Ops:
  1.2 6.4 %collective-permute-start = (bf16[3,8,8,128]{3,2,1,0:T(8,128)(2,1)S(1)}, bf16[3,8,8,128]{3,2,1,0:T(8,128)(2,1)S(1)}, u32[]{:S(2)}, u32[]{:S(2)}) collective-permute-start(bf16[3,8,8,128]{3,2,1,0:T(8,128)(2,1)S(1)} %get-tuple-element.28), channel_id=1, source_target_pairs={{0,0},{1,4},{2,8},{3,12},{4,1},{5,5},{6,9},{7,13},{8,2},{9,6},{10,... | collective-permute-start | bytes 147464 | tf_op jit(solution)/shard_map/ppermute | solution.py:56
  7.6 14.6 %collective-permute-start.1 = (bf16[1,16,8,128]{3,2,1,0:T(8,128)(2,1)S(1)}, bf16[1,16,8,128]{3,2,1,0:T(8,128)(2,1)S(1)}, u32[]{:S(2)}, u32[]{:S(2)}) collective-permute-start(bf16[1,16,8,128]{3,2,1,0:T(8,128)(2,1)S(1)} %get-tuple-element.53), channel_id=1, source_target_pairs={{0,64},{4,68},{8,72},{12,76},{16,80},{20,84},{24,88},{28,92},{32,9... | collective-permute-start | bytes 98312 | tf_op jit(solution)/shard_map/ppermute | solution.py:52
  10.6 13.2 %collective-permute-start.2 = (bf16[1,16,8,128]{3,2,1,0:T(8,128)(2,1)S(1)}, bf16[1,16,8,128]{3,2,1,0:T(8,128)(2,1)S(1)}, u32[]{:S(2)}, u32[]{:S(2)}) collective-permute-start(bf16[1,16,8,128]{3,2,1,0:T(8,128)(2,1)S(1)} %get-tuple-element.53), channel_id=1, source_target_pairs={{0,128},{4,132},{8,136},{12,140},{16,144},{20,148},{24,152},{28,15... | collective-permute-start | bytes 98312 | tf_op jit(solution)/shard_map/ppermute | solution.py:52
  15.8 9.1 %collective-permute-start.3 = (bf16[1,16,8,128]{3,2,1,0:T(8,128)(2,1)S(1)}, bf16[1,16,8,128]{3,2,1,0:T(8,128)(2,1)S(1)}, u32[]{:S(2)}, u32[]{:S(2)}) collective-permute-start(bf16[1,16,8,128]{3,2,1,0:T(8,128)(2,1)S(1)} %get-tuple-element.53), channel_id=1, source_target_pairs={{0,192},{4,196},{8,200},{12,204},{16,208},{20,212},{24,216},{28,22... | collective-permute-start | bytes 98312 | tf_op jit(solution)/shard_map/ppermute | solution.py:52
  18.1 6.8 %collective-permute-start.4 = (bf16[2,8,8,128]{3,2,1,0:T(8,128)(2,1)S(1)}, bf16[2,8,8,128]{3,2,1,0:T(8,128)(2,1)S(1)}, u32[]{:S(2)}, u32[]{:S(2)}) collective-permute-start(bf16[2,8,8,128]{3,2,1,0:T(8,128)(2,1)S(1)} %get-tuple-element.46.refs_4_), channel_id=1, source_target_pairs={{0,8},{4,12},{8,0},{12,4},{16,24},{20,28},{24,16},{28,20},{32,40},... | collective-permute-start | bytes 98312 | tf_op jit(solution)/shard_map/ppermute | solution.py:52
  22.2 2.9 %collective-permute-start.5 = (bf16[2,8,8,128]{3,2,1,0:T(8,128)(2,1)S(1)}, bf16[2,8,8,128]{3,2,1,0:T(8,128)(2,1)S(1)}, u32[]{:S(2)}, u32[]{:S(2)}) collective-permute-start(bf16[2,8,8,128]{3,2,1,0:T(8,128)(2,1)S(1)} %slice.39.refs_0_), channel_id=1, source_target_pairs={{0,2},{1,3},{2,0},{3,1},{4,6},{5,7},{6,4},{7,5},{8,10},{9,11},{10,... | collective-permute-start | bytes 98312 | tf_op jit(solution)/shard_map/ppermute | solution.py:60
  22.2 7.9 %collective-permute-start.11 = (bf16[2,8,8,128]{3,2,1,0:T(8,128)(2,1)S(1)}, bf16[2,8,8,128]{3,2,1,0:T(8,128)(2,1)S(1)}, u32[]{:S(2)}, u32[]{:S(2)}) collective-permute-start(bf16[2,8,8,128]{3,2,1,0:T(8,128)(2,1)S(1)} %get-tuple-element.46.refs_4_), channel_id=1, source_target_pairs={{0,4},{4,8},{8,12},{12,0},{16,20},{20,24},{24,28},{28,16},{32,36},... | collective-permute-start | bytes 98312 | tf_op jit(solution)/shard_map/ppermute | solution.py:52
  23.8 11.7 %collective-permute-start.12 = (bf16[2,8,8,128]{3,2,1,0:T(8,128)(2,1)S(1)}, bf16[2,8,8,128]{3,2,1,0:T(8,128)(2,1)S(1)}, u32[]{:S(2)}, u32[]{:S(2)}) collective-permute-start(bf16[2,8,8,128]{3,2,1,0:T(8,128)(2,1)S(1)} %get-tuple-element.46.refs_4_), channel_id=1, source_target_pairs={{0,12},{4,0},{8,4},{12,8},{16,28},{20,16},{24,20},{28,24},{32,44},... | collective-permute-start | bytes 98312 | tf_op jit(solution)/shard_map/ppermute | solution.py:52
  25.2 11.5 %collective-permute-start.6 = (bf16[4,16,8,128]{3,2,1,0:T(8,128)(2,1)S(1)}, bf16[4,16,8,128]{3,2,1,0:T(8,128)(2,1)S(1)}, u32[]{:S(2)}, u32[]{:S(2)}) collective-permute-start(bf16[4,16,8,128]{3,2,1,0:T(8,128)(2,1)S(1)} %pad_maximum_fusion), channel_id=1, source_target_pairs={{0,16},{4,20},{8,24},{12,28},{16,32},{20,36},{24,40},{28,44},{32,4... | collective-permute-start | bytes 393224 | tf_op jit(solution)/shard_map/ppermute | solution.py:52
  26.5 10.3 %collective-permute-start.7 = (bf16[4,16,8,128]{3,2,1,0:T(8,128)(2,1)S(1)}, bf16[4,16,8,128]{3,2,1,0:T(8,128)(2,1)S(1)}, u32[]{:S(2)}, u32[]{:S(2)}) collective-permute-start(bf16[4,16,8,128]{3,2,1,0:T(8,128)(2,1)S(1)} %pad_maximum_fusion), channel_id=1, source_target_pairs={{0,32},{4,36},{8,40},{12,44},{16,48},{20,52},{24,56},{28,60},{32,0... | collective-permute-start | bytes 393224 | tf_op jit(solution)/shard_map/ppermute | solution.py:52
  28.9 7.8 %collective-permute-start.8 = (bf16[4,16,8,128]{3,2,1,0:T(8,128)(2,1)S(1)}, bf16[4,16,8,128]{3,2,1,0:T(8,128)(2,1)S(1)}, u32[]{:S(2)}, u32[]{:S(2)}) collective-permute-start(bf16[4,16,8,128]{3,2,1,0:T(8,128)(2,1)S(1)} %pad_maximum_fusion), channel_id=1, source_target_pairs={{0,48},{4,52},{8,56},{12,60},{16,0},{20,4},{24,8},{28,12},{32,16},... | collective-permute-start | bytes 393224 | tf_op jit(solution)/shard_map/ppermute | solution.py:52
  30.1 6.3 %collective-permute-start.10 = (bf16[2,8,8,128]{3,2,1,0:T(8,128)(2,1)S(1)}, bf16[2,8,8,128]{3,2,1,0:T(8,128)(2,1)S(1)}, u32[]{:S(2)}, u32[]{:S(2)}) collective-permute-start(bf16[2,8,8,128]{3,2,1,0:T(8,128)(2,1)S(1)} %collective-permute-done.5.refs_2_), channel_id=1, source_target_pairs={{0,1},{1,0},{2,3},{3,2},{4,5},{5,4},{6,7},{7,6},{8,9},{9,8},{10,11... | collective-permute-start | bytes 98312 | tf_op jit(solution)/shard_map/ppermute | solution.py:60
  36.8 6.4 %collective-permute-start.14 = (bf16[16,8,8,128]{3,2,1,0:T(8,128)(2,1)S(1)}, bf16[16,8,8,128]{3,2,1,0:T(8,128)(2,1)S(1)}, u32[]{:S(2)}, u32[]{:S(2)}) collective-permute-start(bf16[16,8,8,128]{3,2,1,0:T(8,128)(2,1)S(1)} %get-tuple-element.52.refs_0_), channel_id=1, source_target_pairs={{0,2},{1,3},{2,0},{3,1},{4,6},{5,7},{6,4},{7,5},{8,10},{9,11},{10,... | collective-permute-start | bytes 786440 | tf_op jit(solution)/shard_map/ppermute | solution.py:60
  38.0 12.4 %collective-permute-start.13 = (bf16[16,8,8,128]{3,2,1,0:T(8,128)(2,1)S(1)}, bf16[16,8,8,128]{3,2,1,0:T(8,128)(2,1)S(1)}, u32[]{:S(2)}, u32[]{:S(2)}) collective-permute-start(bf16[16,8,8,128]{3,2,1,0:T(8,128)(2,1)S(1)} %get-tuple-element.52.refs_0_), channel_id=1, source_target_pairs={{0,1},{1,0},{2,3},{3,2},{4,5},{5,4},{6,7},{7,6},{8,9},{9,8},{10,11... | collective-permute-start | bytes 786440 | tf_op jit(solution)/shard_map/ppermute | solution.py:60
  40.5 9.9 %collective-permute-start.18 = (bf16[16,8,8,128]{3,2,1,0:T(8,128)(2,1)S(1)}, bf16[16,8,8,128]{3,2,1,0:T(8,128)(2,1)S(1)}, u32[]{:S(2)}, u32[]{:S(2)}) collective-permute-start(bf16[16,8,8,128]{3,2,1,0:T(8,128)(2,1)S(1)} %get-tuple-element.51.refs_4_), channel_id=1, source_target_pairs={{0,8},{4,12},{8,0},{12,4},{16,24},{20,28},{24,16},{28,20},{32,40},... | collective-permute-start | bytes 786440 | tf_op jit(solution)/shard_map/ppermute | solution.py:52
  40.6 14.9 %collective-permute-start.16 = (bf16[16,8,8,128]{3,2,1,0:T(8,128)(2,1)S(1)}, bf16[16,8,8,128]{3,2,1,0:T(8,128)(2,1)S(1)}, u32[]{:S(2)}, u32[]{:S(2)}) collective-permute-start(bf16[16,8,8,128]{3,2,1,0:T(8,128)(2,1)S(1)} %get-tuple-element.51.refs_4_), channel_id=1, source_target_pairs={{0,4},{4,8},{8,12},{12,0},{16,20},{20,24},{24,28},{28,16},{32,36},... | collective-permute-start | bytes 786440 | tf_op jit(solution)/shard_map/ppermute | solution.py:52
  40.8 14.7 %collective-permute-start.17 = (bf16[16,8,8,128]{3,2,1,0:T(8,128)(2,1)S(1)}, bf16[16,8,8,128]{3,2,1,0:T(8,128)(2,1)S(1)}, u32[]{:S(2)}, u32[]{:S(2)}) collective-permute-start(bf16[16,8,8,128]{3,2,1,0:T(8,128)(2,1)S(1)} %get-tuple-element.51.refs_4_), channel_id=1, source_target_pairs={{0,12},{4,0},{8,4},{12,8},{16,28},{20,16},{24,20},{28,24},{32,44},... | collective-permute-start | bytes 786440 | tf_op jit(solution)/shard_map/ppermute | solution.py:52
  43.3 7.2 %collective-permute-start.15 = (bf16[16,8,8,128]{3,2,1,0:T(8,128)(2,1)S(1)}, bf16[16,8,8,128]{3,2,1,0:T(8,128)(2,1)S(1)}, u32[]{:S(2)}, u32[]{:S(2)}) collective-permute-start(bf16[16,8,8,128]{3,2,1,0:T(8,128)(2,1)S(1)} %collective-permute-done.14.refs_2_), channel_id=1, source_target_pairs={{0,1},{1,0},{2,3},{3,2},{4,5},{5,4},{6,7},{7,6},{8,9},{9,8},{10,11... | collective-permute-start | bytes 786440 | tf_op jit(solution)/shard_map/ppermute | solution.py:60
  60.9 2.5 %collective-permute-start.19 = (f32[8,16]{1,0:T(8,128)S(1)}, f32[8,16]{1,0:T(8,128)S(1)}, u32[]{:S(2)}, u32[]{:S(2)}) collective-permute-start(f32[8,16]{1,0:T(8,128)S(1)} %get-tuple-element.55), channel_id=1, source_target_pairs={{0,1},{1,0},{2,3},{3,2},{4,5},{5,4},{6,7},{7,6},{8,9},{9,8},{10,11... | collective-permute-start | bytes 1544 | tf_op jit(solution)/shard_map/ppermute | solution.py:60
  61.6 2.5 %collective-permute-start.20 = (f32[8,16]{1,0:T(8,128)S(1)}, f32[8,16]{1,0:T(8,128)S(1)}, u32[]{:S(2)}, u32[]{:S(2)}) collective-permute-start(f32[8,16]{1,0:T(8,128)S(1)} %get-tuple-element.57), channel_id=1, source_target_pairs={{0,2},{1,3},{2,0},{3,1},{4,6},{5,7},{6,4},{7,5},{8,10},{9,11},{10,... | collective-permute-start | bytes 1544 | tf_op jit(solution)/shard_map/ppermute | solution.py:60
  62.1 3.4 %collective-permute-start.21 = (f32[8,16]{1,0:T(8,128)S(1)}, f32[8,16]{1,0:T(8,128)S(1)}, u32[]{:S(2)}, u32[]{:S(2)}) collective-permute-start(f32[8,16]{1,0:T(8,128)S(1)} %get-tuple-element.56), channel_id=1, source_target_pairs={{0,3},{1,2},{2,1},{3,0},{4,7},{5,6},{6,5},{7,4},{8,11},{9,10},{10,... | collective-permute-start | bytes 1544 | tf_op jit(solution)/shard_map/ppermute | solution.py:60
  65.5 2.5 %collective-permute-start.22 = (f32[2,16]{1,0:T(2,128)S(1)}, f32[2,16]{1,0:T(2,128)S(1)}, u32[]{:S(2)}, u32[]{:S(2)}) collective-permute-start(f32[2,16]{1,0:T(2,128)S(1)} %get-tuple-element.58), channel_id=1, source_target_pairs={{0,12},{4,0},{8,4},{12,8},{16,28},{20,16},{24,20},{28,24},{32,44},... | collective-permute-start | bytes 392 | tf_op jit(solution)/shard_map/ppermute | solution.py:52
  65.7 3.9 %collective-permute-start.23 = (f32[2,16]{1,0:T(2,128)S(1)}, f32[2,16]{1,0:T(2,128)S(1)}, u32[]{:S(2)}, u32[]{:S(2)}) collective-permute-start(f32[2,16]{1,0:T(2,128)S(1)} %get-tuple-element.60), channel_id=1, source_target_pairs={{0,8},{4,12},{8,0},{12,4},{16,24},{20,28},{24,16},{28,20},{32,40},... | collective-permute-start | bytes 392 | tf_op jit(solution)/shard_map/ppermute | solution.py:52
  66.9 3.9 %collective-permute-start.24 = (f32[2,16]{1,0:T(2,128)S(1)}, f32[2,16]{1,0:T(2,128)S(1)}, u32[]{:S(2)}, u32[]{:S(2)}) collective-permute-start(f32[2,16]{1,0:T(2,128)S(1)} %get-tuple-element.59), channel_id=1, source_target_pairs={{0,4},{4,8},{8,12},{12,0},{16,20},{20,24},{24,28},{28,16},{32,36},... | collective-permute-start | bytes 392 | tf_op jit(solution)/shard_map/ppermute | solution.py:52
  (2 other events, 9.1 us)
